TPU v7x, 128 devices: a whole 4x4x4 slice. The times are simulated.
128 devices in a mesh: blocks: 128 (over y, z, x, core).
Axes of the slice: x: 4, y: 4, z: 4, core: 2. Of those that a mesh axis runs over, the one named last changes fastest.
Arguments:
- pdfs: float32 [512, 19, 4096], P('blocks'), may hold values from 0.25 to 21, as said below
- plan: int32 [512], P('blocks'), may hold values from 0 to 511, as said below
- neighbours: int32 [512, 6], P('blocks'), may hold values from -1 to 511, as said below
- flags: int32 [512, 4096], P('blocks'), may hold values 0 or 1
Outputs:
- final_pdfs: float32 [512, 19, 4096], P('blocks')
Inputs may be any that keep to these rules, and one draw needn't show every extreme that they name: `plan`: A permutation of the places. Each device sends exactly 1 block to each of 4 owners, which lie at distinct offsets from -2 to 2 around the cycle of devices; the offsets are the same for every device, and an owner keeps the received blocks in an order of offset that is the same for every owner. `neighbours`: Symmetric: if the block across the upper face of b along an axis is n, the block across the lower face of n along that axis is b. A neighbour's owner lies within 2 devices of the block's owner around the cycle, never the block itself; for every offset from 1 to 2 in either direction, exactly 6 faces of one device's blocks border blocks of the device at that offset. `pdfs`: positive populations near a rest state.
All inputs are finite; a program needn't handle non-finite values. No bound on the sum of `flags` on one device may be relied on, other than what follows from the above.
Results may differ from a plain program's by a relative error of at most 0.0001.
Values sent between devices are 32-bit elements; how exact they have to be, the bound alone decides.
No kernel may reach another device: no remote copies, remote signals or barrier semaphores. Data moves between devices by JAX's collectives and lax.ppermute only.
A program may use at most 192 MiB of HBM per device.

v0:
```python
import jax
import jax.numpy as jnp
import numpy as np
from jax import lax
from jax.sharding import PartitionSpec as P

EDGE = 16
BLK_DEV = 4
GROUPS = 4
REACH = 2
STEPS = 3


VELOCITY_TABLE = np.array(
    [
        [0, 0, 0],
        [1, 0, 0],
        [-1, 0, 0],
        [0, 1, 0],
        [0, -1, 0],
        [0, 0, 1],
        [0, 0, -1],
        [1, 1, 0],
        [-1, -1, 0],
        [1, -1, 0],
        [-1, 1, 0],
        [1, 0, 1],
        [-1, 0, -1],
        [1, 0, -1],
        [-1, 0, 1],
        [0, 1, 1],
        [0, -1, -1],
        [0, 1, -1],
        [0, -1, 1],
    ],
    np.int32,
)
WEIGHT_TABLE = np.array([1.0 / 3.0] + [1.0 / 18.0] * 6 + [1.0 / 36.0] * 12)
REST_DENSITY = 36.0
SHEAR_RATE = 1.6
FACE_FLIP = np.array([1, 0, 3, 2, 5, 4], np.int32)


def from_behind(block, axis, distance):
    devices = range(lax.axis_size(axis))
    route = [((i - distance) % len(devices), i) for i in devices]
    return lax.ppermute(block, axis, route)


def opposite_table():
    result = []
    for pop_id in range(19):
        same = np.all(VELOCITY_TABLE == -VELOCITY_TABLE[pop_id][None, :], axis=1)
        result.append(int(np.argmax(same)))
    return np.array(result, np.int32)


def collision_matrix():
    speeds = VELOCITY_TABLE * 1.0
    along_x, along_y, along_z = (speeds[:, 0], speeds[:, 1], speeds[:, 2])
    squared = along_x * along_x + along_y * along_y + along_z * along_z
    rows = [
        np.ones(19),
        19 * squared - 30,
        (21 * squared * squared - 53 * squared + 24) / 2,
        along_x,
        (5 * squared - 9) * along_x,
        along_y,
        (5 * squared - 9) * along_y,
        along_z,
        (5 * squared - 9) * along_z,
        3 * along_x * along_x - squared,
        (3 * squared - 5) * (3 * along_x * along_x - squared),
        along_y * along_y - along_z * along_z,
        (3 * squared - 5) * (along_y * along_y - along_z * along_z),
        along_x * along_y,
        along_y * along_z,
        along_x * along_z,
        along_x * (along_y * along_y - along_z * along_z),
        along_y * (along_z * along_z - along_x * along_x),
        along_z * (along_x * along_x - along_y * along_y),
    ]
    moments = np.stack(rows)
    rates = np.array(
        [
            0,
            1.19,
            1.4,
            0,
            1.2,
            0,
            1.2,
            0,
            1.2,
            SHEAR_RATE,
            1.4,
            SHEAR_RATE,
            1.4,
            SHEAR_RATE,
            SHEAR_RATE,
            SHEAR_RATE,
            1.98,
            1.98,
            1.98,
        ]
    )
    norms = np.sum(moments * moments, axis=1)
    return moments.T * (rates / norms)[None, :] @ moments


def face_tables(edge):
    face_pops = np.zeros((6, 5), np.int32)
    face_cells = np.zeros((6, edge * edge), np.int32)
    grid_u, grid_v = np.meshgrid(np.arange(edge), np.arange(edge), indexing="ij")
    for face_id in range(6):
        axis_id = face_id // 2
        side_sign = 1 if face_id % 2 else -1
        face_pops[face_id] = [
            pop_id for pop_id in range(19) if int(VELOCITY_TABLE[pop_id][axis_id]) == side_sign
        ]
        others = [other for other in range(3) if other != axis_id]
        points = np.zeros((3, edge, edge), np.int32)
        points[axis_id] = edge - 1 if side_sign > 0 else 0
        points[others[0]] = grid_u
        points[others[1]] = grid_v
        face_cells[face_id] = (points[0] * edge * edge + points[1] * edge + points[2]).reshape(-1)
    return (face_pops, face_cells)


def collide(pdfs, flags):
    speeds = jnp.asarray(VELOCITY_TABLE, jnp.float32)
    weights = jnp.asarray(WEIGHT_TABLE, jnp.float32)
    kernel = jnp.asarray(collision_matrix(), jnp.float32)
    density = jnp.sum(pdfs, axis=1)
    momentum = jnp.einsum("ia,bic->bac", speeds, pdfs, precision=lax.Precision.HIGHEST)
    projected = jnp.einsum("ia,bac->bic", speeds, momentum, precision=lax.Precision.HIGHEST)
    speed_sq = jnp.sum(momentum * momentum, axis=1)
    equilibrium = weights[None, :, None] * (
        density[:, None, :]
        + 3.0 * projected
        + (4.5 * projected * projected - 1.5 * speed_sq[:, None, :]) / REST_DENSITY
    )
    relaxed = pdfs - jnp.einsum(
        "ij,bjc->bic", kernel, pdfs - equilibrium, precision=lax.Precision.HIGHEST
    )
    reflected = pdfs[:, opposite_table(), :]
    return jnp.where(flags[:, None, :] == 1, relaxed, reflected)


def outgoing_faces(post, edge):
    face_pops, face_cells = face_tables(edge)
    return post[:, face_pops[:, :, None], face_cells[:, None, :]]


def stream_slices(post, ghost, missing, edge):
    count = post.shape[0]
    opposite = opposite_table()
    face_pops, face_cells = face_tables(edge)
    field = post.reshape(count, 19, edge, edge, edge)
    coords = np.stack(np.meshgrid(np.arange(edge), np.arange(edge), np.arange(edge), indexing="ij"))
    results = []
    for pop_id in range(19):
        speed = VELOCITY_TABLE[pop_id]
        anchor = coords - speed[:, None, None, None]
        outside = (anchor < 0) | (anchor >= edge)
        crossings = outside.sum(axis=0)
        padded = jnp.pad(field[:, pop_id], ((0, 0), (1, 1), (1, 1), (1, 1)))
        lacking = jnp.asarray(crossings >= 2)[None, :, :, :]
        for axis_id in range(3):
            speed_part = int(speed[axis_id])
            if speed_part == 0:
                continue
            face_id = 2 * axis_id if speed_part > 0 else 2 * axis_id + 1
            pop_pos = int(np.argmax(face_pops[face_id ^ 1] == pop_id))
            plane = ghost[:, face_id, pop_pos].reshape(count, edge, edge)
            spots = [slice(None), slice(1, edge + 1), slice(1, edge + 1), slice(1, edge + 1)]
            spots[axis_id + 1] = 0 if speed_part > 0 else edge + 1
            padded = padded.at[tuple(spots)].set(plane)
            single = (crossings == 1) & outside[axis_id]
            lacking = (
                lacking
                | jnp.asarray(single)[None, :, :, :] & missing[:, face_id][:, None, None, None]
            )
        begins = [1 - int(value) for value in speed]
        read = padded[
            :,
            begins[0] : begins[0] + edge,
            begins[1] : begins[1] + edge,
            begins[2] : begins[2] + edge,
        ]
        results.append(jnp.where(lacking, field[:, int(opposite[pop_id])], read))
    return jnp.stack(results, axis=1).reshape(post.shape)


def body(pdfs, plan, neighbours, flags):
    blocks = pdfs.shape[0]
    cells = pdfs.shape[2]
    cycle = lax.axis_size("blocks")
    myself = lax.axis_index("blocks")
    per_peer = BLK_DEV // GROUPS
    owner_off = (plan // blocks - myself + REACH) % cycle - REACH
    target_slot = plan % blocks
    slot_ids = jnp.arange(blocks)
    rows_list = []
    slots_list = []
    for offset in range(-REACH, REACH + 1):
        chosen = owner_off == offset
        rank_pos = jnp.cumsum(chosen.astype(jnp.int32)) - 1
        matches = chosen[None, :] & (rank_pos[None, :] == jnp.arange(per_peer)[:, None])
        source_slot = jnp.sum(jnp.where(matches, slot_ids[None, :], 0), axis=1)
        present = jnp.any(matches, axis=1)
        packed = jnp.take(pdfs, source_slot, axis=0)
        slots_out = jnp.where(present, jnp.take(target_slot, source_slot), blocks).astype(jnp.int32)
        if offset != 0:
            packed, slots_out = from_behind((packed, slots_out), "blocks", offset)
        rows_list.append(packed)
        slots_list.append(slots_out)
    arrived = jnp.concatenate(rows_list, axis=0)
    arrived_slots = jnp.concatenate(slots_list, axis=0)
    moved = jnp.zeros((blocks + 1, 19, cells), jnp.float32).at[arrived_slots].set(arrived)[:blocks]
    missing = neighbours < 0
    safe_ids = jnp.maximum(neighbours, 0)
    nb_slot = safe_ids % blocks
    nb_offset = jnp.where(missing, 0, (safe_ids // blocks - myself + REACH) % cycle - REACH)
    offset_flat = nb_offset.reshape(-1)
    rows_needed = ((offset_flat + REACH) * blocks + nb_slot.reshape(-1)) * 6 + jnp.tile(
        jnp.asarray(FACE_FLIP, jnp.int32), blocks
    )
    for step_id in range(STEPS):
        post = collide(moved, flags)
        faces = outgoing_faces(post, EDGE).reshape(blocks * 6, 5 * EDGE * EDGE)
        pieces = []
        for offset in range(-REACH, REACH + 1):
            if offset == 0:
                pieces.append(faces)
            else:
                pieces.append(from_behind(faces, "blocks", -offset))
        pool = jnp.concatenate(pieces, axis=0)
        ghost = jnp.take(pool, rows_needed, axis=0).reshape(blocks, 6, 5, EDGE * EDGE)
        moved = stream_slices(post, ghost, missing, EDGE)
    return moved


def solution(mesh):
    placed = (P("blocks", None, None), P("blocks"), P("blocks", None), P("blocks", None))
    return jax.shard_map(
        body, mesh=mesh, in_specs=placed, out_specs=P("blocks", None, None), check_vma=False
    )
```

profile of v0, /device:TPU:1, one launch (start us, length us, event | category | flops | bytes accessed | tf_op | source)
XLA Modules:
  0.0 1511.9 jit_solution(12753591985166559831)
XLA Ops:
  90.5 19.2 %copy.249 = f32[4,19,4096]{0,2,1:T(8,128)} copy(f32[4,19,4096]{2,1,0:T(8,128)} %fusion.3) | data formatting | bytes 2490368 | tf_op jit(solution)/shard_map/jit(_where)/select_n | solution.py:147
  109.7 111.7 %gather_fusion.1 = f32[7680,4]{1,0:T(8,128)} fusion(f32[4,19,4096]{0,2,1:T(8,128)} %copy.249, s32[7680]{0:T(1024)S(1)} %reshape.4503), kind=kCustom, calls=%fused_computation.4 | custom fusion | bytes 307200 | tf_op jit(solution)/shard_map/gather | solution.py:152
  305.2 12.6 scatter.354
  328.0 12.1 scatter.350
  418.5 12.5 scatter.336
  432.6 11.2 scatter.340
  456.4 10.7 scatter.314
  503.7 11.2 scatter.316
  530.1 10.9 scatter.320
  560.2 18.1 %copy.264 = f32[4,19,4096]{0,2,1:T(8,128)} copy(f32[4,19,4096]{2,1,0:T(8,128)S(1)} %fusion.5) | data formatting | bytes 2490368 | tf_op jit(solution)/shard_map/jit(_where)/select_n | solution.py:147
  578.2 111.7 %gather_fusion.3 = f32[7680,4]{1,0:T(8,128)} fusion(f32[4,19,4096]{0,2,1:T(8,128)} %copy.264, s32[7680]{0:T(1024)S(1)} %reshape.4503), kind=kCustom, calls=%fused_computation.6 | custom fusion | bytes 307200 | tf_op jit(solution)/shard_map/gather | solution.py:152
  765.4 12.1 scatter.404
  787.8 12.1 scatter.400
  799.9 10.6 scatter.405
  879.5 11.2 scatter.386
  893.5 12.5 scatter.390
  963.9 11.2 scatter.366
  1020.1 18.1 %copy.279 = f32[4,19,4096]{0,2,1:T(8,128)} copy(f32[4,19,4096]{2,1,0:T(8,128)S(1)} %fusion.7) | data formatting | bytes 2490368 | tf_op jit(solution)/shard_map/jit(_where)/select_n | solution.py:147
  1038.2 111.7 %gather_fusion.5 = f32[7680,4]{1,0:T(8,128)} fusion(f32[4,19,4096]{0,2,1:T(8,128)} %copy.279, s32[7680]{0:T(1024)S(1)} %reshape.4503), kind=kCustom, calls=%fused_computation.8 | custom fusion | bytes 307200 | tf_op jit(solution)/shard_map/gather | solution.py:152
  1221.1 12.6 scatter.454
  1244.1 12.6 scatter.450
  1351.3 12.6 scatter.436
  1366.7 12.8 scatter.440
  1446.3 12.6 scatter.416
  (1188 shorter events, 886.5 us)
Async XLA Ops:
  18.0 50.9 %collective-permute-start.4 = (f32[1,19,4096]{2,1,0:T(8,128)S(1)}, f32[1,19,4096]{2,1,0:T(8,128)S(1)}, u32[]{:S(2)}, u32[]{:S(2)}) collective-permute-start(f32[1,19,4096]{2,1,0:T(8,128)S(1)} %copy_select_fusion.4), channel_id=1, source_target_pairs={{2,0},{3,1},{4,2},{5,3},{6,4},{7,5},{8,6},{9,7},{10,8},{11,9},{12,... | collective-permute-start | bytes 933896 | tf_op jit(solution)/shard_map/ppermute | solution.py:47
  27.5 42.1 %collective-permute-start.5 = (f32[1,19,4096]{2,1,0:T(8,128)S(1)}, f32[1,19,4096]{2,1,0:T(8,128)S(1)}, u32[]{:S(2)}, u32[]{:S(2)}) collective-permute-start(f32[1,19,4096]{2,1,0:T(8,128)S(1)} %copy_select_fusion.3), channel_id=1, source_target_pairs={{1,0},{2,1},{3,2},{4,3},{5,4},{6,5},{7,6},{8,7},{9,8},{10,9},{11,1... | collective-permute-start | bytes 933896 | tf_op jit(solution)/shard_map/ppermute | solution.py:47
  28.7 42.6 %collective-permute-start.6 = (f32[1,19,4096]{2,1,0:T(8,128)S(1)}, f32[1,19,4096]{2,1,0:T(8,128)S(1)}, u32[]{:S(2)}, u32[]{:S(2)}) collective-permute-start(f32[1,19,4096]{2,1,0:T(8,128)S(1)} %copy_select_fusion.1), channel_id=1, source_target_pairs={{127,0},{0,1},{1,2},{2,3},{3,4},{4,5},{5,6},{6,7},{7,8},{8,9},{9,1... | collective-permute-start | bytes 933896 | tf_op jit(solution)/shard_map/ppermute | solution.py:47
  29.8 42.4 %collective-permute-start.7 = (f32[1,19,4096]{2,1,0:T(8,128)S(1)}, f32[1,19,4096]{2,1,0:T(8,128)S(1)}, u32[]{:S(2)}, u32[]{:S(2)}) collective-permute-start(f32[1,19,4096]{2,1,0:T(8,128)S(1)} %copy_select_fusion), channel_id=1, source_target_pairs={{126,0},{127,1},{0,2},{1,3},{2,4},{3,5},{4,6},{5,7},{6,8},{7,9},{8... | collective-permute-start | bytes 933896 | tf_op jit(solution)/shard_map/ppermute | solution.py:47
  32.5 15.3 %collective-permute-start.1 = (s32[1]{0:T(128)}, s32[1]{0:T(128)}, u32[]{:S(2)}, u32[]{:S(2)}) collective-permute-start(s32[1]{0:T(128)} %select_n.356), channel_id=1, source_target_pairs={{1,0},{2,1},{3,2},{4,3},{5,4},{6,5},{7,6},{8,7},{9,8},{10,9},{11,1... | collective-permute-start | bytes 20 | tf_op jit(solution)/shard_map/ppermute | solution.py:47
  41.6 515.7 %copy-start.185 = (pred[4,4096]{1,0:T(4,128)(4,1)}, pred[4,4096]{1,0:T(4,128)(4,1)S(1)}, u32[]{:S(2)}) copy-start(pred[4,4096]{1,0:T(4,128)(4,1)S(1)} %broadcast_compare_fusion) | copy-start | bytes 49156
  47.8 8.1 collective-permute-start.2
  55.9 7.9 collective-permute-start.3
  63.8 2.5 collective-permute-start
  225.6 53.7 %collective-permute-start.8 = (f32[24,1280]{1,0:T(8,128)}, f32[24,1280]{1,0:T(8,128)}, u32[]{:S(2)}, u32[]{:S(2)}) collective-permute-start(f32[24,1280]{1,0:T(8,128)} %bitcast.121), channel_id=1, source_target_pairs={{126,0},{127,1},{0,2},{1,3},{2,4},{3,5},{4,6},{5,7},{6,8},{7,9},{8... | collective-permute-start | bytes 368648 | tf_op jit(solution)/shard_map/ppermute | solution.py:47
  225.6 55.2 %collective-permute-start.9 = (f32[24,1280]{1,0:T(8,128)}, f32[24,1280]{1,0:T(8,128)}, u32[]{:S(2)}, u32[]{:S(2)}) collective-permute-start(f32[24,1280]{1,0:T(8,128)} %bitcast.121), channel_id=1, source_target_pairs={{127,0},{0,1},{1,2},{2,3},{3,4},{4,5},{5,6},{6,7},{7,8},{8,9},{9,1... | collective-permute-start | bytes 368648 | tf_op jit(solution)/shard_map/ppermute | solution.py:47
  234.9 49.0 %collective-permute-start.10 = (f32[24,1280]{1,0:T(8,128)}, f32[24,1280]{1,0:T(8,128)}, u32[]{:S(2)}, u32[]{:S(2)}) collective-permute-start(f32[24,1280]{1,0:T(8,128)} %bitcast.121), channel_id=1, source_target_pairs={{1,0},{2,1},{3,2},{4,3},{5,4},{6,5},{7,6},{8,7},{9,8},{10,9},{11,1... | collective-permute-start | bytes 368648 | tf_op jit(solution)/shard_map/ppermute | solution.py:47
  235.6 49.9 %collective-permute-start.11 = (f32[24,1280]{1,0:T(8,128)}, f32[24,1280]{1,0:T(8,128)}, u32[]{:S(2)}, u32[]{:S(2)}) collective-permute-start(f32[24,1280]{1,0:T(8,128)} %bitcast.121), channel_id=1, source_target_pairs={{2,0},{3,1},{4,2},{5,3},{6,4},{7,5},{8,6},{9,7},{10,8},{11,9},{12,... | collective-permute-start | bytes 368648 | tf_op jit(solution)/shard_map/ppermute | solution.py:47
  694.0 46.4 %collective-permute-start.12 = (f32[24,1280]{1,0:T(8,128)}, f32[24,1280]{1,0:T(8,128)}, u32[]{:S(2)}, u32[]{:S(2)}) collective-permute-start(f32[24,1280]{1,0:T(8,128)} %bitcast.165), channel_id=1, source_target_pairs={{126,0},{127,1},{0,2},{1,3},{2,4},{3,5},{4,6},{5,7},{6,8},{7,9},{8... | collective-permute-start | bytes 368648 | tf_op jit(solution)/shard_map/ppermute | solution.py:47
  694.0 48.0 %collective-permute-start.13 = (f32[24,1280]{1,0:T(8,128)}, f32[24,1280]{1,0:T(8,128)}, u32[]{:S(2)}, u32[]{:S(2)}) collective-permute-start(f32[24,1280]{1,0:T(8,128)} %bitcast.165), channel_id=1, source_target_pairs={{127,0},{0,1},{1,2},{2,3},{3,4},{4,5},{5,6},{6,7},{7,8},{8,9},{9,1... | collective-permute-start | bytes 368648 | tf_op jit(solution)/shard_map/ppermute | solution.py:47
  695.7 49.4 %collective-permute-start.14 = (f32[24,1280]{1,0:T(8,128)}, f32[24,1280]{1,0:T(8,128)}, u32[]{:S(2)}, u32[]{:S(2)}) collective-permute-start(f32[24,1280]{1,0:T(8,128)} %bitcast.165), channel_id=1, source_target_pairs={{1,0},{2,1},{3,2},{4,3},{5,4},{6,5},{7,6},{8,7},{9,8},{10,9},{11,1... | collective-permute-start | bytes 368648 | tf_op jit(solution)/shard_map/ppermute | solution.py:47
  696.1 50.6 %collective-permute-start.15 = (f32[24,1280]{1,0:T(8,128)}, f32[24,1280]{1,0:T(8,128)}, u32[]{:S(2)}, u32[]{:S(2)}) collective-permute-start(f32[24,1280]{1,0:T(8,128)} %bitcast.165), channel_id=1, source_target_pairs={{2,0},{3,1},{4,2},{5,3},{6,4},{7,5},{8,6},{9,7},{10,8},{11,9},{12,... | collective-permute-start | bytes 368648 | tf_op jit(solution)/shard_map/ppermute | solution.py:47
  1153.3 46.7 %collective-permute-start.16 = (f32[24,1280]{1,0:T(8,128)S(1)}, f32[24,1280]{1,0:T(8,128)}, u32[]{:S(2)}, u32[]{:S(2)}) collective-permute-start(f32[24,1280]{1,0:T(8,128)S(1)} %bitcast.556), channel_id=1, source_target_pairs={{126,0},{127,1},{0,2},{1,3},{2,4},{3,5},{4,6},{5,7},{6,8},{7,9},{8... | collective-permute-start | bytes 368648 | tf_op jit(solution)/shard_map/ppermute | solution.py:47
  1153.4 47.6 %collective-permute-start.17 = (f32[24,1280]{1,0:T(8,128)S(1)}, f32[24,1280]{1,0:T(8,128)}, u32[]{:S(2)}, u32[]{:S(2)}) collective-permute-start(f32[24,1280]{1,0:T(8,128)S(1)} %bitcast.557), channel_id=1, source_target_pairs={{127,0},{0,1},{1,2},{2,3},{3,4},{4,5},{5,6},{6,7},{7,8},{8,9},{9,1... | collective-permute-start | bytes 368648 | tf_op jit(solution)/shard_map/ppermute | solution.py:47
  1155.1 46.8 %collective-permute-start.18 = (f32[24,1280]{1,0:T(8,128)S(1)}, f32[24,1280]{1,0:T(8,128)}, u32[]{:S(2)}, u32[]{:S(2)}) collective-permute-start(f32[24,1280]{1,0:T(8,128)S(1)} %bitcast.558), channel_id=1, source_target_pairs={{1,0},{2,1},{3,2},{4,3},{5,4},{6,5},{7,6},{8,7},{9,8},{10,9},{11,1... | collective-permute-start | bytes 368648 | tf_op jit(solution)/shard_map/ppermute | solution.py:47
  1155.6 47.3 %collective-permute-start.19 = (f32[24,1280]{1,0:T(8,128)S(1)}, f32[24,1280]{1,0:T(8,128)}, u32[]{:S(2)}, u32[]{:S(2)}) collective-permute-start(f32[24,1280]{1,0:T(8,128)S(1)} %bitcast.559), channel_id=1, source_target_pairs={{2,0},{3,1},{4,2},{5,3},{6,4},{7,5},{8,6},{9,7},{10,8},{11,9},{12,... | collective-permute-start | bytes 368648 | tf_op jit(solution)/shard_map/ppermute | solution.py:47
  1221.0 50.1 %copy-start.160 = (pred[16,16,16]{2,1,0:T(8,128)(4,1)S(1)}, pred[16,16,16]{2,1,0:T(8,128)(4,1)}, u32[]{:S(2)}) copy-start(pred[16,16,16]{2,1,0:T(8,128)(4,1)} %constant.2295.clone) | copy-start | bytes 12292
  1221.0 50.1 %copy-start.163 = (pred[16,16,16]{2,1,0:T(8,128)(4,1)S(1)}, pred[16,16,16]{2,1,0:T(8,128)(4,1)}, u32[]{:S(2)}) copy-start(pred[16,16,16]{2,1,0:T(8,128)(4,1)} %constant.2296.clone) | copy-start | bytes 12292
  1221.0 50.1 %copy-start.166 = (pred[16,16,16]{2,1,0:T(8,128)(4,1)S(1)}, pred[16,16,16]{2,1,0:T(8,128)(4,1)}, u32[]{:S(2)}) copy-start(pred[16,16,16]{2,1,0:T(8,128)(4,1)} %constant.2297.clone) | copy-start | bytes 12292
  (342 other events, 6303.2 us)
where the time goes:
time: 1530 us; the launch traced here: 1510 us
  local copies, waits for them, and re-layouts  1340 us (88%)
  other arithmetic  66.1 us (4%)
  starting transfers between devices  54.5 us (4%)
  between operations  20.9 us (1%)
  matrix products  18.2 us (1%)
    scatter x90, local copies, waits for them, and re-layouts, stream_slices(): padded = padded.at[tuple(spots)].set(plane)  624 us
    gather x6, local copies, waits for them, and re-layouts, outgoing_faces(): return post[:, face_pops[:, :, None], face_cells[:, None, :]]  345 us
    pad x54, local copies, waits for them, and re-layouts, stream_slices(): padded = jnp.pad(field[:, pop_id], ((0, 0), (1, 1), (1, 1), (1, 1)))  59 us
    select_n x6, local copies, waits for them, and re-layouts, collide(): return jnp.where(flags[:, None, :] == 1, relaxed, reflected)  57.7 us
    ppermute x20, starting transfers between devices, from_behind(): return lax.ppermute(block, axis, route)  54.5 us
    another operation x62, local copies, waits for them, and re-layouts, stream_slices(): return jnp.stack(results, axis=1).reshape(post.shape)  53.2 us
    another operation x90, local copies, waits for them, and re-layouts  52.3 us
    select_n x18, other arithmetic, stream_slices(): results.append(jnp.where(lacking, field[:, int(opposite[pop_id])], read))  50.9 us
  transfers between devices with their start and end apart: 20, of which 3 were waited for; matrix products, arithmetic and copies ran while one was open for 9% of the time, Pallas kernels for 0%

commit v1 on v0

v1 whole, which is shorter than its diff:
```python
import functools

import jax
import jax.numpy as jnp
import numpy as np
from jax import lax
from jax.experimental import pallas as pl
from jax.experimental.pallas import tpu as pltpu
from jax.sharding import PartitionSpec as P

EDGE = 16
BLK_DEV = 4
REACH = 2
STEPS = 3
POPS = 19
ROWS = EDGE**3 // 128
BLOCK_ROWS = POPS * ROWS
FACE_ROWS = 16
FACES = 6 * BLK_DEV
PEER_FACES = 6
OFFSETS = (-2, -1, 1, 2)
REST_DENSITY = 36.0
SHEAR_RATE = 1.6
VMEM_BYTES = 24 * 1024 * 1024

VELOCITIES = [
    (0, 0, 0), (1, 0, 0), (-1, 0, 0), (0, 1, 0), (0, -1, 0), (0, 0, 1), (0, 0, -1),
    (1, 1, 0), (-1, -1, 0), (1, -1, 0), (-1, 1, 0), (1, 0, 1), (-1, 0, -1), (1, 0, -1),
    (-1, 0, 1), (0, 1, 1), (0, -1, -1), (0, 1, -1), (0, -1, 1),
]
OPPOSITE = [VELOCITIES.index((-a, -b, -c)) for a, b, c in VELOCITIES]
FACE_POPS = [
    [i for i, c in enumerate(VELOCITIES) if c[face // 2] == (1 if face % 2 else -1)]
    for face in range(6)
]
WEIGHTS = [1.0 / 3.0] + [1.0 / 18.0] * 6 + [1.0 / 36.0] * 12


def moment_constants():
    c = np.array(VELOCITIES) * 1.0
    x, y, z = c[:, 0], c[:, 1], c[:, 2]
    s = x * x + y * y + z * z
    rows = {
        "e": 19 * s - 30,
        "eps": (21 * s * s - 53 * s + 24) / 2,
        "q": (5 * s - 9) * x,
        "pxx": 3 * x * x - s,
        "pixx": (3 * s - 5) * (3 * x * x - s),
        "pww": y * y - z * z,
        "piww": (3 * s - 5) * (y * y - z * z),
        "pxy": x * y,
        "m": x * (y * y - z * z),
    }
    rates = {
        "e": 1.19, "eps": 1.4, "q": 1.2, "pxx": SHEAR_RATE, "pixx": 1.4, "pww": SHEAR_RATE,
        "piww": 1.4, "pxy": SHEAR_RATE, "m": 1.98,
    }
    scale = {k: float(rates[k] / np.sum(rows[k] ** 2)) for k in rows}
    w = np.array(WEIGHTS)

    def of(row, term):
        return float(np.sum(rows[row] * w * term))

    square = [(4.5 * x * x - 1.5) / REST_DENSITY, (4.5 * y * y - 1.5) / REST_DENSITY,
              (4.5 * z * z - 1.5) / REST_DENSITY]
    terms = {
        "e_rho": of("e", 1.0), "eps_rho": of("eps", 1.0), "q_j": of("q", 3 * x),
        "pxy_jj": of("pxy", 9.0 * x * y / REST_DENSITY),
    }
    for name in ("e", "eps", "pxx", "pixx", "pww", "piww"):
        terms[name] = [of(name, t) for t in square]
    return scale, terms


SCALE, TERMS = moment_constants()


def relax(f):
    ex, ey, ez = f[1] + f[2], f[3] + f[4], f[5] + f[6]
    ox, oy, oz = f[1] - f[2], f[3] - f[4], f[5] - f[6]
    a, oa = f[7] + f[8], f[7] - f[8]
    b, ob = f[9] + f[10], f[9] - f[10]
    c, oc = f[11] + f[12], f[11] - f[12]
    d, od = f[13] + f[14], f[13] - f[14]
    g, og = f[15] + f[16], f[15] - f[16]
    h, oh = f[17] + f[18], f[17] - f[18]
    sxy, sxz, syz = a + b, c + d, g + h
    axial = ex + (ey + ez)
    diagonal = sxy + (sxz + syz)
    rho = f[0] + (axial + diagonal)
    xy_x, xz_x = oa + ob, oc + od
    xy_y, yz_y = oa - ob, og + oh
    xz_z, yz_z = oc - od, og - oh
    dx, dy, dz = xy_x + xz_x, xy_y + yz_y, xz_z + yz_z
    jx, jy, jz = ox + dx, oy + dy, oz + dz
    xx, yy, zz = jx * jx, jy * jy, jz * jz

    def even(name, value):
        k = TERMS[name]
        if abs(k[1] - k[2]) < 1e-12 and abs(k[0] - k[1]) < 1e-12:
            quad = (k[0] * SCALE[name]) * (xx + yy + zz)
        elif abs(k[0]) < 1e-12:
            quad = (k[1] * SCALE[name]) * (yy - zz)
        else:
            quad = (k[0] * SCALE[name]) * xx + (k[1] * SCALE[name]) * (yy + zz)
        return SCALE[name] * value - quad

    t_e = even("e", 8.0 * diagonal - 30.0 * f[0] - 11.0 * axial - TERMS["e_rho"] * rho)
    t_eps = even("eps", 12.0 * f[0] - 4.0 * axial + diagonal - TERMS["eps_rho"] * rho)
    p_axis = 2.0 * ex - (ey + ez)
    p_diag = (sxy + sxz) - 2.0 * syz
    w_axis = ey - ez
    w_diag = sxy - sxz
    t_pxx = even("pxx", p_axis + p_diag)
    t_pixx = even("pixx", p_diag - 2.0 * p_axis)
    t_pww = even("pww", w_axis + w_diag)
    t_piww = even("piww", w_diag - 2.0 * w_axis)
    k_p = TERMS["pxy_jj"]
    t_xy = SCALE["pxy"] * ((a - b) - k_p * (jx * jy))
    t_yz = SCALE["pxy"] * ((g - h) - k_p * (jy * jz))
    t_xz = SCALE["pxy"] * ((c - d) - k_p * (jx * jz))
    k_q = TERMS["q_j"]
    t_qx = SCALE["q"] * (dx - 4.0 * ox - k_q * jx)
    t_qy = SCALE["q"] * (dy - 4.0 * oy - k_q * jy)
    t_qz = SCALE["q"] * (dz - 4.0 * oz - k_q * jz)
    t_mx = SCALE["m"] * (xy_x - xz_x)
    t_my = SCALE["m"] * (yz_y - xy_y)
    t_mz = SCALE["m"] * (xz_z - yz_z)

    base_axis = -11.0 * t_e - 4.0 * t_eps
    base_diag = 8.0 * t_e + t_eps
    p1 = t_pxx - 2.0 * t_pixx
    w1 = t_pww - 2.0 * t_piww
    p2 = t_pxx + t_pixx
    w2 = t_pww + t_piww
    kx = base_axis + 2.0 * p1
    k_yz = base_axis - p1
    ky, kz = k_yz + w1, k_yz - w1
    near = base_diag + p2
    kxy, kxz, kyz = near + w2, near - w2, base_diag - 2.0 * p2
    qx4, qy4, qz4 = -4.0 * t_qx, -4.0 * t_qy, -4.0 * t_qz
    xp, xm = t_qx + t_mx, t_qx - t_mx
    yp, ym = t_qy + t_my, t_qy - t_my
    zp, zm = t_qz + t_mz, t_qz - t_mz
    pairs = [
        (kx, qx4), (ky, qy4), (kz, qz4),
        (kxy + t_xy, xp + ym), (kxy - t_xy, xp - ym),
        (kxz + t_xz, xm + zp), (kxz - t_xz, xm - zp),
        (kyz + t_yz, yp + zm), (kyz - t_yz, yp - zm),
    ]
    out = [f[0] - (12.0 * t_eps - 30.0 * t_e)]
    for n, (same, odd) in enumerate(pairs):
        out.append(f[2 * n + 1] - (same + odd))
        out.append(f[2 * n + 2] - (same - odd))
    return out


def collide_block(source, flags, target):
    for chunk in range(ROWS // 8):
        rows = [pl.ds(i * ROWS + chunk * 8, 8) for i in range(POPS)]
        f = [source(r) for r in rows]
        fluid = flags(pl.ds(chunk * 8, 8)) == 1
        post = relax(f)
        for i in range(POPS):
            target(rows[i], jnp.where(fluid, post[i], f[OPPOSITE[i]]))


def lanes_of(shape):
    return lax.broadcasted_iota(jnp.int32, shape, 1)


def roll_lanes(value, shift):
    shift %= 128
    return pltpu.roll(value, shift, 1) if shift else value


def pack_faces(load, store):
    lane = lanes_of((FACE_ROWS, 128))
    for face in (0, 1):
        first = 0 if face == 0 else ROWS - 2
        for k, i in enumerate(FACE_POPS[face]):
            store(face, slice(2 * k, 2 * k + 2), load(pl.ds(i * ROWS + first, 2)))
    for face in (2, 3):
        total = None
        for k, i in enumerate(FACE_POPS[face]):
            plane = load(pl.ds(i * ROWS + face - 2, EDGE, stride=2))
            plane = roll_lanes(plane, 16 * k if face == 2 else 16 * k - 112)
            total = plane if total is None else jnp.where(lane // 16 == k, plane, total)
        store(face, slice(0, FACE_ROWS), total)
    for face in (4, 5):
        total = None
        for half in range(2):
            for k, i in enumerate(FACE_POPS[face]):
                spot = 5 * half + k
                plane = load(pl.ds(i * ROWS + half * 16, 16))
                plane = roll_lanes(plane, spot if face == 4 else spot - 15)
                total = plane if total is None else jnp.where(lane % 16 == spot, plane, total)
        store(face, slice(0, FACE_ROWS), total)


def edge_mask(axis, part, row, lane):
    if axis == 0:
        return row < 2 if part > 0 else row >= ROWS - 2
    if axis == 1:
        if part > 0:
            return (row % 2 == 0) & (lane < 16)
        return (row % 2 == 1) & (lane >= 112)
    return lane % 16 == (0 if part > 0 else 15)


PAD = 8


def stream_block(load, ghost, wide, store):
    row = lax.broadcasted_iota(jnp.int32, (ROWS, 128), 0)
    lane = lanes_of((ROWS, 128))
    lane16 = lanes_of((16, 128))
    for i, (cx, cy, cz) in enumerate(VELOCITIES):
        shift = 16 * cy + cz
        faces = [0 if cx > 0 else 1, 2 if cy > 0 else 3, 4 if cz > 0 else 5]
        place = [FACE_POPS[face ^ 1].index(i) if part else None for face, part in zip(faces, (cx, cy, cz))]
        post = load(pl.ds(i * ROWS, ROWS))
        moved = roll_lanes(post, shift)
        if cz:
            plane = ghost(faces[2], slice(0, 16))
            spot = (0 if cz > 0 else 15) + 16 * cy
            incoming = jnp.concatenate(
                [roll_lanes(plane, spot - place[2]), roll_lanes(plane, spot - 5 - place[2])], axis=0
            )
            moved = jnp.where(lane % 16 == spot % 16, incoming, moved)
        if cx or cy:
            wide[i, PAD : PAD + ROWS, :] = moved
            if cx:
                two = ghost(faces[0], slice(2 * place[0], 2 * place[0] + 2))
                start = PAD - 2 if cx > 0 else PAD + ROWS
                wide[i, start : start + 2, :] = roll_lanes(two, shift)
            if cy:
                plane = ghost(faces[1], slice(0, 16))
                plane = roll_lanes(plane, (0 if cy > 0 else 112) - 16 * place[1] + cz)
                spots = pl.ds(PAD - 1 if cy > 0 else PAD + 2, EDGE, stride=2)
                keep = lane16 >= 16 if cy > 0 else lane16 < 112
                wide[i, spots, :] = jnp.where(keep, wide[i, spots, :], plane)
            moved = wide[i, PAD - 2 * cx : PAD - 2 * cx + ROWS, :]
            if cy:
                start = PAD - 2 * cx - cy
                across = wide[i, start : start + ROWS, :]
                moved = jnp.where(lane >= 16 if cy > 0 else lane < 112, moved, across)
        parts = [(axis, part) for axis, part in enumerate((cx, cy, cz)) if part]
        if len(parts) == 2:
            beyond = edge_mask(*parts[0], row, lane) & edge_mask(*parts[1], row, lane)
            moved = jnp.where(beyond, load(pl.ds(OPPOSITE[i] * ROWS, ROWS)), moved)
        store(pl.ds(i * ROWS, ROWS), moved)


def bounce_face(face, load, new_load, store):
    row = lax.broadcasted_iota(jnp.int32, (ROWS, 128), 0)
    lane = lanes_of((ROWS, 128))
    part = -1 if face % 2 else 1
    mask = edge_mask(face // 2, part, row, lane)
    for i in FACE_POPS[face ^ 1]:
        rows = pl.ds(i * ROWS, ROWS)
        store(rows, jnp.where(mask, load(pl.ds(OPPOSITE[i] * ROWS, ROWS)), new_load(rows)))


def cycle_offset(place, cycle):
    offset = lax.shift_right_arithmetic(place, 2) - lax.axis_index("blocks")
    offset = jnp.where(offset > REACH, offset - cycle, offset)
    return jnp.where(offset < -REACH, offset + cycle, offset)


def pack_kernel(cycle, plan, pdfs, *outs):
    offsets = [cycle_offset(plan[j], cycle) for j in range(BLK_DEV)]
    for out, offset in zip(outs, OFFSETS + (0,)):
        slot = jnp.int32(0)
        for j in range(BLK_DEV):
            slot = jnp.where(offsets[j] == offset, j, slot)
        for first in range(0, POPS, 8):
            count = min(8, POPS - first)
            for c in range(ROWS):
                out[pl.ds(first * ROWS + c, count, stride=ROWS), :] = pdfs[
                    slot, first : first + count, c * 128 : (c + 1) * 128
                ]


def index_kernel(cycle, neighbours, sends, receives, ranks):
    for n in range(FACES):
        sends[n] = 0
    for n in range((len(OFFSETS) + 1) * FACES):
        ranks[n] = -1
    counts = [jnp.int32(0) for _ in OFFSETS]
    for n in range(FACES):
        place = neighbours[n // 6, n % 6]
        offset = cycle_offset(place, cycle)
        across = (place & 3) * 6 + (n % 6 ^ 1)
        receives[n] = jnp.where(place < 0, -1, FACES + across)
        for o, value in enumerate(OFFSETS):
            mine = (place >= 0) & (offset == value)
            at = jnp.where(mine, o, len(OFFSETS)) * FACES
            ranks[at + across] = n

            @pl.when(mine & (counts[o] < PEER_FACES))
            def _(o=o, count=counts[o]):
                sends[o * PEER_FACES + count] = n

            counts[o] = counts[o] + mine.astype(jnp.int32)
    for o in range(len(OFFSETS)):
        seen = jnp.int32(0)
        for key in range(FACES):
            face = ranks[o * FACES + key]
            found = face >= 0

            @pl.when(found)
            def _(o=o, seen=seen, face=face):
                receives[face] = o * PEER_FACES + jnp.minimum(seen, PEER_FACES - 1)

            seen = seen + found.astype(jnp.int32)


def send_faces(sends, faces, outs):
    for o, out in enumerate(outs):
        for r in range(PEER_FACES):
            out[r * FACE_ROWS : (r + 1) * FACE_ROWS, :] = faces[sends[o * PEER_FACES + r]]


def pack_block(post, faces, b):
    def store(face, rows, value):
        faces[b * 6 + face, rows, :] = value

    pack_faces(lambda rows: post[b, rows, :], store)


def first_kernel(cycle, plan, sends, flags, *refs):
    arrived, (post, faces), outs = refs[:5], refs[5:7], refs[7:]
    for j in range(BLK_DEV):
        offset = cycle_offset(plan[j], cycle)
        slot = plan[j] & 3
        for source, value in zip(arrived, OFFSETS + (0,)):

            @pl.when(offset == value)
            def _(source=source):
                def store(rows, value):
                    post[slot, rows, :] = value

                collide_block(lambda r: source[r, :], lambda r: flags[slot, r, :], store)

    @pl.loop(0, BLK_DEV)
    def _(b):
        pack_block(post, faces, b)

    send_faces(sends, faces, outs)


def fill_pool(pool, arrived, own):
    for o, source in enumerate(arrived):
        for r in range(PEER_FACES):
            pool[o * PEER_FACES + r] = source[r * FACE_ROWS : (r + 1) * FACE_ROWS, :]
    pool[FACES:] = own[...]


def move_block(b, receives, post, pool, wide, new):
    spots = [receives[b * 6 + face] for face in range(6)]
    safe = [jnp.maximum(spot, 0) for spot in spots]

    def store(rows, value):
        new[rows, :] = value

    stream_block(
        lambda rows: post[b, rows, :],
        lambda face, rows: pool[safe[face], rows, :],
        wide,
        store,
    )
    for face in range(6):

        @pl.when(spots[face] < 0)
        def _(face=face):
            bounce_face(face, lambda rows: post[b, rows, :], lambda rows: new[rows, :], store)


def step_kernel(sends, receives, flags, post, own, *refs):
    arrived, (post_out, faces), outs, (pool, wide, new) = refs[:4], refs[4:6], refs[6:10], refs[10:]
    fill_pool(pool, arrived, own)

    @pl.loop(0, BLK_DEV)
    def _(b):
        move_block(b, receives, post, pool, wide, new)

        def store(rows, value):
            post_out[b, rows, :] = value

        collide_block(lambda r: new[r, :], lambda r: flags[b, r, :], store)
        pack_block(post_out, faces, b)

    send_faces(sends, faces, outs)


def last_kernel(receives, post, own, *refs):
    arrived, out, (pool, wide, new) = refs[:4], refs[4], refs[5:]
    fill_pool(pool, arrived, own)

    @pl.loop(0, BLK_DEV)
    def _(b):
        move_block(b, receives, post, pool, wide, new)
        for first in range(0, POPS, 8):
            count = min(8, POPS - first)
            for c in range(ROWS):
                out[b, first : first + count, c * 128 : (c + 1) * 128] = new[
                    pl.ds(first * ROWS + c, count, stride=ROWS), :
                ]


SMEM = pl.BlockSpec(memory_space=pltpu.SMEM)
VMEM = pl.BlockSpec(memory_space=pltpu.VMEM)
BLOCK = jax.ShapeDtypeStruct((BLOCK_ROWS, 128), jnp.float32)
POST = jax.ShapeDtypeStruct((BLK_DEV, BLOCK_ROWS, 128), jnp.float32)
OWN = jax.ShapeDtypeStruct((FACES, FACE_ROWS, 128), jnp.float32)
SENT = jax.ShapeDtypeStruct((PEER_FACES * FACE_ROWS, 128), jnp.float32)
MOVE_SCRATCH = [
    pltpu.VMEM((2 * FACES, FACE_ROWS, 128), jnp.float32),
    pltpu.VMEM((POPS, ROWS + 2 * PAD, 128), jnp.float32),
    pltpu.VMEM((BLOCK_ROWS, 128), jnp.float32),
]


def call(kernel, in_specs, out_shapes, out_specs, scratch=(), flops=0, bytes_accessed=0):
    return pl.pallas_call(
        kernel,
        in_specs=in_specs,
        out_shape=out_shapes,
        out_specs=out_specs,
        scratch_shapes=list(scratch),
        compiler_params=pltpu.CompilerParams(vmem_limit_bytes=VMEM_BYTES),
        cost_estimate=pl.CostEstimate(
            flops=flops, bytes_accessed=bytes_accessed, transcendentals=0
        ),
    )


def from_behind(value, distance, cycle):
    route = [((i - distance) % cycle, i) for i in range(cycle)]
    return lax.ppermute(value, "blocks", route)


def body(pdfs, plan, neighbours, flags):
    cycle = lax.axis_size("blocks")
    size = 4 * pdfs.size
    sent = call(
        functools.partial(pack_kernel, cycle), [SMEM, VMEM], [BLOCK] * 5, [VMEM] * 5,
        bytes_accessed=2 * size,
    )(plan, pdfs)
    arrived = [from_behind(value, o, cycle) for value, o in zip(sent, OFFSETS)] + [sent[4]]
    table = jax.ShapeDtypeStruct((FACES,), jnp.int32)
    sends, receives = call(
        functools.partial(index_kernel, cycle), [SMEM], [table] * 2, [SMEM] * 2,
        [pltpu.SMEM(((len(OFFSETS) + 1) * FACES,), jnp.int32)], bytes_accessed=1000,
    )(neighbours)
    cells = flags.reshape(BLK_DEV, ROWS, 128)
    post, own, *faces = call(
        functools.partial(first_kernel, cycle), [SMEM, SMEM, VMEM] + [VMEM] * 5,
        [POST, OWN] + [SENT] * 4, [VMEM] * 6, flops=300 * pdfs.size // POPS, bytes_accessed=2 * size,
    )(plan, sends, cells, *arrived)
    for _ in range(STEPS - 1):
        came = [from_behind(value, -o, cycle) for value, o in zip(faces[::-1], OFFSETS)]
        post, own, *faces = call(
            step_kernel, [SMEM, SMEM, VMEM, VMEM, VMEM] + [VMEM] * 4,
            [POST, OWN] + [SENT] * 4, [VMEM] * 6, MOVE_SCRATCH,
            flops=300 * pdfs.size // POPS, bytes_accessed=2 * size,
        )(sends, receives, cells, post, own, *came)
    came = [from_behind(value, -o, cycle) for value, o in zip(faces[::-1], OFFSETS)]
    return call(
        last_kernel, [SMEM, VMEM, VMEM] + [VMEM] * 4,
        jax.ShapeDtypeStruct(pdfs.shape, jnp.float32), VMEM, MOVE_SCRATCH,
        bytes_accessed=2 * size,
    )(receives, post, own, *came)


def solution(mesh):
    placed = (P("blocks", None, None), P("blocks"), P("blocks", None), P("blocks", None))
    return jax.shard_map(
        body, mesh=mesh, in_specs=placed, out_specs=P("blocks", None, None), check_vma=False
    )
```

time: 1530 us -> 75.9 us (0.05); the launches traced: 1510 us -> 74.5 us
  local copies, waits for them, and re-layouts: 1340 us -> 3.89 us
  other arithmetic: 66.1 us -> 0 us
  between operations: 20.9 us -> 0.14 us
  matrix products: 18.2 us -> 0 us
  starting transfers between devices: 54.5 us -> 38.4 us
    scatter x91 -> x0, local copies, waits for them, and re-layouts: 627 us -> none  [the longest x90 624 us: stream_slices(): padded = padded.at[tuple(spots)].set(plane)]
    gather x14 -> x0, local copies, waits for them, and re-layouts: 363 us -> none  [the longest x6 345 us: outgoing_faces(): return post[:, face_pops[:, :, None], face_cells[:, None, :]]]
    another operation x152 -> x0, local copies, waits for them, and re-layouts: 106 us -> none  [the longest x62 53.2 us: stream_slices(): return jnp.stack(results, axis=1).reshape(post.shape)]
    pad x54 -> x0, local copies, waits for them, and re-layouts: 59 us -> none  [stream_slices(): padded = jnp.pad(field[:, pop_id], ((0, 0), (1, 1), (1, 1), (1, 1)))]
    select_n x6 -> x0, local copies, waits for them, and re-layouts: 57.7 us -> none  [collide(): return jnp.where(flags[:, None, :] == 1, relaxed, reflected)]
    select_n x27 -> x0, other arithmetic: 52.6 us -> none  [the longest x18 50.9 us: stream_slices(): results.append(jnp.where(lacking, field[:, int(opposite[pop_id])], read))]
    unnamed x728 -> x8, local copies, waits for them, and re-layouts: 35.3 us -> 2.05 us
    reduce_sum x38 -> x0, local copies, waits for them, and re-layouts: 32.5 us -> none  [collide(): density = jnp.sum(pdfs, axis=1)]
  transfers between devices with their start and end apart: 20 -> 16, of which waited for: 3 -> 8; matrix products, arithmetic and copies ran while one was open for 9% -> 0% of each run, Pallas kernels for 0% -> 3%
where the time goes in v1:
time: 75.9 us; the launch traced here: 74.5 us
  starting transfers between devices  38.4 us (51%)
  waiting for transfers between devices  19.1 us (25%)
  Pallas kernels  12.9 us (17%)
  local copies, waits for them, and re-layouts  3.89 us (5%)
    ppermute x16, starting transfers between devices, from_behind(): return lax.ppermute(value, 'blocks', route)  38.4 us
    ppermute x16, waiting for transfers between devices, from_behind(): return lax.ppermute(value, 'blocks', route)  19.1 us
    pallas_call x2, Pallas kernels, body(): call(step_kernel, [SMEM, SMEM, VMEM, VMEM, VMEM] + [VMEM] * 4, [POST, OWN...  5.35 us
    pallas_call x1, Pallas kernels, body(): call(last_kernel, [SMEM, VMEM, VMEM] + [VMEM] * 4, jax.ShapeDtypeStruct(p...  2.38 us
    unnamed x8, local copies, waits for them, and re-layouts  2.05 us
    pallas_call x1, Pallas kernels, body(): call(functools.partial(index_kernel, cycle), [SMEM], [table] * 2, [SMEM]...  2.02 us
    pallas_call x1, local copies, waits for them, and re-layouts, body(): call(last_kernel, [SMEM, VMEM, VMEM] + [VMEM] * 4, jax.ShapeDtypeStruct(p...  1.84 us
    pallas_call x1, Pallas kernels, body(): call(functools.partial(first_kernel, cycle), [SMEM, SMEM, VMEM] + [VMEM]...  1.72 us
  transfers between devices with their start and end apart: 16, of which 8 were waited for; matrix products, arithmetic and copies ran while one was open for 0% of the time, Pallas kernels for 3%

profile of v1, /device:TPU:1, one launch (start us, length us, event | category | flops | bytes accessed | tf_op | source)
XLA Modules:
  0.0 74.5 jit_solution(7527357961691566953)
XLA Ops:
  0.0 2.0 %copy.5.pdfs = f32[4,19,4096]{2,1,0:T(8,128)S(1)} copy(f32[4,19,4096]{2,0,1:T(4,128)} %param.4) | data formatting | bytes 2490368 | tf_op args[0]
  2.1 1.5 %shard_map.47 = (f32[608,128]{1,0:T(8,128)S(1)}, f32[608,128]{1,0:T(8,128)S(1)}, f32[608,128]{1,0:T(8,128)S(1)}, f32[608,128]{1,0:T(8,128)S(1)}, f32[608,128]{1,0:T(8,128)S(1)}) custom-call(s32[4]{0:T(128)S(1)} %copy-done, f32[4,19,4096]{2,1,0:T(8,128)S(1)} %copy.5.pdfs), custom_call_target="tpu_custom_call" | custom-call | bytes 2490368 | tf_op jit(solution)/shard_map/pallas_call | solution.py:447
  3.6 9.3 %collective-permute-start = (f32[608,128]{1,0:T(8,128)S(1)}, f32[608,128]{1,0:T(8,128)S(1)}, u32[]{:S(2)}, u32[]{:S(2)}) collective-permute-start(f32[608,128]{1,0:T(8,128)S(1)} %get-tuple-element.32), channel_id=1, source_target_pairs={{2,0},{3,1},{4,2},{5,3},{6,4},{7,5},{8,6},{9,7},{10,8},{11,9},{12,... | collective-permute-start | bytes 933896 | tf_op jit(solution)/shard_map/ppermute | solution.py:441
  12.9 1.0 %collective-permute-start.1 = (f32[608,128]{1,0:T(8,128)S(1)}, f32[608,128]{1,0:T(8,128)S(1)}, u32[]{:S(2)}, u32[]{:S(2)}) collective-permute-start(f32[608,128]{1,0:T(8,128)S(1)} %get-tuple-element.33), channel_id=1, source_target_pairs={{1,0},{2,1},{3,2},{4,3},{5,4},{6,5},{7,6},{8,7},{9,8},{10,9},{11,1... | collective-permute-start | bytes 933896 | tf_op jit(solution)/shard_map/ppermute | solution.py:441
  13.8 0.8 %collective-permute-start.2 = (f32[608,128]{1,0:T(8,128)S(1)}, f32[608,128]{1,0:T(8,128)S(1)}, u32[]{:S(2)}, u32[]{:S(2)}) collective-permute-start(f32[608,128]{1,0:T(8,128)S(1)} %get-tuple-element.34), channel_id=1, source_target_pairs={{127,0},{0,1},{1,2},{2,3},{3,4},{4,5},{5,6},{6,7},{7,8},{8,9},{9,1... | collective-permute-start | bytes 933896 | tf_op jit(solution)/shard_map/ppermute | solution.py:441
  14.6 2.0 %shard_map.46 = (s32[24]{0:T(128)S(1)}, s32[24]{0:T(128)S(1)}) custom-call(s32[4,6]{1,0:T(4,128)S(1)} %copy-done.1), custom_call_target="tpu_custom_call" | custom-call | bytes 1000 | tf_op jit(solution)/shard_map/pallas_call | solution.py:453
  16.7 2.2 %collective-permute-done.refs_0_ = f32[608,128]{1,0:T(8,128)S(1)} collective-permute-done((f32[608,128]{1,0:T(8,128)S(1)}, f32[608,128]{1,0:T(8,128)S(1)}, u32[]{:S(2)}, u32[]{:S(2)}) %collective-permute-start) | collective-permute-done | bytes 311328 | tf_op jit(solution)/shard_map/ppermute | solution.py:441
  19.2 2.0 %collective-permute-done.2.refs_2_ = f32[608,128]{1,0:T(8,128)S(1)} collective-permute-done((f32[608,128]{1,0:T(8,128)S(1)}, f32[608,128]{1,0:T(8,128)S(1)}, u32[]{:S(2)}, u32[]{:S(2)}) %collective-permute-start.2) | collective-permute-done | bytes 311328 | tf_op jit(solution)/shard_map/ppermute | solution.py:441
  21.2 10.3 %collective-permute-done.3.refs_3_ = f32[608,128]{1,0:T(8,128)S(1)} collective-permute-done((f32[608,128]{1,0:T(8,128)S(1)}, f32[608,128]{1,0:T(8,128)S(1)}, u32[]{:S(2)}, u32[]{:S(2)}) %collective-permute-start.3) | collective-permute-done | bytes 311328 | tf_op jit(solution)/shard_map/ppermute | solution.py:441
  31.6 1.7 %shard_map.48 = (f32[4,608,128]{2,1,0:T(8,128)S(1)}, f32[24,16,128]{2,1,0:T(8,128)S(1)}, f32[96,128]{1,0:T(8,128)S(1)}, f32[96,128]{1,0:T(8,128)S(1)}, f32[96,128]{1,0:T(8,128)S(1)}, /*index=5*/f32[96,128]{1,0:T(8,128)S(1)}) custom-call(s32[4]{0:T(128)S(1)} %copy-done, s32[24]{0:T(128)S(1)} %get-tuple-element.31.sends, s32[4,32,128]{2,1,0:T(8,128)S(1)} %bitcast.4, ...), custom_call_target="tpu_custom_call" | custom-call | flops 4915200 | bytes 2490368 | tf_op jit(solution)/shard_map/pallas_call | solution.py:458
  34.0 6.8 %collective-permute-start.7 = (f32[96,128]{1,0:T(8,128)S(1)}, f32[96,128]{1,0:T(8,128)S(1)}, u32[]{:S(2)}, u32[]{:S(2)}) collective-permute-start(f32[96,128]{1,0:T(8,128)S(1)} %get-tuple-element.42), channel_id=1, source_target_pairs={{2,0},{3,1},{4,2},{5,3},{6,4},{7,5},{8,6},{9,7},{10,8},{11,9},{12,... | collective-permute-start | bytes 147464 | tf_op jit(solution)/shard_map/ppermute | solution.py:441
  40.8 1.0 %collective-permute-done.4.refs_0_ = f32[96,128]{1,0:T(8,128)S(1)} collective-permute-done((f32[96,128]{1,0:T(8,128)S(1)}, f32[96,128]{1,0:T(8,128)S(1)}, u32[]{:S(2)}, u32[]{:S(2)}) %collective-permute-start.4) | collective-permute-done | bytes 49184 | tf_op jit(solution)/shard_map/ppermute | solution.py:441
  42.3 2.7 %shard_map.49 = (f32[4,608,128]{2,1,0:T(8,128)S(1)}, f32[24,16,128]{2,1,0:T(8,128)S(1)}, f32[96,128]{1,0:T(8,128)S(1)}, f32[96,128]{1,0:T(8,128)S(1)}, f32[96,128]{1,0:T(8,128)S(1)}, /*index=5*/f32[96,128]{1,0:T(8,128)S(1)}) custom-call(s32[24]{0:T(128)S(1)} %get-tuple-element.31.sends, s32[24]{0:T(128)S(1)} %get-tuple-element.30.receives, ...), custom_call_target="tpu_custom_call" | custom-call | flops 4915200 | bytes 2490368 | tf_op jit(solution)/shard_map/pallas_call | solution.py:464
  45.0 1.8 %collective-permute-start.9 = (f32[96,128]{1,0:T(8,128)S(1)}, f32[96,128]{1,0:T(8,128)S(1)}, u32[]{:S(2)}, u32[]{:S(2)}) collective-permute-start(f32[96,128]{1,0:T(8,128)S(1)} %get-tuple-element.46), channel_id=1, source_target_pairs={{127,0},{0,1},{1,2},{2,3},{3,4},{4,5},{5,6},{6,7},{7,8},{8,9},{9,1... | collective-permute-start | bytes 147464 | tf_op jit(solution)/shard_map/ppermute | solution.py:441
  46.9 0.8 %collective-permute-start.10 = (f32[96,128]{1,0:T(8,128)S(1)}, f32[96,128]{1,0:T(8,128)S(1)}, u32[]{:S(2)}, u32[]{:S(2)}) collective-permute-start(f32[96,128]{1,0:T(8,128)S(1)} %get-tuple-element.47), channel_id=1, source_target_pairs={{1,0},{2,1},{3,2},{4,3},{5,4},{6,5},{7,6},{8,7},{9,8},{10,9},{11,1... | collective-permute-start | bytes 147464 | tf_op jit(solution)/shard_map/ppermute | solution.py:441
  47.7 7.0 %collective-permute-start.11 = (f32[96,128]{1,0:T(8,128)S(1)}, f32[96,128]{1,0:T(8,128)S(1)}, u32[]{:S(2)}, u32[]{:S(2)}) collective-permute-start(f32[96,128]{1,0:T(8,128)S(1)} %get-tuple-element.48), channel_id=1, source_target_pairs={{2,0},{3,1},{4,2},{5,3},{6,4},{7,5},{8,6},{9,7},{10,8},{11,9},{12,... | collective-permute-start | bytes 147464 | tf_op jit(solution)/shard_map/ppermute | solution.py:441
  54.7 1.3 %collective-permute-done.11.refs_3_ = f32[96,128]{1,0:T(8,128)S(1)} collective-permute-done((f32[96,128]{1,0:T(8,128)S(1)}, f32[96,128]{1,0:T(8,128)S(1)}, u32[]{:S(2)}, u32[]{:S(2)}) %collective-permute-start.11) | collective-permute-done | bytes 49184 | tf_op jit(solution)/shard_map/ppermute | solution.py:441
  56.0 2.7 %shard_map.50 = (f32[4,608,128]{2,1,0:T(8,128)S(1)}, f32[24,16,128]{2,1,0:T(8,128)S(1)}, f32[96,128]{1,0:T(8,128)S(1)}, f32[96,128]{1,0:T(8,128)S(1)}, f32[96,128]{1,0:T(8,128)S(1)}, /*index=5*/f32[96,128]{1,0:T(8,128)S(1)}) custom-call(s32[24]{0:T(128)S(1)} %get-tuple-element.31.sends, s32[24]{0:T(128)S(1)} %get-tuple-element.30.receives, ...), custom_call_target="tpu_custom_call" | custom-call | flops 4915200 | bytes 2490368 | tf_op jit(solution)/shard_map/pallas_call | solution.py:464
  58.7 2.2 %collective-permute-start.13 = (f32[96,128]{1,0:T(8,128)S(1)}, f32[96,128]{1,0:T(8,128)S(1)}, u32[]{:S(2)}, u32[]{:S(2)}) collective-permute-start(f32[96,128]{1,0:T(8,128)S(1)} %get-tuple-element.52), channel_id=1, source_target_pairs={{127,0},{0,1},{1,2},{2,3},{3,4},{4,5},{5,6},{6,7},{7,8},{8,9},{9,1... | collective-permute-start | bytes 147464 | tf_op jit(solution)/shard_map/ppermute | solution.py:441
  61.0 0.8 %collective-permute-start.14 = (f32[96,128]{1,0:T(8,128)S(1)}, f32[96,128]{1,0:T(8,128)S(1)}, u32[]{:S(2)}, u32[]{:S(2)}) collective-permute-start(f32[96,128]{1,0:T(8,128)S(1)} %get-tuple-element.53), channel_id=1, source_target_pairs={{1,0},{2,1},{3,2},{4,3},{5,4},{6,5},{7,6},{8,7},{9,8},{10,9},{11,1... | collective-permute-start | bytes 147464 | tf_op jit(solution)/shard_map/ppermute | solution.py:441
  61.8 7.1 %collective-permute-start.15 = (f32[96,128]{1,0:T(8,128)S(1)}, f32[96,128]{1,0:T(8,128)S(1)}, u32[]{:S(2)}, u32[]{:S(2)}) collective-permute-start(f32[96,128]{1,0:T(8,128)S(1)} %get-tuple-element.54), channel_id=1, source_target_pairs={{2,0},{3,1},{4,2},{5,3},{6,4},{7,5},{8,6},{9,7},{10,8},{11,9},{12,... | collective-permute-start | bytes 147464 | tf_op jit(solution)/shard_map/ppermute | solution.py:441
  68.9 1.4 %collective-permute-done.15.refs_3_ = f32[96,128]{1,0:T(8,128)S(1)} collective-permute-done((f32[96,128]{1,0:T(8,128)S(1)}, f32[96,128]{1,0:T(8,128)S(1)}, u32[]{:S(2)}, u32[]{:S(2)}) %collective-permute-start.15) | collective-permute-done | bytes 49184 | tf_op jit(solution)/shard_map/ppermute | solution.py:441
  70.2 2.4 %shard_map.51 = f32[4,19,4096]{2,1,0:T(8,128)S(1)} custom-call(s32[24]{0:T(128)S(1)} %get-tuple-element.30.receives, f32[4,608,128]{2,1,0:T(8,128)S(1)} %get-tuple-element.49.post, f32[24,16,128]{2,1,0:T(8,128)S(1)} %get-tuple-element.50.own, f32[96,128]{1,0:T(8,128)S(1)} %collective-permute-done.12.refs_0_, f32[96,128]{1,0:T(8,128)S(1)} %collective-permute-done.13.refs_1_, ...), custom_call_target="tpu_custom_call" | custom-call | bytes 2490368 | tf_op jit(solution)/shard_map/pallas_call | solution.py:470
  72.6 1.8 %copy.6 = f32[4,19,4096]{2,0,1:T(4,128)} copy(f32[4,19,4096]{2,1,0:T(8,128)S(1)} %shard_map.51) | data formatting | bytes 2490368 | tf_op jit(solution)/shard_map/pallas_call | solution.py:470
  (23 shorter events, 1.7 us)
Async XLA Ops:
  0.0 2.0 %copy-start = (s32[4]{0:T(128)S(1)}, s32[4]{0:T(128)}, u32[]{:S(2)}) copy-start(s32[4]{0:T(128)} %plan.3) | copy-start | bytes 52
  2.0 12.6 %copy-start.1 = (s32[4,6]{1,0:T(4,128)S(1)}, s32[4,6]{1,0:T(4,128)}, u32[]{:S(2)}) copy-start(s32[4,6]{1,0:T(4,128)} %neighbours.1) | copy-start | bytes 292
  2.1 14.6 %copy-start.2 = (s32[4,4096]{1,0:T(4,128)S(1)}, s32[4,4096]{1,0:T(4,128)}, u32[]{:S(2)}) copy-start(s32[4,4096]{1,0:T(4,128)} %param.7) | copy-start | bytes 196612
  3.6 15.3 %collective-permute-start = (f32[608,128]{1,0:T(8,128)S(1)}, f32[608,128]{1,0:T(8,128)S(1)}, u32[]{:S(2)}, u32[]{:S(2)}) collective-permute-start(f32[608,128]{1,0:T(8,128)S(1)} %get-tuple-element.32), channel_id=1, source_target_pairs={{2,0},{3,1},{4,2},{5,3},{6,4},{7,5},{8,6},{9,7},{10,8},{11,9},{12,... | collective-permute-start | bytes 933896 | tf_op jit(solution)/shard_map/ppermute | solution.py:441
  12.9 6.3 %collective-permute-start.1 = (f32[608,128]{1,0:T(8,128)S(1)}, f32[608,128]{1,0:T(8,128)S(1)}, u32[]{:S(2)}, u32[]{:S(2)}) collective-permute-start(f32[608,128]{1,0:T(8,128)S(1)} %get-tuple-element.33), channel_id=1, source_target_pairs={{1,0},{2,1},{3,2},{4,3},{5,4},{6,5},{7,6},{8,7},{9,8},{10,9},{11,1... | collective-permute-start | bytes 933896 | tf_op jit(solution)/shard_map/ppermute | solution.py:441
  13.8 7.4 %collective-permute-start.2 = (f32[608,128]{1,0:T(8,128)S(1)}, f32[608,128]{1,0:T(8,128)S(1)}, u32[]{:S(2)}, u32[]{:S(2)}) collective-permute-start(f32[608,128]{1,0:T(8,128)S(1)} %get-tuple-element.34), channel_id=1, source_target_pairs={{127,0},{0,1},{1,2},{2,3},{3,4},{4,5},{5,6},{6,7},{7,8},{8,9},{9,1... | collective-permute-start | bytes 933896 | tf_op jit(solution)/shard_map/ppermute | solution.py:441
  14.6 17.0 %collective-permute-start.3 = (f32[608,128]{1,0:T(8,128)S(1)}, f32[608,128]{1,0:T(8,128)S(1)}, u32[]{:S(2)}, u32[]{:S(2)}) collective-permute-start(f32[608,128]{1,0:T(8,128)S(1)} %get-tuple-element.35), channel_id=1, source_target_pairs={{126,0},{127,1},{0,2},{1,3},{2,4},{3,5},{4,6},{5,7},{6,8},{7,9},{8... | collective-permute-start | bytes 933896 | tf_op jit(solution)/shard_map/ppermute | solution.py:441
  33.3 8.4 %collective-permute-start.4 = (f32[96,128]{1,0:T(8,128)S(1)}, f32[96,128]{1,0:T(8,128)S(1)}, u32[]{:S(2)}, u32[]{:S(2)}) collective-permute-start(f32[96,128]{1,0:T(8,128)S(1)} %get-tuple-element.39), channel_id=1, source_target_pairs={{126,0},{127,1},{0,2},{1,3},{2,4},{3,5},{4,6},{5,7},{6,8},{7,9},{8... | collective-permute-start | bytes 147464 | tf_op jit(solution)/shard_map/ppermute | solution.py:441
  33.4 8.4 %collective-permute-start.5 = (f32[96,128]{1,0:T(8,128)S(1)}, f32[96,128]{1,0:T(8,128)S(1)}, u32[]{:S(2)}, u32[]{:S(2)}) collective-permute-start(f32[96,128]{1,0:T(8,128)S(1)} %get-tuple-element.40), channel_id=1, source_target_pairs={{127,0},{0,1},{1,2},{2,3},{3,4},{4,5},{5,6},{6,7},{7,8},{8,9},{9,1... | collective-permute-start | bytes 147464 | tf_op jit(solution)/shard_map/ppermute | solution.py:441
  33.5 8.3 %collective-permute-start.6 = (f32[96,128]{1,0:T(8,128)S(1)}, f32[96,128]{1,0:T(8,128)S(1)}, u32[]{:S(2)}, u32[]{:S(2)}) collective-permute-start(f32[96,128]{1,0:T(8,128)S(1)} %get-tuple-element.41), channel_id=1, source_target_pairs={{1,0},{2,1},{3,2},{4,3},{5,4},{6,5},{7,6},{8,7},{9,8},{10,9},{11,1... | collective-permute-start | bytes 147464 | tf_op jit(solution)/shard_map/ppermute | solution.py:441
  34.0 8.3 %collective-permute-start.7 = (f32[96,128]{1,0:T(8,128)S(1)}, f32[96,128]{1,0:T(8,128)S(1)}, u32[]{:S(2)}, u32[]{:S(2)}) collective-permute-start(f32[96,128]{1,0:T(8,128)S(1)} %get-tuple-element.42), channel_id=1, source_target_pairs={{2,0},{3,1},{4,2},{5,3},{6,4},{7,5},{8,6},{9,7},{10,8},{11,9},{12,... | collective-permute-start | bytes 147464 | tf_op jit(solution)/shard_map/ppermute | solution.py:441
  44.9 9.7 %collective-permute-start.8 = (f32[96,128]{1,0:T(8,128)S(1)}, f32[96,128]{1,0:T(8,128)S(1)}, u32[]{:S(2)}, u32[]{:S(2)}) collective-permute-start(f32[96,128]{1,0:T(8,128)S(1)} %get-tuple-element.45), channel_id=1, source_target_pairs={{126,0},{127,1},{0,2},{1,3},{2,4},{3,5},{4,6},{5,7},{6,8},{7,9},{8... | collective-permute-start | bytes 147464 | tf_op jit(solution)/shard_map/ppermute | solution.py:441
  45.0 9.7 %collective-permute-start.9 = (f32[96,128]{1,0:T(8,128)S(1)}, f32[96,128]{1,0:T(8,128)S(1)}, u32[]{:S(2)}, u32[]{:S(2)}) collective-permute-start(f32[96,128]{1,0:T(8,128)S(1)} %get-tuple-element.46), channel_id=1, source_target_pairs={{127,0},{0,1},{1,2},{2,3},{3,4},{4,5},{5,6},{6,7},{7,8},{8,9},{9,1... | collective-permute-start | bytes 147464 | tf_op jit(solution)/shard_map/ppermute | solution.py:441
  46.9 7.8 %collective-permute-start.10 = (f32[96,128]{1,0:T(8,128)S(1)}, f32[96,128]{1,0:T(8,128)S(1)}, u32[]{:S(2)}, u32[]{:S(2)}) collective-permute-start(f32[96,128]{1,0:T(8,128)S(1)} %get-tuple-element.47), channel_id=1, source_target_pairs={{1,0},{2,1},{3,2},{4,3},{5,4},{6,5},{7,6},{8,7},{9,8},{10,9},{11,1... | collective-permute-start | bytes 147464 | tf_op jit(solution)/shard_map/ppermute | solution.py:441
  47.7 8.3 %collective-permute-start.11 = (f32[96,128]{1,0:T(8,128)S(1)}, f32[96,128]{1,0:T(8,128)S(1)}, u32[]{:S(2)}, u32[]{:S(2)}) collective-permute-start(f32[96,128]{1,0:T(8,128)S(1)} %get-tuple-element.48), channel_id=1, source_target_pairs={{2,0},{3,1},{4,2},{5,3},{6,4},{7,5},{8,6},{9,7},{10,8},{11,9},{12,... | collective-permute-start | bytes 147464 | tf_op jit(solution)/shard_map/ppermute | solution.py:441
  58.7 10.2 %collective-permute-start.12 = (f32[96,128]{1,0:T(8,128)S(1)}, f32[96,128]{1,0:T(8,128)S(1)}, u32[]{:S(2)}, u32[]{:S(2)}) collective-permute-start(f32[96,128]{1,0:T(8,128)S(1)} %get-tuple-element.51), channel_id=1, source_target_pairs={{126,0},{127,1},{0,2},{1,3},{2,4},{3,5},{4,6},{5,7},{6,8},{7,9},{8... | collective-permute-start | bytes 147464 | tf_op jit(solution)/shard_map/ppermute | solution.py:441
  58.7 10.1 %collective-permute-start.13 = (f32[96,128]{1,0:T(8,128)S(1)}, f32[96,128]{1,0:T(8,128)S(1)}, u32[]{:S(2)}, u32[]{:S(2)}) collective-permute-start(f32[96,128]{1,0:T(8,128)S(1)} %get-tuple-element.52), channel_id=1, source_target_pairs={{127,0},{0,1},{1,2},{2,3},{3,4},{4,5},{5,6},{6,7},{7,8},{8,9},{9,1... | collective-permute-start | bytes 147464 | tf_op jit(solution)/shard_map/ppermute | solution.py:441
  61.0 7.9 %collective-permute-start.14 = (f32[96,128]{1,0:T(8,128)S(1)}, f32[96,128]{1,0:T(8,128)S(1)}, u32[]{:S(2)}, u32[]{:S(2)}) collective-permute-start(f32[96,128]{1,0:T(8,128)S(1)} %get-tuple-element.53), channel_id=1, source_target_pairs={{1,0},{2,1},{3,2},{4,3},{5,4},{6,5},{7,6},{8,7},{9,8},{10,9},{11,1... | collective-permute-start | bytes 147464 | tf_op jit(solution)/shard_map/ppermute | solution.py:441
  61.8 8.5 %collective-permute-start.15 = (f32[96,128]{1,0:T(8,128)S(1)}, f32[96,128]{1,0:T(8,128)S(1)}, u32[]{:S(2)}, u32[]{:S(2)}) collective-permute-start(f32[96,128]{1,0:T(8,128)S(1)} %get-tuple-element.54), channel_id=1, source_target_pairs={{2,0},{3,1},{4,2},{5,3},{6,4},{7,5},{8,6},{9,7},{10,8},{11,9},{12,... | collective-permute-start | bytes 147464 | tf_op jit(solution)/shard_map/ppermute | solution.py:441

commit v2 on v1

--- a/solution.py
+++ b/solution.py
@@ -270,16 +270,12 @@
 
 def pack_kernel(cycle, plan, pdfs, *outs):
     offsets = [cycle_offset(plan[j], cycle) for j in range(BLK_DEV)]
-    for out, offset in zip(outs, OFFSETS + (0,)):
+    values = [sent_offset(kind)[0] for kind in BLOCK_ORDER] + [0]
+    for out, offset in zip(outs, values):
         slot = jnp.int32(0)
         for j in range(BLK_DEV):
             slot = jnp.where(offsets[j] == offset, j, slot)
-        for first in range(0, POPS, 8):
-            count = min(8, POPS - first)
-            for c in range(ROWS):
-                out[pl.ds(first * ROWS + c, count, stride=ROWS), :] = pdfs[
-                    slot, first : first + count, c * 128 : (c + 1) * 128
-                ]
+        out[...] = pdfs[pl.ds(slot, BLOCK_ROWS, stride=BLK_DEV), :]
 
 
 def index_kernel(cycle, neighbours, sends, receives, ranks):
@@ -316,8 +312,31 @@
             seen = seen + found.astype(jnp.int32)
 
 
+ROUTES = {
+    "p2": lambda i: i + 2,
+    "m2": lambda i: i - 2,
+    "p1": lambda i: i + 1,
+    "m1": lambda i: i - 1,
+    "x": lambda i: i + 1 if i % 2 else i - 1,
+    "a": lambda i: i ^ 1,
+}
+BLOCK_ORDER = ('p2', 'x', 'm2', 'a')
+FACE_ORDER = ('p2', 'x', 'm2', 'a')
+
+
+def sent_offset(kind):
+    core = lax.axis_index("blocks") & 1
+    to = {"p2": 2, "m2": -2, "p1": 1, "m1": -1, "x": 2 * core - 1, "a": 1 - 2 * core}[kind]
+    return to, -to if kind in ("x", "a") else to
+
+
+def offset_place(offset):
+    return offset + REACH - (offset > 0) if isinstance(offset, int) else (offset + 3) >> 1
+
+
 def send_faces(sends, faces, outs):
-    for o, out in enumerate(outs):
+    for kind, out in zip(FACE_ORDER, outs):
+        o = offset_place(sent_offset(kind)[0])
         for r in range(PEER_FACES):
             out[r * FACE_ROWS : (r + 1) * FACE_ROWS, :] = faces[sends[o * PEER_FACES + r]]
 
@@ -329,19 +348,24 @@
     pack_faces(lambda rows: post[b, rows, :], store)
 
 
+def flags_of(flags, b):
+    return lambda rows: flags[pl.ds(BLK_DEV * rows.start + b, rows.size, stride=BLK_DEV), :]
+
+
 def first_kernel(cycle, plan, sends, flags, *refs):
     arrived, (post, faces), outs = refs[:5], refs[5:7], refs[7:]
+    values = [sent_offset(kind)[1] for kind in BLOCK_ORDER] + [0]
     for j in range(BLK_DEV):
         offset = cycle_offset(plan[j], cycle)
         slot = plan[j] & 3
-        for source, value in zip(arrived, OFFSETS + (0,)):
+        for source, value in zip(arrived, values):
 
             @pl.when(offset == value)
             def _(source=source):
                 def store(rows, value):
                     post[slot, rows, :] = value
 
-                collide_block(lambda r: source[r, :], lambda r: flags[slot, r, :], store)
+                collide_block(lambda r: source[r, :], flags_of(flags, slot), store)
 
     @pl.loop(0, BLK_DEV)
     def _(b):
@@ -351,19 +375,16 @@
 
 
 def fill_pool(pool, arrived, own):
-    for o, source in enumerate(arrived):
+    for kind, source in zip(FACE_ORDER, arrived):
+        o = offset_place(-sent_offset(kind)[1])
         for r in range(PEER_FACES):
             pool[o * PEER_FACES + r] = source[r * FACE_ROWS : (r + 1) * FACE_ROWS, :]
     pool[FACES:] = own[...]
 
 
-def move_block(b, receives, post, pool, wide, new):
+def move_block(b, receives, post, pool, wide, new_load, store):
     spots = [receives[b * 6 + face] for face in range(6)]
     safe = [jnp.maximum(spot, 0) for spot in spots]
-
-    def store(rows, value):
-        new[rows, :] = value
-
     stream_block(
         lambda rows: post[b, rows, :],
         lambda face, rows: pool[safe[face], rows, :],
@@ -374,7 +395,7 @@
 
         @pl.when(spots[face] < 0)
         def _(face=face):
-            bounce_face(face, lambda rows: post[b, rows, :], lambda rows: new[rows, :], store)
+            bounce_face(face, lambda rows: post[b, rows, :], new_load, store)
 
 
 def step_kernel(sends, receives, flags, post, own, *refs):
@@ -383,30 +404,33 @@
 
     @pl.loop(0, BLK_DEV)
     def _(b):
-        move_block(b, receives, post, pool, wide, new)
+        def store_new(rows, value):
+            new[rows, :] = value
+
+        move_block(b, receives, post, pool, wide, lambda rows: new[rows, :], store_new)
 
         def store(rows, value):
             post_out[b, rows, :] = value
 
-        collide_block(lambda r: new[r, :], lambda r: flags[b, r, :], store)
+        collide_block(lambda r: new[r, :], flags_of(flags, b), store)
         pack_block(post_out, faces, b)
 
     send_faces(sends, faces, outs)
 
 
 def last_kernel(receives, post, own, *refs):
-    arrived, out, (pool, wide, new) = refs[:4], refs[4], refs[5:]
+    arrived, out, (pool, wide) = refs[:4], refs[4], refs[5:]
     fill_pool(pool, arrived, own)
 
     @pl.loop(0, BLK_DEV)
     def _(b):
-        move_block(b, receives, post, pool, wide, new)
-        for first in range(0, POPS, 8):
-            count = min(8, POPS - first)
-            for c in range(ROWS):
-                out[b, first : first + count, c * 128 : (c + 1) * 128] = new[
-                    pl.ds(first * ROWS + c, count, stride=ROWS), :
-                ]
+        def spots(rows):
+            return pl.ds(BLK_DEV * rows.start + b, rows.size, stride=BLK_DEV)
+
+        def store(rows, value):
+            out[spots(rows), :] = value
+
+        move_block(b, receives, post, pool, wide, lambda rows: out[spots(rows), :], store)
 
 
 SMEM = pl.BlockSpec(memory_space=pltpu.SMEM)
@@ -415,11 +439,9 @@
 POST = jax.ShapeDtypeStruct((BLK_DEV, BLOCK_ROWS, 128), jnp.float32)
 OWN = jax.ShapeDtypeStruct((FACES, FACE_ROWS, 128), jnp.float32)
 SENT = jax.ShapeDtypeStruct((PEER_FACES * FACE_ROWS, 128), jnp.float32)
-MOVE_SCRATCH = [
-    pltpu.VMEM((2 * FACES, FACE_ROWS, 128), jnp.float32),
-    pltpu.VMEM((POPS, ROWS + 2 * PAD, 128), jnp.float32),
-    pltpu.VMEM((BLOCK_ROWS, 128), jnp.float32),
-]
+POOL = pltpu.VMEM((2 * FACES, FACE_ROWS, 128), jnp.float32)
+WIDE = pltpu.VMEM((POPS, ROWS + 2 * PAD, 128), jnp.float32)
+NEW = pltpu.VMEM((BLOCK_ROWS, 128), jnp.float32)
 
 
 def call(kernel, in_specs, out_shapes, out_specs, scratch=(), flops=0, bytes_accessed=0):
@@ -436,42 +458,49 @@
     )
 
 
-def from_behind(value, distance, cycle):
-    route = [((i - distance) % cycle, i) for i in range(cycle)]
-    return lax.ppermute(value, "blocks", route)
+def exchange(buffers, order, cycle):
+    return [
+        lax.ppermute(value, "blocks", [(i, ROUTES[kind](i) % cycle) for i in range(cycle)])
+        for value, kind in zip(buffers, order)
+    ]
 
 
 def body(pdfs, plan, neighbours, flags):
     cycle = lax.axis_size("blocks")
     size = 4 * pdfs.size
+    rows = pdfs.transpose(1, 0, 2).reshape(POPS, BLK_DEV, ROWS, 128)
+    rows = rows.transpose(0, 2, 1, 3).reshape(BLK_DEV * BLOCK_ROWS, 128)
     sent = call(
         functools.partial(pack_kernel, cycle), [SMEM, VMEM], [BLOCK] * 5, [VMEM] * 5,
         bytes_accessed=2 * size,
-    )(plan, pdfs)
-    arrived = [from_behind(value, o, cycle) for value, o in zip(sent, OFFSETS)] + [sent[4]]
+    )(plan, rows)
+    arrived = exchange(sent, BLOCK_ORDER, cycle) + [sent[4]]
     table = jax.ShapeDtypeStruct((FACES,), jnp.int32)
     sends, receives = call(
         functools.partial(index_kernel, cycle), [SMEM], [table] * 2, [SMEM] * 2,
         [pltpu.SMEM(((len(OFFSETS) + 1) * FACES,), jnp.int32)], bytes_accessed=1000,
     )(neighbours)
-    cells = flags.reshape(BLK_DEV, ROWS, 128)
+    cells = flags.reshape(BLK_DEV, ROWS, 128).transpose(1, 0, 2).reshape(BLK_DEV * ROWS, 128)
+    outs = dict(
+        out_shapes=[POST, OWN] + [SENT] * 4, out_specs=[VMEM] * 6,
+        flops=300 * pdfs.size // POPS, bytes_accessed=2 * size,
+    )
     post, own, *faces = call(
-        functools.partial(first_kernel, cycle), [SMEM, SMEM, VMEM] + [VMEM] * 5,
-        [POST, OWN] + [SENT] * 4, [VMEM] * 6, flops=300 * pdfs.size // POPS, bytes_accessed=2 * size,
+        functools.partial(first_kernel, cycle), [SMEM, SMEM] + [VMEM] * 6, **outs
     )(plan, sends, cells, *arrived)
     for _ in range(STEPS - 1):
-        came = [from_behind(value, -o, cycle) for value, o in zip(faces[::-1], OFFSETS)]
+        came = exchange(faces, FACE_ORDER, cycle)
         post, own, *faces = call(
-            step_kernel, [SMEM, SMEM, VMEM, VMEM, VMEM] + [VMEM] * 4,
-            [POST, OWN] + [SENT] * 4, [VMEM] * 6, MOVE_SCRATCH,
-            flops=300 * pdfs.size // POPS, bytes_accessed=2 * size,
+            step_kernel, [SMEM, SMEM] + [VMEM] * 7, scratch=[POOL, WIDE, NEW], **outs
         )(sends, receives, cells, post, own, *came)
-    came = [from_behind(value, -o, cycle) for value, o in zip(faces[::-1], OFFSETS)]
-    return call(
-        last_kernel, [SMEM, VMEM, VMEM] + [VMEM] * 4,
-        jax.ShapeDtypeStruct(pdfs.shape, jnp.float32), VMEM, MOVE_SCRATCH,
+    came = exchange(faces, FACE_ORDER, cycle)
+    out = call(
+        last_kernel, [SMEM] + [VMEM] * 6,
+        jax.ShapeDtypeStruct((BLK_DEV * BLOCK_ROWS, 128), jnp.float32), VMEM, [POOL, WIDE],
         bytes_accessed=2 * size,
     )(receives, post, own, *came)
+    out = out.reshape(POPS, ROWS, BLK_DEV, 128).transpose(2, 0, 1, 3)
+    return out.reshape(pdfs.shape)
 
 
 def solution(mesh):

time: 75.9 us -> 62.3 us (0.82); the launches traced: 74.5 us -> 62.2 us
  waiting for transfers between devices: 19.1 us -> 6.07 us
  starting transfers between devices: 38.4 us -> 41.5 us
  local copies, waits for them, and re-layouts: 3.89 us -> 1.97 us
    ppermute x16, waiting for transfers between devices: 19.1 us -> 6.07 us  [exchange(): lax.ppermute(value, 'blocks', [(i, ROUTES[kind](i) % cycle) for i in rang...]
    ppermute x16, starting transfers between devices: 38.4 us -> 41.5 us  [exchange(): lax.ppermute(value, 'blocks', [(i, ROUTES[kind](i) % cycle) for i in rang...]
    pallas_call x1 -> x0, local copies, waits for them, and re-layouts: 1.84 us -> none  [body(): call(last_kernel, [SMEM, VMEM, VMEM] + [VMEM] * 4, jax.ShapeDtypeStruct(p...]
    unnamed x8 -> x10, local copies, waits for them, and re-layouts: 2.05 us -> 1.97 us
where the time goes in v2:
time: 62.3 us; the launch traced here: 62.2 us
  starting transfers between devices  41.5 us (67%)
  Pallas kernels  12.6 us (20%)
  waiting for transfers between devices  6.07 us (10%)
  local copies, waits for them, and re-layouts  1.97 us (3%)
    ppermute x16, starting transfers between devices, exchange(): lax.ppermute(value, 'blocks', [(i, ROUTES[kind](i) % cycle) for i in rang...  41.5 us
    ppermute x16, waiting for transfers between devices, exchange(): lax.ppermute(value, 'blocks', [(i, ROUTES[kind](i) % cycle) for i in rang...  6.07 us
    pallas_call x2, Pallas kernels, body(): call(step_kernel, [SMEM, SMEM] + [VMEM] * 7, scratch=[POOL, WIDE, NEW], *...  5.36 us
    pallas_call x1, Pallas kernels, body(): call(last_kernel, [SMEM] + [VMEM] * 6, jax.ShapeDtypeStruct((BLK_DEV * BL...  2.69 us
    pallas_call x1, Pallas kernels, body(): call(functools.partial(index_kernel, cycle), [SMEM], [table] * 2, [SMEM]...  2.02 us
    unnamed x10, local copies, waits for them, and re-layouts  1.97 us
    pallas_call x1, Pallas kernels, body(): call(functools.partial(first_kernel, cycle), [SMEM, SMEM] + [VMEM] * 6, *...  1.72 us
  transfers between devices with their start and end apart: 16, of which 8 were waited for; matrix products, arithmetic and copies ran while one was open for 0% of the time, Pallas kernels for 3%

profile of v2, /device:TPU:1, one launch (start us, length us, event | category | flops | bytes accessed | tf_op | source)
XLA Modules:
  0.0 62.2 jit_solution(12841302913077784239)
XLA Ops:
  0.0 1.3 %copy-done = f32[4,19,4096]{2,0,1:T(4,128)S(1)} copy-done((f32[4,19,4096]{2,0,1:T(4,128)S(1)}, f32[4,19,4096]{2,0,1:T(4,128)}, u32[]{:S(2)}) %copy-start) | copy-done | bytes 1245208
  1.3 0.7 %copy-done.2 = s32[4]{0:T(128)S(1)} copy-done((s32[4]{0:T(128)S(1)}, s32[4]{0:T(128)}, u32[]{:S(2)}) %copy-start.2) | copy-done | bytes 40
  2.0 0.8 %shard_map.47 = (f32[608,128]{1,0:T(8,128)S(1)}, f32[608,128]{1,0:T(8,128)S(1)}, f32[608,128]{1,0:T(8,128)S(1)}, f32[608,128]{1,0:T(8,128)S(1)}, f32[608,128]{1,0:T(8,128)S(1)}) custom-call(s32[4]{0:T(128)S(1)} %copy-done.2, f32[2432,128]{1,0:T(8,128)S(1)} %bitcast.17), custom_call_target="tpu_custom_call" | custom-call | bytes 2490368 | tf_op jit(solution)/shard_map/pallas_call | solution.py:473
  2.7 2.1 %collective-permute-start = (f32[608,128]{1,0:T(8,128)S(1)}, f32[608,128]{1,0:T(8,128)S(1)}, u32[]{:S(2)}, u32[]{:S(2)}) collective-permute-start(f32[608,128]{1,0:T(8,128)S(1)} %get-tuple-element.32), channel_id=1, source_target_pairs={{0,2},{1,3},{2,4},{3,5},{4,6},{5,7},{6,8},{7,9},{8,10},{9,11},{10,... | collective-permute-start | bytes 933896 | tf_op jit(solution)/shard_map/ppermute | solution.py:463
  4.8 2.1 %collective-permute-start.1 = (f32[608,128]{1,0:T(8,128)S(1)}, f32[608,128]{1,0:T(8,128)S(1)}, u32[]{:S(2)}, u32[]{:S(2)}) collective-permute-start(f32[608,128]{1,0:T(8,128)S(1)} %get-tuple-element.33), channel_id=1, source_target_pairs={{0,127},{1,2},{2,1},{3,4},{4,3},{5,6},{6,5},{7,8},{8,7},{9,10},{10... | collective-permute-start | bytes 933896 | tf_op jit(solution)/shard_map/ppermute | solution.py:463
  6.9 5.7 %collective-permute-start.2 = (f32[608,128]{1,0:T(8,128)S(1)}, f32[608,128]{1,0:T(8,128)S(1)}, u32[]{:S(2)}, u32[]{:S(2)}) collective-permute-start(f32[608,128]{1,0:T(8,128)S(1)} %get-tuple-element.34), channel_id=1, source_target_pairs={{0,126},{1,127},{2,0},{3,1},{4,2},{5,3},{6,4},{7,5},{8,6},{9,7},{1... | collective-permute-start | bytes 933896 | tf_op jit(solution)/shard_map/ppermute | solution.py:463
  12.6 1.6 %collective-permute-start.3 = (f32[608,128]{1,0:T(8,128)S(1)}, f32[608,128]{1,0:T(8,128)S(1)}, u32[]{:S(2)}, u32[]{:S(2)}) collective-permute-start(f32[608,128]{1,0:T(8,128)S(1)} %get-tuple-element.35), channel_id=1, source_target_pairs={{0,1},{1,0},{2,3},{3,2},{4,5},{5,4},{6,7},{7,6},{8,9},{9,8},{10,11... | collective-permute-start | bytes 933896 | tf_op jit(solution)/shard_map/ppermute | solution.py:463
  14.2 2.0 %shard_map.46 = (s32[24]{0:T(128)S(1)}, s32[24]{0:T(128)S(1)}) custom-call(s32[4,6]{1,0:T(4,128)S(1)} %copy-done.4), custom_call_target="tpu_custom_call" | custom-call | bytes 1000 | tf_op jit(solution)/shard_map/pallas_call | solution.py:479
  16.2 2.9 %collective-permute-done.refs_0_ = f32[608,128]{1,0:T(8,128)S(1)} collective-permute-done((f32[608,128]{1,0:T(8,128)S(1)}, f32[608,128]{1,0:T(8,128)S(1)}, u32[]{:S(2)}, u32[]{:S(2)}) %collective-permute-start) | collective-permute-done | bytes 311328 | tf_op jit(solution)/shard_map/ppermute | solution.py:463
  19.6 1.7 %shard_map.48 = (f32[4,608,128]{2,1,0:T(8,128)S(1)}, f32[24,16,128]{2,1,0:T(8,128)S(1)}, f32[96,128]{1,0:T(8,128)S(1)}, f32[96,128]{1,0:T(8,128)S(1)}, f32[96,128]{1,0:T(8,128)S(1)}, /*index=5*/f32[96,128]{1,0:T(8,128)S(1)}) custom-call(s32[4]{0:T(128)S(1)} %copy-done.3, s32[24]{0:T(128)S(1)} %get-tuple-element.31.sends, s32[128,128]{1,0:T(8,128)S(1)} %bitcast.18, ...), custom_call_target="tpu_custom_call" | custom-call | flops 4915200 | bytes 2490368 | tf_op jit(solution)/shard_map/pallas_call | solution.py:488
  21.5 1.8 %collective-permute-start.5 = (f32[96,128]{1,0:T(8,128)S(1)}, f32[96,128]{1,0:T(8,128)S(1)}, u32[]{:S(2)}, u32[]{:S(2)}) collective-permute-start(f32[96,128]{1,0:T(8,128)S(1)} %get-tuple-element.40), channel_id=1, source_target_pairs={{0,127},{1,2},{2,1},{3,4},{4,3},{5,6},{6,5},{7,8},{8,7},{9,10},{10... | collective-permute-start | bytes 147464 | tf_op jit(solution)/shard_map/ppermute | solution.py:463
  23.3 9.1 %collective-permute-start.6 = (f32[96,128]{1,0:T(8,128)S(1)}, f32[96,128]{1,0:T(8,128)S(1)}, u32[]{:S(2)}, u32[]{:S(2)}) collective-permute-start(f32[96,128]{1,0:T(8,128)S(1)} %get-tuple-element.41), channel_id=1, source_target_pairs={{0,126},{1,127},{2,0},{3,1},{4,2},{5,3},{6,4},{7,5},{8,6},{9,7},{1... | collective-permute-start | bytes 147464 | tf_op jit(solution)/shard_map/ppermute | solution.py:463
  32.4 1.0 %collective-permute-start.7 = (f32[96,128]{1,0:T(8,128)S(1)}, f32[96,128]{1,0:T(8,128)S(1)}, u32[]{:S(2)}, u32[]{:S(2)}) collective-permute-start(f32[96,128]{1,0:T(8,128)S(1)} %get-tuple-element.42), channel_id=1, source_target_pairs={{0,1},{1,0},{2,3},{3,2},{4,5},{5,4},{6,7},{7,6},{8,9},{9,8},{10,11... | collective-permute-start | bytes 147464 | tf_op jit(solution)/shard_map/ppermute | solution.py:463
  33.6 0.7 %collective-permute-done.7.refs_3_ = f32[96,128]{1,0:T(8,128)S(1)} collective-permute-done((f32[96,128]{1,0:T(8,128)S(1)}, f32[96,128]{1,0:T(8,128)S(1)}, u32[]{:S(2)}, u32[]{:S(2)}) %collective-permute-start.7) | collective-permute-done | bytes 49184 | tf_op jit(solution)/shard_map/ppermute | solution.py:463
  34.3 2.7 %shard_map.49 = (f32[4,608,128]{2,1,0:T(8,128)S(1)}, f32[24,16,128]{2,1,0:T(8,128)S(1)}, f32[96,128]{1,0:T(8,128)S(1)}, f32[96,128]{1,0:T(8,128)S(1)}, f32[96,128]{1,0:T(8,128)S(1)}, /*index=5*/f32[96,128]{1,0:T(8,128)S(1)}) custom-call(s32[24]{0:T(128)S(1)} %get-tuple-element.31.sends, s32[24]{0:T(128)S(1)} %get-tuple-element.30.receives, ...), custom_call_target="tpu_custom_call" | custom-call | flops 4915200 | bytes 2490368 | tf_op jit(solution)/shard_map/pallas_call | solution.py:493
  37.1 7.8 %collective-permute-start.10 = (f32[96,128]{1,0:T(8,128)S(1)}, f32[96,128]{1,0:T(8,128)S(1)}, u32[]{:S(2)}, u32[]{:S(2)}) collective-permute-start(f32[96,128]{1,0:T(8,128)S(1)} %get-tuple-element.47), channel_id=1, source_target_pairs={{0,126},{1,127},{2,0},{3,1},{4,2},{5,3},{6,4},{7,5},{8,6},{9,7},{1... | collective-permute-start | bytes 147464 | tf_op jit(solution)/shard_map/ppermute | solution.py:463
  44.9 0.9 %collective-permute-start.11 = (f32[96,128]{1,0:T(8,128)S(1)}, f32[96,128]{1,0:T(8,128)S(1)}, u32[]{:S(2)}, u32[]{:S(2)}) collective-permute-start(f32[96,128]{1,0:T(8,128)S(1)} %get-tuple-element.48), channel_id=1, source_target_pairs={{0,1},{1,0},{2,3},{3,2},{4,5},{5,4},{6,7},{7,6},{8,9},{9,8},{10,11... | collective-permute-start | bytes 147464 | tf_op jit(solution)/shard_map/ppermute | solution.py:463
  46.1 0.6 collective-permute-done.11.refs_3_
  46.7 2.7 %shard_map.50 = (f32[4,608,128]{2,1,0:T(8,128)S(1)}, f32[24,16,128]{2,1,0:T(8,128)S(1)}, f32[96,128]{1,0:T(8,128)S(1)}, f32[96,128]{1,0:T(8,128)S(1)}, f32[96,128]{1,0:T(8,128)S(1)}, /*index=5*/f32[96,128]{1,0:T(8,128)S(1)}) custom-call(s32[24]{0:T(128)S(1)} %get-tuple-element.31.sends, s32[24]{0:T(128)S(1)} %get-tuple-element.30.receives, ...), custom_call_target="tpu_custom_call" | custom-call | flops 4915200 | bytes 2490368 | tf_op jit(solution)/shard_map/pallas_call | solution.py:493
  49.7 0.9 %collective-permute-start.13 = (f32[96,128]{1,0:T(8,128)S(1)}, f32[96,128]{1,0:T(8,128)S(1)}, u32[]{:S(2)}, u32[]{:S(2)}) collective-permute-start(f32[96,128]{1,0:T(8,128)S(1)} %get-tuple-element.52), channel_id=1, source_target_pairs={{0,127},{1,2},{2,1},{3,4},{4,3},{5,6},{6,5},{7,8},{8,7},{9,10},{10... | collective-permute-start | bytes 147464 | tf_op jit(solution)/shard_map/ppermute | solution.py:463
  50.6 7.5 %collective-permute-start.14 = (f32[96,128]{1,0:T(8,128)S(1)}, f32[96,128]{1,0:T(8,128)S(1)}, u32[]{:S(2)}, u32[]{:S(2)}) collective-permute-start(f32[96,128]{1,0:T(8,128)S(1)} %get-tuple-element.53), channel_id=1, source_target_pairs={{0,126},{1,127},{2,0},{3,1},{4,2},{5,3},{6,4},{7,5},{8,6},{9,7},{1... | collective-permute-start | bytes 147464 | tf_op jit(solution)/shard_map/ppermute | solution.py:463
  58.0 0.6 collective-permute-start.15
  58.6 0.6 collective-permute-done.14.refs_2_
  59.5 2.7 %shard_map.51 = f32[2432,128]{1,0:T(8,128)} custom-call(s32[24]{0:T(128)S(1)} %get-tuple-element.30.receives, f32[4,608,128]{2,1,0:T(8,128)S(1)} %get-tuple-element.49.post, f32[24,16,128]{2,1,0:T(8,128)S(1)} %get-tuple-element.50.own, f32[96,128]{1,0:T(8,128)S(1)} %collective-permute-done.12.refs_0_, f32[96,128]{1,0:T(8,128)S(1)} %collective-permute-done.13.refs_1_, ...), custom_call_target="tpu_custom_call" | custom-call | bytes 2490368 | tf_op jit(solution)/shard_map/pallas_call | solution.py:497
  (24 shorter events, 1.8 us)
Async XLA Ops:
  0.0 19.6 %copy-start.3 = (s32[4]{0:T(128)S(1)}, s32[4]{0:T(128)}, u32[]{:S(2)}) copy-start(s32[4]{0:T(128)} %plan.3) | copy-start | bytes 52
  0.0 1.3 %copy-start = (f32[4,19,4096]{2,0,1:T(4,128)S(1)}, f32[4,19,4096]{2,0,1:T(4,128)}, u32[]{:S(2)}) copy-start(f32[4,19,4096]{2,0,1:T(4,128)} %param.4) | copy-start | bytes 3735556
  1.3 0.7 %copy-start.2 = (s32[4]{0:T(128)S(1)}, s32[4]{0:T(128)}, u32[]{:S(2)}) copy-start(s32[4]{0:T(128)} %plan.3) | copy-start | bytes 52
  2.0 12.2 %copy-start.4 = (s32[4,6]{1,0:T(4,128)S(1)}, s32[4,6]{1,0:T(4,128)}, u32[]{:S(2)}) copy-start(s32[4,6]{1,0:T(4,128)} %neighbours.1) | copy-start | bytes 292
  2.0 17.7 %copy-start.1 = (s32[4,4096]{1,0:T(4,128)S(1)}, s32[4,4096]{1,0:T(4,128)}, u32[]{:S(2)}) copy-start(s32[4,4096]{1,0:T(4,128)} %param.7) | copy-start | bytes 196612
  2.7 16.4 %collective-permute-start = (f32[608,128]{1,0:T(8,128)S(1)}, f32[608,128]{1,0:T(8,128)S(1)}, u32[]{:S(2)}, u32[]{:S(2)}) collective-permute-start(f32[608,128]{1,0:T(8,128)S(1)} %get-tuple-element.32), channel_id=1, source_target_pairs={{0,2},{1,3},{2,4},{3,5},{4,6},{5,7},{6,8},{7,9},{8,10},{9,11},{10,... | collective-permute-start | bytes 933896 | tf_op jit(solution)/shard_map/ppermute | solution.py:463
  4.8 14.3 %collective-permute-start.1 = (f32[608,128]{1,0:T(8,128)S(1)}, f32[608,128]{1,0:T(8,128)S(1)}, u32[]{:S(2)}, u32[]{:S(2)}) collective-permute-start(f32[608,128]{1,0:T(8,128)S(1)} %get-tuple-element.33), channel_id=1, source_target_pairs={{0,127},{1,2},{2,1},{3,4},{4,3},{5,6},{6,5},{7,8},{8,7},{9,10},{10... | collective-permute-start | bytes 933896 | tf_op jit(solution)/shard_map/ppermute | solution.py:463
  6.9 12.7 %collective-permute-start.2 = (f32[608,128]{1,0:T(8,128)S(1)}, f32[608,128]{1,0:T(8,128)S(1)}, u32[]{:S(2)}, u32[]{:S(2)}) collective-permute-start(f32[608,128]{1,0:T(8,128)S(1)} %get-tuple-element.34), channel_id=1, source_target_pairs={{0,126},{1,127},{2,0},{3,1},{4,2},{5,3},{6,4},{7,5},{8,6},{9,7},{1... | collective-permute-start | bytes 933896 | tf_op jit(solution)/shard_map/ppermute | solution.py:463
  12.6 7.1 %collective-permute-start.3 = (f32[608,128]{1,0:T(8,128)S(1)}, f32[608,128]{1,0:T(8,128)S(1)}, u32[]{:S(2)}, u32[]{:S(2)}) collective-permute-start(f32[608,128]{1,0:T(8,128)S(1)} %get-tuple-element.35), channel_id=1, source_target_pairs={{0,1},{1,0},{2,3},{3,2},{4,5},{5,4},{6,7},{7,6},{8,9},{9,8},{10,11... | collective-permute-start | bytes 933896 | tf_op jit(solution)/shard_map/ppermute | solution.py:463
  21.4 12.0 %collective-permute-start.4 = (f32[96,128]{1,0:T(8,128)S(1)}, f32[96,128]{1,0:T(8,128)S(1)}, u32[]{:S(2)}, u32[]{:S(2)}) collective-permute-start(f32[96,128]{1,0:T(8,128)S(1)} %get-tuple-element.39), channel_id=1, source_target_pairs={{0,2},{1,3},{2,4},{3,5},{4,6},{5,7},{6,8},{7,9},{8,10},{9,11},{10,... | collective-permute-start | bytes 147464 | tf_op jit(solution)/shard_map/ppermute | solution.py:463
  21.5 11.9 %collective-permute-start.5 = (f32[96,128]{1,0:T(8,128)S(1)}, f32[96,128]{1,0:T(8,128)S(1)}, u32[]{:S(2)}, u32[]{:S(2)}) collective-permute-start(f32[96,128]{1,0:T(8,128)S(1)} %get-tuple-element.40), channel_id=1, source_target_pairs={{0,127},{1,2},{2,1},{3,4},{4,3},{5,6},{6,5},{7,8},{8,7},{9,10},{10... | collective-permute-start | bytes 147464 | tf_op jit(solution)/shard_map/ppermute | solution.py:463
  23.3 10.3 %collective-permute-start.6 = (f32[96,128]{1,0:T(8,128)S(1)}, f32[96,128]{1,0:T(8,128)S(1)}, u32[]{:S(2)}, u32[]{:S(2)}) collective-permute-start(f32[96,128]{1,0:T(8,128)S(1)} %get-tuple-element.41), channel_id=1, source_target_pairs={{0,126},{1,127},{2,0},{3,1},{4,2},{5,3},{6,4},{7,5},{8,6},{9,7},{1... | collective-permute-start | bytes 147464 | tf_op jit(solution)/shard_map/ppermute | solution.py:463
  32.4 1.9 %collective-permute-start.7 = (f32[96,128]{1,0:T(8,128)S(1)}, f32[96,128]{1,0:T(8,128)S(1)}, u32[]{:S(2)}, u32[]{:S(2)}) collective-permute-start(f32[96,128]{1,0:T(8,128)S(1)} %get-tuple-element.42), channel_id=1, source_target_pairs={{0,1},{1,0},{2,3},{3,2},{4,5},{5,4},{6,7},{7,6},{8,9},{9,8},{10,11... | collective-permute-start | bytes 147464 | tf_op jit(solution)/shard_map/ppermute | solution.py:463
  37.0 8.9 %collective-permute-start.8 = (f32[96,128]{1,0:T(8,128)S(1)}, f32[96,128]{1,0:T(8,128)S(1)}, u32[]{:S(2)}, u32[]{:S(2)}) collective-permute-start(f32[96,128]{1,0:T(8,128)S(1)} %get-tuple-element.45), channel_id=1, source_target_pairs={{0,2},{1,3},{2,4},{3,5},{4,6},{5,7},{6,8},{7,9},{8,10},{9,11},{10,... | collective-permute-start | bytes 147464 | tf_op jit(solution)/shard_map/ppermute | solution.py:463
  37.0 8.8 %collective-permute-start.9 = (f32[96,128]{1,0:T(8,128)S(1)}, f32[96,128]{1,0:T(8,128)S(1)}, u32[]{:S(2)}, u32[]{:S(2)}) collective-permute-start(f32[96,128]{1,0:T(8,128)S(1)} %get-tuple-element.46), channel_id=1, source_target_pairs={{0,127},{1,2},{2,1},{3,4},{4,3},{5,6},{6,5},{7,8},{8,7},{9,10},{10... | collective-permute-start | bytes 147464 | tf_op jit(solution)/shard_map/ppermute | solution.py:463
  37.1 9.0 %collective-permute-start.10 = (f32[96,128]{1,0:T(8,128)S(1)}, f32[96,128]{1,0:T(8,128)S(1)}, u32[]{:S(2)}, u32[]{:S(2)}) collective-permute-start(f32[96,128]{1,0:T(8,128)S(1)} %get-tuple-element.47), channel_id=1, source_target_pairs={{0,126},{1,127},{2,0},{3,1},{4,2},{5,3},{6,4},{7,5},{8,6},{9,7},{1... | collective-permute-start | bytes 147464 | tf_op jit(solution)/shard_map/ppermute | solution.py:463
  44.9 1.8 %collective-permute-start.11 = (f32[96,128]{1,0:T(8,128)S(1)}, f32[96,128]{1,0:T(8,128)S(1)}, u32[]{:S(2)}, u32[]{:S(2)}) collective-permute-start(f32[96,128]{1,0:T(8,128)S(1)} %get-tuple-element.48), channel_id=1, source_target_pairs={{0,1},{1,0},{2,3},{3,2},{4,5},{5,4},{6,7},{7,6},{8,9},{9,8},{10,11... | collective-permute-start | bytes 147464 | tf_op jit(solution)/shard_map/ppermute | solution.py:463
  49.4 9.2 %collective-permute-start.12 = (f32[96,128]{1,0:T(8,128)S(1)}, f32[96,128]{1,0:T(8,128)S(1)}, u32[]{:S(2)}, u32[]{:S(2)}) collective-permute-start(f32[96,128]{1,0:T(8,128)S(1)} %get-tuple-element.51), channel_id=1, source_target_pairs={{0,2},{1,3},{2,4},{3,5},{4,6},{5,7},{6,8},{7,9},{8,10},{9,11},{10,... | collective-permute-start | bytes 147464 | tf_op jit(solution)/shard_map/ppermute | solution.py:463
  49.7 8.9 %collective-permute-start.13 = (f32[96,128]{1,0:T(8,128)S(1)}, f32[96,128]{1,0:T(8,128)S(1)}, u32[]{:S(2)}, u32[]{:S(2)}) collective-permute-start(f32[96,128]{1,0:T(8,128)S(1)} %get-tuple-element.52), channel_id=1, source_target_pairs={{0,127},{1,2},{2,1},{3,4},{4,3},{5,6},{6,5},{7,8},{8,7},{9,10},{10... | collective-permute-start | bytes 147464 | tf_op jit(solution)/shard_map/ppermute | solution.py:463
  50.6 8.7 %collective-permute-start.14 = (f32[96,128]{1,0:T(8,128)S(1)}, f32[96,128]{1,0:T(8,128)S(1)}, u32[]{:S(2)}, u32[]{:S(2)}) collective-permute-start(f32[96,128]{1,0:T(8,128)S(1)} %get-tuple-element.53), channel_id=1, source_target_pairs={{0,126},{1,127},{2,0},{3,1},{4,2},{5,3},{6,4},{7,5},{8,6},{9,7},{1... | collective-permute-start | bytes 147464 | tf_op jit(solution)/shard_map/ppermute | solution.py:463
  58.0 1.5 %collective-permute-start.15 = (f32[96,128]{1,0:T(8,128)S(1)}, f32[96,128]{1,0:T(8,128)S(1)}, u32[]{:S(2)}, u32[]{:S(2)}) collective-permute-start(f32[96,128]{1,0:T(8,128)S(1)} %get-tuple-element.54), channel_id=1, source_target_pairs={{0,1},{1,0},{2,3},{3,2},{4,5},{5,4},{6,7},{7,6},{8,9},{9,8},{10,11... | collective-permute-start | bytes 147464 | tf_op jit(solution)/shard_map/ppermute | solution.py:463

commit v3 on v2

--- a/solution.py
+++ b/solution.py
@@ -211,35 +211,17 @@
 PAD = 8
 
 
-def stream_block(load, ghost, wide, store):
+def double_mask(parts, row, lane):
+    return edge_mask(*parts[0], row, lane) & edge_mask(*parts[1], row, lane)
+
+
+def stream_inside(load, wide, store):
     row = lax.broadcasted_iota(jnp.int32, (ROWS, 128), 0)
     lane = lanes_of((ROWS, 128))
-    lane16 = lanes_of((16, 128))
     for i, (cx, cy, cz) in enumerate(VELOCITIES):
-        shift = 16 * cy + cz
-        faces = [0 if cx > 0 else 1, 2 if cy > 0 else 3, 4 if cz > 0 else 5]
-        place = [FACE_POPS[face ^ 1].index(i) if part else None for face, part in zip(faces, (cx, cy, cz))]
-        post = load(pl.ds(i * ROWS, ROWS))
-        moved = roll_lanes(post, shift)
-        if cz:
-            plane = ghost(faces[2], slice(0, 16))
-            spot = (0 if cz > 0 else 15) + 16 * cy
-            incoming = jnp.concatenate(
-                [roll_lanes(plane, spot - place[2]), roll_lanes(plane, spot - 5 - place[2])], axis=0
-            )
-            moved = jnp.where(lane % 16 == spot % 16, incoming, moved)
+        moved = roll_lanes(load(pl.ds(i * ROWS, ROWS)), 16 * cy + cz)
         if cx or cy:
             wide[i, PAD : PAD + ROWS, :] = moved
-            if cx:
-                two = ghost(faces[0], slice(2 * place[0], 2 * place[0] + 2))
-                start = PAD - 2 if cx > 0 else PAD + ROWS
-                wide[i, start : start + 2, :] = roll_lanes(two, shift)
-            if cy:
-                plane = ghost(faces[1], slice(0, 16))
-                plane = roll_lanes(plane, (0 if cy > 0 else 112) - 16 * place[1] + cz)
-                spots = pl.ds(PAD - 1 if cy > 0 else PAD + 2, EDGE, stride=2)
-                keep = lane16 >= 16 if cy > 0 else lane16 < 112
-                wide[i, spots, :] = jnp.where(keep, wide[i, spots, :], plane)
             moved = wide[i, PAD - 2 * cx : PAD - 2 * cx + ROWS, :]
             if cy:
                 start = PAD - 2 * cx - cy
@@ -247,9 +229,62 @@
                 moved = jnp.where(lane >= 16 if cy > 0 else lane < 112, moved, across)
         parts = [(axis, part) for axis, part in enumerate((cx, cy, cz)) if part]
         if len(parts) == 2:
-            beyond = edge_mask(*parts[0], row, lane) & edge_mask(*parts[1], row, lane)
+            beyond = double_mask(parts, row, lane)
             moved = jnp.where(beyond, load(pl.ds(OPPOSITE[i] * ROWS, ROWS)), moved)
         store(pl.ds(i * ROWS, ROWS), moved)
+
+
+def fill_ghosts(pops, base, ghost, target):
+    row = lax.broadcasted_iota(jnp.int32, (ROWS, 128), 0)
+    lane = lanes_of((ROWS, 128))
+    row2 = lax.broadcasted_iota(jnp.int32, (2, 128), 0)
+    lane2 = lanes_of((2, 128))
+    row16 = lax.broadcasted_iota(jnp.int32, (16, 128), 0)
+    lane16 = lanes_of((16, 128))
+    for i in pops:
+        cx, cy, cz = VELOCITIES[i]
+        faces = [0 if cx > 0 else 1, 2 if cy > 0 else 3, 4 if cz > 0 else 5]
+        place = [FACE_POPS[face ^ 1].index(i) if part else None for face, part in zip(faces, (cx, cy, cz))]
+        value = base(pl.ds(i * ROWS, ROWS))
+        if cz:
+            plane = ghost(faces[2], slice(0, 16))
+            spot = (0 if cz > 0 else 15) + 16 * cy
+            incoming = jnp.concatenate(
+                [roll_lanes(plane, spot - place[2]), roll_lanes(plane, spot - 5 - place[2])], axis=0
+            )
+            if cx:
+                incoming = pltpu.roll(incoming, 2 * cx % ROWS, 0)
+            if cy:
+                across = pltpu.roll(incoming, cy % ROWS, 0)
+                incoming = jnp.where(lane >= 16 if cy > 0 else lane < 112, incoming, across)
+            mask = edge_mask(2, cz, row, lane)
+            for axis, part in ((0, cx), (1, cy)):
+                if part:
+                    mask = mask & jnp.logical_not(edge_mask(axis, part, row, lane))
+            value = jnp.where(mask, incoming, value)
+        target[pl.ds(i * ROWS, ROWS), :] = value
+        if cx:
+            two = roll_lanes(ghost(faces[0], slice(2 * place[0], 2 * place[0] + 2)), 16 * cy + cz)
+            spots = pl.ds(i * ROWS + (0 if cx > 0 else ROWS - 2), 2)
+            if cy:
+                swapped = jnp.concatenate([two[1:2], two[0:1]], axis=0)
+                two = jnp.where(lane2 >= 16 if cy > 0 else lane2 < 112, two, swapped)
+                two = jnp.where(edge_mask(1, cy, row2, lane2), target[spots, :], two)
+            if cz:
+                two = jnp.where(edge_mask(2, cz, row2, lane2), target[spots, :], two)
+            target[spots, :] = two
+        if cy:
+            plane = roll_lanes(
+                ghost(faces[1], slice(0, 16)), (0 if cy > 0 else 112) - 16 * place[1] + cz
+            )
+            mask = lane16 < 16 if cy > 0 else lane16 >= 112
+            if cx:
+                plane = pltpu.roll(plane, cx % EDGE, 0)
+                mask = mask & (row16 != (0 if cx > 0 else EDGE - 1))
+            if cz:
+                mask = mask & jnp.logical_not(edge_mask(2, cz, row16, lane16))
+            spots = pl.ds(i * ROWS + (0 if cy > 0 else 1), EDGE, stride=2)
+            target[spots, :] = jnp.where(mask, plane, target[spots, :])
 
 
 def bounce_face(face, load, new_load, store):
@@ -268,14 +303,13 @@
     return jnp.where(offset < -REACH, offset + cycle, offset)
 
 
-def pack_kernel(cycle, plan, pdfs, *outs):
-    offsets = [cycle_offset(plan[j], cycle) for j in range(BLK_DEV)]
+def pack_kernel(moves, pdfs, *outs):
     values = [sent_offset(kind)[0] for kind in BLOCK_ORDER] + [0]
-    for out, offset in zip(outs, values):
-        slot = jnp.int32(0)
+    for out, value in zip(outs, values):
+        source = jnp.int32(0)
         for j in range(BLK_DEV):
-            slot = jnp.where(offsets[j] == offset, j, slot)
-        out[...] = pdfs[pl.ds(slot, BLOCK_ROWS, stride=BLK_DEV), :]
+            source = jnp.where(moves[j] == value, j, source)
+        out[...] = pdfs[pl.ds(source, BLOCK_ROWS, stride=BLK_DEV), :]
 
 
 def index_kernel(cycle, neighbours, sends, receives, ranks):
@@ -352,15 +386,14 @@
     return lambda rows: flags[pl.ds(BLK_DEV * rows.start + b, rows.size, stride=BLK_DEV), :]
 
 
-def first_kernel(cycle, plan, sends, flags, *refs):
+def first_kernel(moves, sends, flags, *refs):
     arrived, (post, faces), outs = refs[:5], refs[5:7], refs[7:]
     values = [sent_offset(kind)[1] for kind in BLOCK_ORDER] + [0]
     for j in range(BLK_DEV):
-        offset = cycle_offset(plan[j], cycle)
-        slot = plan[j] & 3
+        slot = moves[BLK_DEV + j]
         for source, value in zip(arrived, values):
 
-            @pl.when(offset == value)
+            @pl.when(moves[j] == value)
             def _(source=source):
                 def store(rows, value):
                     post[slot, rows, :] = value
@@ -382,32 +415,44 @@
     pool[FACES:] = own[...]
 
 
-def move_block(b, receives, post, pool, wide, new_load, store):
-    spots = [receives[b * 6 + face] for face in range(6)]
-    safe = [jnp.maximum(spot, 0) for spot in spots]
-    stream_block(
-        lambda rows: post[b, rows, :],
-        lambda face, rows: pool[safe[face], rows, :],
-        wide,
-        store,
-    )
-    for face in range(6):
-
-        @pl.when(spots[face] < 0)
-        def _(face=face):
-            bounce_face(face, lambda rows: post[b, rows, :], new_load, store)
-
-
-def step_kernel(sends, receives, flags, post, own, *refs):
-    arrived, (post_out, faces), outs, (pool, wide, new) = refs[:4], refs[4:6], refs[6:10], refs[10:]
-    fill_pool(pool, arrived, own)
-
+def inside_kernel(post, new, wide):
     @pl.loop(0, BLK_DEV)
     def _(b):
-        def store_new(rows, value):
-            new[rows, :] = value
-
-        move_block(b, receives, post, pool, wide, lambda rows: new[rows, :], store_new)
+        def store(rows, value):
+            new[b, rows, :] = value
+
+        stream_inside(lambda rows: post[b, rows, :], wide, store)
+
+
+def fill_block(b, pops, receives, inside, pool, new):
+    spots = [jnp.maximum(receives[b * 6 + face], 0) for face in range(6)]
+    fill_ghosts(
+        pops,
+        lambda rows: inside[b, rows, :],
+        lambda face, rows: pool[spots[face], rows, :],
+        new,
+    )
+
+
+def bounce_block(b, receives, post, new):
+    def store(rows, value):
+        new[rows, :] = value
+
+    for face in range(6):
+
+        @pl.when(receives[b * 6 + face] < 0)
+        def _(face=face):
+            bounce_face(face, lambda rows: post[b, rows, :], lambda rows: new[rows, :], store)
+
+
+def step_kernel(sends, receives, flags, post, inside, own, *refs):
+    arrived, (post_out, faces), outs, (pool, new) = refs[:4], refs[4:6], refs[6:10], refs[10:]
+    fill_pool(pool, arrived, own)
+
+    @pl.loop(0, BLK_DEV)
+    def _(b):
+        fill_block(b, range(POPS), receives, inside, pool, new)
+        bounce_block(b, receives, post, new)
 
         def store(rows, value):
             post_out[b, rows, :] = value
@@ -418,23 +463,42 @@
     send_faces(sends, faces, outs)
 
 
-def last_kernel(receives, post, own, *refs):
-    arrived, out, (pool, wide) = refs[:4], refs[4], refs[5:]
+def last_kernel(receives, post, inside, own, *refs):
+    arrived, out, (pool, new, whole, sem) = refs[:4], refs[4], refs[5:]
     fill_pool(pool, arrived, own)
 
-    @pl.loop(0, BLK_DEV)
-    def _(b):
-        def spots(rows):
-            return pl.ds(BLK_DEV * rows.start + b, rows.size, stride=BLK_DEV)
-
-        def store(rows, value):
-            out[spots(rows), :] = value
-
-        move_block(b, receives, post, pool, wide, lambda rows: out[spots(rows), :], store)
+    def store_out(i):
+        for b in range(BLK_DEV):
+            whole[pl.ds(i * ROWS * BLK_DEV + b, ROWS, stride=BLK_DEV), :] = new[
+                b, i * ROWS : (i + 1) * ROWS, :
+            ]
+        rows = pl.ds(i * ROWS * BLK_DEV, ROWS * BLK_DEV)
+        copy = pltpu.make_async_copy(whole.at[rows, :], out.at[rows, :], sem.at[i])
+        copy.start()
+        return copy
+
+    copies = []
+    for i in range(POPS):
+        for b in range(BLK_DEV):
+            fill_block(b, [i], receives, inside, pool, new.at[b])
+        copies.append(store_out(i))
+    for copy in copies:
+        copy.wait()
+    least = receives[0]
+    for n in range(1, FACES):
+        least = jnp.minimum(least, receives[n])
+
+    @pl.when(least < 0)
+    def _():
+        for b in range(BLK_DEV):
+            bounce_block(b, receives, post, new.at[b])
+        for copy in [store_out(i) for i in range(POPS)]:
+            copy.wait()
 
 
 SMEM = pl.BlockSpec(memory_space=pltpu.SMEM)
 VMEM = pl.BlockSpec(memory_space=pltpu.VMEM)
+HBM = pl.BlockSpec(memory_space=pltpu.HBM)
 BLOCK = jax.ShapeDtypeStruct((BLOCK_ROWS, 128), jnp.float32)
 POST = jax.ShapeDtypeStruct((BLK_DEV, BLOCK_ROWS, 128), jnp.float32)
 OWN = jax.ShapeDtypeStruct((FACES, FACE_ROWS, 128), jnp.float32)
@@ -444,7 +508,9 @@
 NEW = pltpu.VMEM((BLOCK_ROWS, 128), jnp.float32)
 
 
-def call(kernel, in_specs, out_shapes, out_specs, scratch=(), flops=0, bytes_accessed=0):
+def call(
+    kernel, in_specs, out_shapes, out_specs, scratch=(), flops=0, bytes_accessed=0
+):
     return pl.pallas_call(
         kernel,
         in_specs=in_specs,
@@ -470,10 +536,10 @@
     size = 4 * pdfs.size
     rows = pdfs.transpose(1, 0, 2).reshape(POPS, BLK_DEV, ROWS, 128)
     rows = rows.transpose(0, 2, 1, 3).reshape(BLK_DEV * BLOCK_ROWS, 128)
+    moves = jnp.concatenate([cycle_offset(plan, cycle), plan & 3])
     sent = call(
-        functools.partial(pack_kernel, cycle), [SMEM, VMEM], [BLOCK] * 5, [VMEM] * 5,
-        bytes_accessed=2 * size,
-    )(plan, rows)
+        pack_kernel, [SMEM, VMEM], [BLOCK] * 5, [VMEM] * 5, bytes_accessed=2 * size
+    )(moves, rows)
     arrived = exchange(sent, BLOCK_ORDER, cycle) + [sent[4]]
     table = jax.ShapeDtypeStruct((FACES,), jnp.int32)
     sends, receives = call(
@@ -485,20 +551,24 @@
         out_shapes=[POST, OWN] + [SENT] * 4, out_specs=[VMEM] * 6,
         flops=300 * pdfs.size // POPS, bytes_accessed=2 * size,
     )
+    inside = call(inside_kernel, [VMEM], POST, VMEM, [WIDE], bytes_accessed=2 * size)
     post, own, *faces = call(
-        functools.partial(first_kernel, cycle), [SMEM, SMEM] + [VMEM] * 6, **outs
-    )(plan, sends, cells, *arrived)
+        first_kernel, [SMEM, SMEM] + [VMEM] * 6, **outs
+    )(moves, sends, cells, *arrived)
     for _ in range(STEPS - 1):
         came = exchange(faces, FACE_ORDER, cycle)
         post, own, *faces = call(
-            step_kernel, [SMEM, SMEM] + [VMEM] * 7, scratch=[POOL, WIDE, NEW], **outs
-        )(sends, receives, cells, post, own, *came)
+            step_kernel, [SMEM, SMEM] + [VMEM] * 8, scratch=[POOL, NEW], **outs
+        )(sends, receives, cells, post, inside(post), own, *came)
     came = exchange(faces, FACE_ORDER, cycle)
+    whole = (BLK_DEV * BLOCK_ROWS, 128)
     out = call(
-        last_kernel, [SMEM] + [VMEM] * 6,
-        jax.ShapeDtypeStruct((BLK_DEV * BLOCK_ROWS, 128), jnp.float32), VMEM, [POOL, WIDE],
+        last_kernel, [SMEM] + [VMEM] * 7,
+        jax.ShapeDtypeStruct(whole, jnp.float32), HBM,
+        [POOL, pltpu.VMEM(POST.shape, jnp.float32), pltpu.VMEM(whole, jnp.float32),
+         pltpu.SemaphoreType.DMA((POPS,))],
         bytes_accessed=2 * size,
-    )(receives, post, own, *came)
+    )(receives, post, inside(post), own, *came)
     out = out.reshape(POPS, ROWS, BLK_DEV, 128).transpose(2, 0, 1, 3)
     return out.reshape(pdfs.shape)
 

time: 62.3 us -> 61 us (0.979)
  waiting for transfers between devices: 6.07 us -> 4.08 us
  other arithmetic: 0 us -> 0.75 us
  local copies, waits for them, and re-layouts: 1.97 us -> 1.3 us
    ppermute x16, waiting for transfers between devices: 6.07 us -> 4.08 us  [exchange(): lax.ppermute(value, 'blocks', [(i, ROUTES[kind](i) % cycle) for i in rang...]
    select_n x0 -> x1, other arithmetic: none -> 0.67 us  [cycle_offset(): return jnp.where(offset < -REACH, offset + cycle, offset)]
    unnamed x10 -> x6, local copies, waits for them, and re-layouts: 1.97 us -> 1.3 us
    pallas_call x5 -> x8, Pallas kernels: 10.5 us -> 11 us  [the longest x2 4.78 us: body(): call(step_kernel, [SMEM, SMEM] + [VMEM] * 8, scratch=[POOL, NEW], **outs)]
  transfers between devices with their start and end apart: 16 -> 16, of which waited for: 8 -> 5; matrix products, arithmetic and copies ran while one was open for 0% -> 0% of each run, Pallas kernels for 3% -> 6%
where the time goes in v3:
time: 61 us; the launch traced here: 60.9 us
  starting transfers between devices  41.5 us (68%)
  Pallas kernels  13.1 us (21%)
  waiting for transfers between devices  4.08 us (7%)
  local copies, waits for them, and re-layouts  1.3 us (2%)
  other arithmetic  0.75 us (1%)
    ppermute x16, starting transfers between devices, exchange(): lax.ppermute(value, 'blocks', [(i, ROUTES[kind](i) % cycle) for i in rang...  41.5 us
    pallas_call x2, Pallas kernels, body(): call(step_kernel, [SMEM, SMEM] + [VMEM] * 8, scratch=[POOL, NEW], **outs)  4.78 us
    ppermute x16, waiting for transfers between devices, exchange(): lax.ppermute(value, 'blocks', [(i, ROUTES[kind](i) % cycle) for i in rang...  4.08 us
    pallas_call x1, Pallas kernels, body(): call(functools.partial(index_kernel, cycle), [SMEM], [table] * 2, [SMEM]...  2.02 us
    pallas_call x3, Pallas kernels, body(): inside(post)  1.91 us
    pallas_call x1, Pallas kernels, body(): call(last_kernel, [SMEM] + [VMEM] * 7, jax.ShapeDtypeStruct(whole, jnp.fl...  1.84 us
    pallas_call x1, Pallas kernels, body(): call(first_kernel, [SMEM, SMEM] + [VMEM] * 6, **outs)  1.75 us
    unnamed x6, local copies, waits for them, and re-layouts  1.3 us
  transfers between devices with their start and end apart: 16, of which 5 were waited for; matrix products, arithmetic and copies ran while one was open for 0% of the time, Pallas kernels for 6%

profile of v3, /device:TPU:1, one launch (start us, length us, event | category | flops | bytes accessed | tf_op | source)
XLA Modules:
  0.0 60.9 jit_solution(11250768848335064032)
XLA Ops:
  0.0 0.7 %compare_select_fusion = (s32[4]{0:T(128)S(1)}, s32[4]{0:T(128)S(1)}) fusion(s32[4]{0:T(128)} %param.5, s32[]{:T(128)S(6)} %axis_index.12), kind=kLoop, calls=%fused_computation | loop fusion | flops 36 | bytes 52 | tf_op jit(solution)/shard_map/jit(_where)/select_n | solution.py:303
  0.8 1.3 %copy-done = f32[4,19,4096]{2,0,1:T(4,128)S(1)} copy-done((f32[4,19,4096]{2,0,1:T(4,128)S(1)}, f32[4,19,4096]{2,0,1:T(4,128)}, u32[]{:S(2)}) %copy-start) | copy-done | bytes 1245208
  2.1 0.7 %shard_map.47 = (f32[608,128]{1,0:T(8,128)S(1)}, f32[608,128]{1,0:T(8,128)S(1)}, f32[608,128]{1,0:T(8,128)S(1)}, f32[608,128]{1,0:T(8,128)S(1)}, f32[608,128]{1,0:T(8,128)S(1)}) custom-call(s32[8]{0:T(128)S(1)} %pad_add_fusion.moves, f32[2432,128]{1,0:T(8,128)S(1)} %bitcast.17), custom_call_target="tpu_custom_call" | custom-call | bytes 2490368 | tf_op jit(solution)/shard_map/pallas_call | solution.py:540
  2.8 2.1 %collective-permute-start = (f32[608,128]{1,0:T(8,128)S(1)}, f32[608,128]{1,0:T(8,128)S(1)}, u32[]{:S(2)}, u32[]{:S(2)}) collective-permute-start(f32[608,128]{1,0:T(8,128)S(1)} %get-tuple-element.32), channel_id=1, source_target_pairs={{0,2},{1,3},{2,4},{3,5},{4,6},{5,7},{6,8},{7,9},{8,10},{9,11},{10,... | collective-permute-start | bytes 933896 | tf_op jit(solution)/shard_map/ppermute | solution.py:529
  4.9 2.1 %collective-permute-start.1 = (f32[608,128]{1,0:T(8,128)S(1)}, f32[608,128]{1,0:T(8,128)S(1)}, u32[]{:S(2)}, u32[]{:S(2)}) collective-permute-start(f32[608,128]{1,0:T(8,128)S(1)} %get-tuple-element.33), channel_id=1, source_target_pairs={{0,127},{1,2},{2,1},{3,4},{4,3},{5,6},{6,5},{7,8},{8,7},{9,10},{10... | collective-permute-start | bytes 933896 | tf_op jit(solution)/shard_map/ppermute | solution.py:529
  7.0 5.7 %collective-permute-start.2 = (f32[608,128]{1,0:T(8,128)S(1)}, f32[608,128]{1,0:T(8,128)S(1)}, u32[]{:S(2)}, u32[]{:S(2)}) collective-permute-start(f32[608,128]{1,0:T(8,128)S(1)} %get-tuple-element.34), channel_id=1, source_target_pairs={{0,126},{1,127},{2,0},{3,1},{4,2},{5,3},{6,4},{7,5},{8,6},{9,7},{1... | collective-permute-start | bytes 933896 | tf_op jit(solution)/shard_map/ppermute | solution.py:529
  12.7 1.6 %collective-permute-start.3 = (f32[608,128]{1,0:T(8,128)S(1)}, f32[608,128]{1,0:T(8,128)S(1)}, u32[]{:S(2)}, u32[]{:S(2)}) collective-permute-start(f32[608,128]{1,0:T(8,128)S(1)} %get-tuple-element.35), channel_id=1, source_target_pairs={{0,1},{1,0},{2,3},{3,2},{4,5},{5,4},{6,7},{7,6},{8,9},{9,8},{10,11... | collective-permute-start | bytes 933896 | tf_op jit(solution)/shard_map/ppermute | solution.py:529
  14.3 2.0 %shard_map.46 = (s32[24]{0:T(128)S(1)}, s32[24]{0:T(128)S(1)}) custom-call(s32[4,6]{1,0:T(4,128)S(1)} %copy-done.2), custom_call_target="tpu_custom_call" | custom-call | bytes 1000 | tf_op jit(solution)/shard_map/pallas_call | solution.py:545
  16.3 2.9 %collective-permute-done.refs_0_ = f32[608,128]{1,0:T(8,128)S(1)} collective-permute-done((f32[608,128]{1,0:T(8,128)S(1)}, f32[608,128]{1,0:T(8,128)S(1)}, u32[]{:S(2)}, u32[]{:S(2)}) %collective-permute-start) | collective-permute-done | bytes 311328 | tf_op jit(solution)/shard_map/ppermute | solution.py:529
  19.7 1.8 %shard_map.48 = (f32[4,608,128]{2,1,0:T(8,128)S(1)}, f32[24,16,128]{2,1,0:T(8,128)S(1)}, f32[96,128]{1,0:T(8,128)S(1)}, f32[96,128]{1,0:T(8,128)S(1)}, f32[96,128]{1,0:T(8,128)S(1)}, /*index=5*/f32[96,128]{1,0:T(8,128)S(1)}) custom-call(s32[8]{0:T(128)S(1)} %pad_add_fusion.moves, s32[24]{0:T(128)S(1)} %get-tuple-element.31.sends, s32[128,128]{1,0:T(8,128)S(1)} %bitcast.18, ...), custom_call_target="tpu_custom_call" | custom-call | flops 4915200 | bytes 2490368 | tf_op jit(solution)/shard_map/pallas_call | solution.py:555
  21.6 1.8 %collective-permute-start.5 = (f32[96,128]{1,0:T(8,128)S(1)}, f32[96,128]{1,0:T(8,128)S(1)}, u32[]{:S(2)}, u32[]{:S(2)}) collective-permute-start(f32[96,128]{1,0:T(8,128)S(1)} %get-tuple-element.40), channel_id=1, source_target_pairs={{0,127},{1,2},{2,1},{3,4},{4,3},{5,6},{6,5},{7,8},{8,7},{9,10},{10... | collective-permute-start | bytes 147464 | tf_op jit(solution)/shard_map/ppermute | solution.py:529
  23.4 9.1 %collective-permute-start.6 = (f32[96,128]{1,0:T(8,128)S(1)}, f32[96,128]{1,0:T(8,128)S(1)}, u32[]{:S(2)}, u32[]{:S(2)}) collective-permute-start(f32[96,128]{1,0:T(8,128)S(1)} %get-tuple-element.41), channel_id=1, source_target_pairs={{0,126},{1,127},{2,0},{3,1},{4,2},{5,3},{6,4},{7,5},{8,6},{9,7},{1... | collective-permute-start | bytes 147464 | tf_op jit(solution)/shard_map/ppermute | solution.py:529
  32.5 1.0 %collective-permute-start.7 = (f32[96,128]{1,0:T(8,128)S(1)}, f32[96,128]{1,0:T(8,128)S(1)}, u32[]{:S(2)}, u32[]{:S(2)}) collective-permute-start(f32[96,128]{1,0:T(8,128)S(1)} %get-tuple-element.42), channel_id=1, source_target_pairs={{0,1},{1,0},{2,3},{3,2},{4,5},{5,4},{6,7},{7,6},{8,9},{9,8},{10,11... | collective-permute-start | bytes 147464 | tf_op jit(solution)/shard_map/ppermute | solution.py:529
  33.5 0.6 %shard_map.49.inside = f32[4,608,128]{2,1,0:T(8,128)S(1)} custom-call(f32[4,608,128]{2,1,0:T(8,128)S(1)} %get-tuple-element.37.post), custom_call_target="tpu_custom_call" | custom-call | bytes 2490368 | tf_op jit(solution)/shard_map/pallas_call | solution.py:562
  34.4 2.4 %shard_map.50 = (f32[4,608,128]{2,1,0:T(8,128)S(1)}, f32[24,16,128]{2,1,0:T(8,128)S(1)}, f32[96,128]{1,0:T(8,128)S(1)}, f32[96,128]{1,0:T(8,128)S(1)}, f32[96,128]{1,0:T(8,128)S(1)}, /*index=5*/f32[96,128]{1,0:T(8,128)S(1)}) custom-call(s32[24]{0:T(128)S(1)} %get-tuple-element.31.sends, s32[24]{0:T(128)S(1)} %get-tuple-element.30.receives, ...), custom_call_target="tpu_custom_call" | custom-call | flops 4915200 | bytes 2490368 | tf_op jit(solution)/shard_map/pallas_call | solution.py:560
  36.9 7.8 %collective-permute-start.10 = (f32[96,128]{1,0:T(8,128)S(1)}, f32[96,128]{1,0:T(8,128)S(1)}, u32[]{:S(2)}, u32[]{:S(2)}) collective-permute-start(f32[96,128]{1,0:T(8,128)S(1)} %get-tuple-element.47), channel_id=1, source_target_pairs={{0,126},{1,127},{2,0},{3,1},{4,2},{5,3},{6,4},{7,5},{8,6},{9,7},{1... | collective-permute-start | bytes 147464 | tf_op jit(solution)/shard_map/ppermute | solution.py:529
  44.7 0.9 %collective-permute-start.11 = (f32[96,128]{1,0:T(8,128)S(1)}, f32[96,128]{1,0:T(8,128)S(1)}, u32[]{:S(2)}, u32[]{:S(2)}) collective-permute-start(f32[96,128]{1,0:T(8,128)S(1)} %get-tuple-element.48), channel_id=1, source_target_pairs={{0,1},{1,0},{2,3},{3,2},{4,5},{5,4},{6,7},{7,6},{8,9},{9,8},{10,11... | collective-permute-start | bytes 147464 | tf_op jit(solution)/shard_map/ppermute | solution.py:529
  45.7 0.6 %shard_map.51.inside = f32[4,608,128]{2,1,0:T(8,128)S(1)} custom-call(f32[4,608,128]{2,1,0:T(8,128)S(1)} %get-tuple-element.43.post), custom_call_target="tpu_custom_call" | custom-call | bytes 2490368 | tf_op jit(solution)/shard_map/pallas_call | solution.py:562
  46.5 2.4 %shard_map.52 = (f32[4,608,128]{2,1,0:T(8,128)S(1)}, f32[24,16,128]{2,1,0:T(8,128)S(1)}, f32[96,128]{1,0:T(8,128)S(1)}, f32[96,128]{1,0:T(8,128)S(1)}, f32[96,128]{1,0:T(8,128)S(1)}, /*index=5*/f32[96,128]{1,0:T(8,128)S(1)}) custom-call(s32[24]{0:T(128)S(1)} %get-tuple-element.31.sends, s32[24]{0:T(128)S(1)} %get-tuple-element.30.receives, ...), custom_call_target="tpu_custom_call" | custom-call | flops 4915200 | bytes 2490368 | tf_op jit(solution)/shard_map/pallas_call | solution.py:560
  49.2 0.9 %collective-permute-start.13 = (f32[96,128]{1,0:T(8,128)S(1)}, f32[96,128]{1,0:T(8,128)S(1)}, u32[]{:S(2)}, u32[]{:S(2)}) collective-permute-start(f32[96,128]{1,0:T(8,128)S(1)} %get-tuple-element.52), channel_id=1, source_target_pairs={{0,127},{1,2},{2,1},{3,4},{4,3},{5,6},{6,5},{7,8},{8,7},{9,10},{10... | collective-permute-start | bytes 147464 | tf_op jit(solution)/shard_map/ppermute | solution.py:529
  50.1 7.5 %collective-permute-start.14 = (f32[96,128]{1,0:T(8,128)S(1)}, f32[96,128]{1,0:T(8,128)S(1)}, u32[]{:S(2)}, u32[]{:S(2)}) collective-permute-start(f32[96,128]{1,0:T(8,128)S(1)} %get-tuple-element.53), channel_id=1, source_target_pairs={{0,126},{1,127},{2,0},{3,1},{4,2},{5,3},{6,4},{7,5},{8,6},{9,7},{1... | collective-permute-start | bytes 147464 | tf_op jit(solution)/shard_map/ppermute | solution.py:529
  57.6 0.6 collective-permute-start.15
  58.1 0.6 %shard_map.53.inside = f32[4,608,128]{2,1,0:T(8,128)S(1)} custom-call(f32[4,608,128]{2,1,0:T(8,128)S(1)} %get-tuple-element.49.post), custom_call_target="tpu_custom_call" | custom-call | bytes 2490368 | tf_op jit(solution)/shard_map/pallas_call | solution.py:571
  59.0 1.8 %shard_map.54 = f32[2432,128]{1,0:T(8,128)} custom-call(s32[24]{0:T(128)S(1)} %get-tuple-element.30.receives, f32[4,608,128]{2,1,0:T(8,128)S(1)} %get-tuple-element.49.post, f32[4,608,128]{2,1,0:T(8,128)S(1)} %shard_map.53.inside, f32[24,16,128]{2,1,0:T(8,128)S(1)} %get-tuple-element.50.own, f32[96,128]{1,0:T(8,128)S(1)} %collective-permute-done.12.refs_0_, ...), custom_call_target="tpu_custom_call" | custom-call | bytes 2490368 | tf_op jit(solution)/shard_map/pallas_call | solution.py:565
  (25 shorter events, 1.8 us)
Async XLA Ops:
  0.0 14.3 %copy-start.2 = (s32[4,6]{1,0:T(4,128)S(1)}, s32[4,6]{1,0:T(4,128)}, u32[]{:S(2)}) copy-start(s32[4,6]{1,0:T(4,128)} %neighbours.1) | copy-start | bytes 292
  0.8 1.3 %copy-start = (f32[4,19,4096]{2,0,1:T(4,128)S(1)}, f32[4,19,4096]{2,0,1:T(4,128)}, u32[]{:S(2)}) copy-start(f32[4,19,4096]{2,0,1:T(4,128)} %param.4) | copy-start | bytes 3735556
  2.0 17.7 %copy-start.1 = (s32[4,4096]{1,0:T(4,128)S(1)}, s32[4,4096]{1,0:T(4,128)}, u32[]{:S(2)}) copy-start(s32[4,4096]{1,0:T(4,128)} %param.7) | copy-start | bytes 196612
  2.8 16.4 %collective-permute-start = (f32[608,128]{1,0:T(8,128)S(1)}, f32[608,128]{1,0:T(8,128)S(1)}, u32[]{:S(2)}, u32[]{:S(2)}) collective-permute-start(f32[608,128]{1,0:T(8,128)S(1)} %get-tuple-element.32), channel_id=1, source_target_pairs={{0,2},{1,3},{2,4},{3,5},{4,6},{5,7},{6,8},{7,9},{8,10},{9,11},{10,... | collective-permute-start | bytes 933896 | tf_op jit(solution)/shard_map/ppermute | solution.py:529
  4.9 14.3 %collective-permute-start.1 = (f32[608,128]{1,0:T(8,128)S(1)}, f32[608,128]{1,0:T(8,128)S(1)}, u32[]{:S(2)}, u32[]{:S(2)}) collective-permute-start(f32[608,128]{1,0:T(8,128)S(1)} %get-tuple-element.33), channel_id=1, source_target_pairs={{0,127},{1,2},{2,1},{3,4},{4,3},{5,6},{6,5},{7,8},{8,7},{9,10},{10... | collective-permute-start | bytes 933896 | tf_op jit(solution)/shard_map/ppermute | solution.py:529
  7.0 12.7 %collective-permute-start.2 = (f32[608,128]{1,0:T(8,128)S(1)}, f32[608,128]{1,0:T(8,128)S(1)}, u32[]{:S(2)}, u32[]{:S(2)}) collective-permute-start(f32[608,128]{1,0:T(8,128)S(1)} %get-tuple-element.34), channel_id=1, source_target_pairs={{0,126},{1,127},{2,0},{3,1},{4,2},{5,3},{6,4},{7,5},{8,6},{9,7},{1... | collective-permute-start | bytes 933896 | tf_op jit(solution)/shard_map/ppermute | solution.py:529
  12.7 7.1 %collective-permute-start.3 = (f32[608,128]{1,0:T(8,128)S(1)}, f32[608,128]{1,0:T(8,128)S(1)}, u32[]{:S(2)}, u32[]{:S(2)}) collective-permute-start(f32[608,128]{1,0:T(8,128)S(1)} %get-tuple-element.35), channel_id=1, source_target_pairs={{0,1},{1,0},{2,3},{3,2},{4,5},{5,4},{6,7},{7,6},{8,9},{9,8},{10,11... | collective-permute-start | bytes 933896 | tf_op jit(solution)/shard_map/ppermute | solution.py:529
  21.5 12.7 %collective-permute-start.4 = (f32[96,128]{1,0:T(8,128)S(1)}, f32[96,128]{1,0:T(8,128)S(1)}, u32[]{:S(2)}, u32[]{:S(2)}) collective-permute-start(f32[96,128]{1,0:T(8,128)S(1)} %get-tuple-element.39), channel_id=1, source_target_pairs={{0,2},{1,3},{2,4},{3,5},{4,6},{5,7},{6,8},{7,9},{8,10},{9,11},{10,... | collective-permute-start | bytes 147464 | tf_op jit(solution)/shard_map/ppermute | solution.py:529
  21.6 12.6 %collective-permute-start.5 = (f32[96,128]{1,0:T(8,128)S(1)}, f32[96,128]{1,0:T(8,128)S(1)}, u32[]{:S(2)}, u32[]{:S(2)}) collective-permute-start(f32[96,128]{1,0:T(8,128)S(1)} %get-tuple-element.40), channel_id=1, source_target_pairs={{0,127},{1,2},{2,1},{3,4},{4,3},{5,6},{6,5},{7,8},{8,7},{9,10},{10... | collective-permute-start | bytes 147464 | tf_op jit(solution)/shard_map/ppermute | solution.py:529
  23.4 10.8 %collective-permute-start.6 = (f32[96,128]{1,0:T(8,128)S(1)}, f32[96,128]{1,0:T(8,128)S(1)}, u32[]{:S(2)}, u32[]{:S(2)}) collective-permute-start(f32[96,128]{1,0:T(8,128)S(1)} %get-tuple-element.41), channel_id=1, source_target_pairs={{0,126},{1,127},{2,0},{3,1},{4,2},{5,3},{6,4},{7,5},{8,6},{9,7},{1... | collective-permute-start | bytes 147464 | tf_op jit(solution)/shard_map/ppermute | solution.py:529
  32.5 1.9 %collective-permute-start.7 = (f32[96,128]{1,0:T(8,128)S(1)}, f32[96,128]{1,0:T(8,128)S(1)}, u32[]{:S(2)}, u32[]{:S(2)}) collective-permute-start(f32[96,128]{1,0:T(8,128)S(1)} %get-tuple-element.42), channel_id=1, source_target_pairs={{0,1},{1,0},{2,3},{3,2},{4,5},{5,4},{6,7},{7,6},{8,9},{9,8},{10,11... | collective-permute-start | bytes 147464 | tf_op jit(solution)/shard_map/ppermute | solution.py:529
  36.8 9.5 %collective-permute-start.8 = (f32[96,128]{1,0:T(8,128)S(1)}, f32[96,128]{1,0:T(8,128)S(1)}, u32[]{:S(2)}, u32[]{:S(2)}) collective-permute-start(f32[96,128]{1,0:T(8,128)S(1)} %get-tuple-element.45), channel_id=1, source_target_pairs={{0,2},{1,3},{2,4},{3,5},{4,6},{5,7},{6,8},{7,9},{8,10},{9,11},{10,... | collective-permute-start | bytes 147464 | tf_op jit(solution)/shard_map/ppermute | solution.py:529
  36.8 9.5 %collective-permute-start.9 = (f32[96,128]{1,0:T(8,128)S(1)}, f32[96,128]{1,0:T(8,128)S(1)}, u32[]{:S(2)}, u32[]{:S(2)}) collective-permute-start(f32[96,128]{1,0:T(8,128)S(1)} %get-tuple-element.46), channel_id=1, source_target_pairs={{0,127},{1,2},{2,1},{3,4},{4,3},{5,6},{6,5},{7,8},{8,7},{9,10},{10... | collective-permute-start | bytes 147464 | tf_op jit(solution)/shard_map/ppermute | solution.py:529
  36.9 9.4 %collective-permute-start.10 = (f32[96,128]{1,0:T(8,128)S(1)}, f32[96,128]{1,0:T(8,128)S(1)}, u32[]{:S(2)}, u32[]{:S(2)}) collective-permute-start(f32[96,128]{1,0:T(8,128)S(1)} %get-tuple-element.47), channel_id=1, source_target_pairs={{0,126},{1,127},{2,0},{3,1},{4,2},{5,3},{6,4},{7,5},{8,6},{9,7},{1... | collective-permute-start | bytes 147464 | tf_op jit(solution)/shard_map/ppermute | solution.py:529
  44.7 1.8 %collective-permute-start.11 = (f32[96,128]{1,0:T(8,128)S(1)}, f32[96,128]{1,0:T(8,128)S(1)}, u32[]{:S(2)}, u32[]{:S(2)}) collective-permute-start(f32[96,128]{1,0:T(8,128)S(1)} %get-tuple-element.48), channel_id=1, source_target_pairs={{0,1},{1,0},{2,3},{3,2},{4,5},{5,4},{6,7},{7,6},{8,9},{9,8},{10,11... | collective-permute-start | bytes 147464 | tf_op jit(solution)/shard_map/ppermute | solution.py:529
  48.9 9.9 %collective-permute-start.12 = (f32[96,128]{1,0:T(8,128)S(1)}, f32[96,128]{1,0:T(8,128)S(1)}, u32[]{:S(2)}, u32[]{:S(2)}) collective-permute-start(f32[96,128]{1,0:T(8,128)S(1)} %get-tuple-element.51), channel_id=1, source_target_pairs={{0,2},{1,3},{2,4},{3,5},{4,6},{5,7},{6,8},{7,9},{8,10},{9,11},{10,... | collective-permute-start | bytes 147464 | tf_op jit(solution)/shard_map/ppermute | solution.py:529
  49.2 9.6 %collective-permute-start.13 = (f32[96,128]{1,0:T(8,128)S(1)}, f32[96,128]{1,0:T(8,128)S(1)}, u32[]{:S(2)}, u32[]{:S(2)}) collective-permute-start(f32[96,128]{1,0:T(8,128)S(1)} %get-tuple-element.52), channel_id=1, source_target_pairs={{0,127},{1,2},{2,1},{3,4},{4,3},{5,6},{6,5},{7,8},{8,7},{9,10},{10... | collective-permute-start | bytes 147464 | tf_op jit(solution)/shard_map/ppermute | solution.py:529
  50.1 8.7 %collective-permute-start.14 = (f32[96,128]{1,0:T(8,128)S(1)}, f32[96,128]{1,0:T(8,128)S(1)}, u32[]{:S(2)}, u32[]{:S(2)}) collective-permute-start(f32[96,128]{1,0:T(8,128)S(1)} %get-tuple-element.53), channel_id=1, source_target_pairs={{0,126},{1,127},{2,0},{3,1},{4,2},{5,3},{6,4},{7,5},{8,6},{9,7},{1... | collective-permute-start | bytes 147464 | tf_op jit(solution)/shard_map/ppermute | solution.py:529
  57.6 1.5 %collective-permute-start.15 = (f32[96,128]{1,0:T(8,128)S(1)}, f32[96,128]{1,0:T(8,128)S(1)}, u32[]{:S(2)}, u32[]{:S(2)}) collective-permute-start(f32[96,128]{1,0:T(8,128)S(1)} %get-tuple-element.54), channel_id=1, source_target_pairs={{0,1},{1,0},{2,3},{3,2},{4,5},{5,4},{6,7},{7,6},{8,9},{9,8},{10,11... | collective-permute-start | bytes 147464 | tf_op jit(solution)/shard_map/ppermute | solution.py:529

commit v4 on v3

--- a/solution.py
+++ b/solution.py
@@ -387,21 +387,27 @@
 
 
 def first_kernel(moves, sends, flags, *refs):
-    arrived, (post, faces), outs = refs[:5], refs[5:7], refs[7:]
+    arrived, (post, faces), outs, new = refs[:5], refs[5:7], refs[7:-1], refs[-1]
     values = [sent_offset(kind)[1] for kind in BLOCK_ORDER] + [0]
+    for n, source in enumerate(arrived):
+        new[n] = source[...]
+    sources = []
     for j in range(BLK_DEV):
-        slot = moves[BLK_DEV + j]
-        for source, value in zip(arrived, values):
-
-            @pl.when(moves[j] == value)
-            def _(source=source):
-                def store(rows, value):
-                    post[slot, rows, :] = value
-
-                collide_block(lambda r: source[r, :], flags_of(flags, slot), store)
-
-    @pl.loop(0, BLK_DEV)
+        source = jnp.int32(0)
+        for n, value in enumerate(values):
+            source = jnp.where(moves[j] == value, n, source)
+        sources.append(source)
+
+    @pl.loop(0, BLK_DEV, unroll=BLK_DEV)
     def _(b):
+        source = jnp.int32(0)
+        for j in range(BLK_DEV):
+            source = jnp.where(moves[BLK_DEV + j] == b, sources[j], source)
+
+        def store(rows, value):
+            post[b, rows, :] = value
+
+        collide_block(lambda r: new[source, r, :], flags_of(flags, b), store)
         pack_block(post, faces, b)
 
     send_faces(sends, faces, outs)
@@ -416,7 +422,7 @@
 
 
 def inside_kernel(post, new, wide):
-    @pl.loop(0, BLK_DEV)
+    @pl.loop(0, BLK_DEV, unroll=BLK_DEV)
     def _(b):
         def store(rows, value):
             new[b, rows, :] = value
@@ -449,7 +455,7 @@
     arrived, (post_out, faces), outs, (pool, new) = refs[:4], refs[4:6], refs[6:10], refs[10:]
     fill_pool(pool, arrived, own)
 
-    @pl.loop(0, BLK_DEV)
+    @pl.loop(0, BLK_DEV, unroll=BLK_DEV)
     def _(b):
         fill_block(b, range(POPS), receives, inside, pool, new)
         bounce_block(b, receives, post, new)
@@ -553,7 +559,8 @@
     )
     inside = call(inside_kernel, [VMEM], POST, VMEM, [WIDE], bytes_accessed=2 * size)
     post, own, *faces = call(
-        first_kernel, [SMEM, SMEM] + [VMEM] * 6, **outs
+        first_kernel, [SMEM, SMEM] + [VMEM] * 6,
+        scratch=[pltpu.VMEM((BLK_DEV + 1, BLOCK_ROWS, 128), jnp.float32)], **outs
     )(moves, sends, cells, *arrived)
     for _ in range(STEPS - 1):
         came = exchange(faces, FACE_ORDER, cycle)

time: 61 us -> 60.3 us (0.989)
  Pallas kernels: 13.1 us -> 11.7 us
  transfers between devices with their start and end apart: 16 -> 16, of which waited for: 5 -> 6; matrix products, arithmetic and copies ran while one was open for 0% -> 0% of each run, Pallas kernels for 6% -> 6%
where the time goes in v4:
time: 60.3 us; the launch traced here: 60.1 us
  starting transfers between devices  41.5 us (69%)
  Pallas kernels  11.7 us (19%)
  waiting for transfers between devices  4.65 us (8%)
  local copies, waits for them, and re-layouts  1.3 us (2%)
  other arithmetic  0.75 us (1%)
    ppermute x16, starting transfers between devices, exchange(): lax.ppermute(value, 'blocks', [(i, ROUTES[kind](i) % cycle) for i in rang...  41.5 us
    ppermute x16, waiting for transfers between devices, exchange(): lax.ppermute(value, 'blocks', [(i, ROUTES[kind](i) % cycle) for i in rang...  4.65 us
    pallas_call x2, Pallas kernels, body(): call(step_kernel, [SMEM, SMEM] + [VMEM] * 8, scratch=[POOL, NEW], **outs)  4.32 us
    pallas_call x1, Pallas kernels, body(): call(functools.partial(index_kernel, cycle), [SMEM], [table] * 2, [SMEM]...  2.02 us
    pallas_call x1, Pallas kernels, body(): call(last_kernel, [SMEM] + [VMEM] * 7, jax.ShapeDtypeStruct(whole, jnp.fl...  1.83 us
    pallas_call x1, Pallas kernels, body(): call(first_kernel, [SMEM, SMEM] + [VMEM] * 6, scratch=[pltpu.VMEM((BLK_DE...  1.47 us
    pallas_call x3, Pallas kernels, body(): inside(post)  1.34 us
    unnamed x6, local copies, waits for them, and re-layouts  1.3 us
  transfers between devices with their start and end apart: 16, of which 6 were waited for; matrix products, arithmetic and copies ran while one was open for 0% of the time, Pallas kernels for 6%

profile of v4, /device:TPU:1, one launch (start us, length us, event | category | flops | bytes accessed | tf_op | source)
XLA Modules:
  0.0 60.1 jit_solution(17331811670966178609)
XLA Ops:
  0.0 0.7 %compare_select_fusion = (s32[4]{0:T(128)S(1)}, s32[4]{0:T(128)S(1)}) fusion(s32[4]{0:T(128)} %param.5, s32[]{:T(128)S(6)} %axis_index.12), kind=kLoop, calls=%fused_computation | loop fusion | flops 36 | bytes 52 | tf_op jit(solution)/shard_map/jit(_where)/select_n | solution.py:303
  0.8 1.3 %copy-done = f32[4,19,4096]{2,0,1:T(4,128)S(1)} copy-done((f32[4,19,4096]{2,0,1:T(4,128)S(1)}, f32[4,19,4096]{2,0,1:T(4,128)}, u32[]{:S(2)}) %copy-start) | copy-done | bytes 1245208
  2.1 0.7 %shard_map.47 = (f32[608,128]{1,0:T(8,128)S(1)}, f32[608,128]{1,0:T(8,128)S(1)}, f32[608,128]{1,0:T(8,128)S(1)}, f32[608,128]{1,0:T(8,128)S(1)}, f32[608,128]{1,0:T(8,128)S(1)}) custom-call(s32[8]{0:T(128)S(1)} %pad_add_fusion.moves, f32[2432,128]{1,0:T(8,128)S(1)} %bitcast.17), custom_call_target="tpu_custom_call" | custom-call | bytes 2490368 | tf_op jit(solution)/shard_map/pallas_call | solution.py:546
  2.8 2.1 %collective-permute-start = (f32[608,128]{1,0:T(8,128)S(1)}, f32[608,128]{1,0:T(8,128)S(1)}, u32[]{:S(2)}, u32[]{:S(2)}) collective-permute-start(f32[608,128]{1,0:T(8,128)S(1)} %get-tuple-element.32), channel_id=1, source_target_pairs={{0,2},{1,3},{2,4},{3,5},{4,6},{5,7},{6,8},{7,9},{8,10},{9,11},{10,... | collective-permute-start | bytes 933896 | tf_op jit(solution)/shard_map/ppermute | solution.py:535
  4.9 2.1 %collective-permute-start.1 = (f32[608,128]{1,0:T(8,128)S(1)}, f32[608,128]{1,0:T(8,128)S(1)}, u32[]{:S(2)}, u32[]{:S(2)}) collective-permute-start(f32[608,128]{1,0:T(8,128)S(1)} %get-tuple-element.33), channel_id=1, source_target_pairs={{0,127},{1,2},{2,1},{3,4},{4,3},{5,6},{6,5},{7,8},{8,7},{9,10},{10... | collective-permute-start | bytes 933896 | tf_op jit(solution)/shard_map/ppermute | solution.py:535
  7.0 5.7 %collective-permute-start.2 = (f32[608,128]{1,0:T(8,128)S(1)}, f32[608,128]{1,0:T(8,128)S(1)}, u32[]{:S(2)}, u32[]{:S(2)}) collective-permute-start(f32[608,128]{1,0:T(8,128)S(1)} %get-tuple-element.34), channel_id=1, source_target_pairs={{0,126},{1,127},{2,0},{3,1},{4,2},{5,3},{6,4},{7,5},{8,6},{9,7},{1... | collective-permute-start | bytes 933896 | tf_op jit(solution)/shard_map/ppermute | solution.py:535
  12.7 1.6 %collective-permute-start.3 = (f32[608,128]{1,0:T(8,128)S(1)}, f32[608,128]{1,0:T(8,128)S(1)}, u32[]{:S(2)}, u32[]{:S(2)}) collective-permute-start(f32[608,128]{1,0:T(8,128)S(1)} %get-tuple-element.35), channel_id=1, source_target_pairs={{0,1},{1,0},{2,3},{3,2},{4,5},{5,4},{6,7},{7,6},{8,9},{9,8},{10,11... | collective-permute-start | bytes 933896 | tf_op jit(solution)/shard_map/ppermute | solution.py:535
  14.3 2.0 %shard_map.46 = (s32[24]{0:T(128)S(1)}, s32[24]{0:T(128)S(1)}) custom-call(s32[4,6]{1,0:T(4,128)S(1)} %copy-done.2), custom_call_target="tpu_custom_call" | custom-call | bytes 1000 | tf_op jit(solution)/shard_map/pallas_call | solution.py:551
  16.3 2.9 %collective-permute-done.refs_0_ = f32[608,128]{1,0:T(8,128)S(1)} collective-permute-done((f32[608,128]{1,0:T(8,128)S(1)}, f32[608,128]{1,0:T(8,128)S(1)}, u32[]{:S(2)}, u32[]{:S(2)}) %collective-permute-start) | collective-permute-done | bytes 311328 | tf_op jit(solution)/shard_map/ppermute | solution.py:535
  19.2 0.5 collective-permute-done.2.refs_2_
  19.7 1.5 %shard_map.48 = (f32[4,608,128]{2,1,0:T(8,128)S(1)}, f32[24,16,128]{2,1,0:T(8,128)S(1)}, f32[96,128]{1,0:T(8,128)S(1)}, f32[96,128]{1,0:T(8,128)S(1)}, f32[96,128]{1,0:T(8,128)S(1)}, /*index=5*/f32[96,128]{1,0:T(8,128)S(1)}) custom-call(s32[8]{0:T(128)S(1)} %pad_add_fusion.moves, s32[24]{0:T(128)S(1)} %get-tuple-element.31.sends, s32[128,128]{1,0:T(8,128)S(1)} %bitcast.18, ...), custom_call_target="tpu_custom_call" | custom-call | flops 4915200 | bytes 2490368 | tf_op jit(solution)/shard_map/pallas_call | solution.py:561
  21.3 1.8 %collective-permute-start.5 = (f32[96,128]{1,0:T(8,128)S(1)}, f32[96,128]{1,0:T(8,128)S(1)}, u32[]{:S(2)}, u32[]{:S(2)}) collective-permute-start(f32[96,128]{1,0:T(8,128)S(1)} %get-tuple-element.40), channel_id=1, source_target_pairs={{0,127},{1,2},{2,1},{3,4},{4,3},{5,6},{6,5},{7,8},{8,7},{9,10},{10... | collective-permute-start | bytes 147464 | tf_op jit(solution)/shard_map/ppermute | solution.py:535
  23.1 9.1 %collective-permute-start.6 = (f32[96,128]{1,0:T(8,128)S(1)}, f32[96,128]{1,0:T(8,128)S(1)}, u32[]{:S(2)}, u32[]{:S(2)}) collective-permute-start(f32[96,128]{1,0:T(8,128)S(1)} %get-tuple-element.41), channel_id=1, source_target_pairs={{0,126},{1,127},{2,0},{3,1},{4,2},{5,3},{6,4},{7,5},{8,6},{9,7},{1... | collective-permute-start | bytes 147464 | tf_op jit(solution)/shard_map/ppermute | solution.py:535
  32.2 1.0 %collective-permute-start.7 = (f32[96,128]{1,0:T(8,128)S(1)}, f32[96,128]{1,0:T(8,128)S(1)}, u32[]{:S(2)}, u32[]{:S(2)}) collective-permute-start(f32[96,128]{1,0:T(8,128)S(1)} %get-tuple-element.42), channel_id=1, source_target_pairs={{0,1},{1,0},{2,3},{3,2},{4,5},{5,4},{6,7},{7,6},{8,9},{9,8},{10,11... | collective-permute-start | bytes 147464 | tf_op jit(solution)/shard_map/ppermute | solution.py:535
  33.2 0.4 shard_map.49.inside
  34.1 2.2 %shard_map.50 = (f32[4,608,128]{2,1,0:T(8,128)S(1)}, f32[24,16,128]{2,1,0:T(8,128)S(1)}, f32[96,128]{1,0:T(8,128)S(1)}, f32[96,128]{1,0:T(8,128)S(1)}, f32[96,128]{1,0:T(8,128)S(1)}, /*index=5*/f32[96,128]{1,0:T(8,128)S(1)}) custom-call(s32[24]{0:T(128)S(1)} %get-tuple-element.31.sends, s32[24]{0:T(128)S(1)} %get-tuple-element.30.receives, ...), custom_call_target="tpu_custom_call" | custom-call | flops 4915200 | bytes 2490368 | tf_op jit(solution)/shard_map/pallas_call | solution.py:567
  36.4 7.8 %collective-permute-start.10 = (f32[96,128]{1,0:T(8,128)S(1)}, f32[96,128]{1,0:T(8,128)S(1)}, u32[]{:S(2)}, u32[]{:S(2)}) collective-permute-start(f32[96,128]{1,0:T(8,128)S(1)} %get-tuple-element.47), channel_id=1, source_target_pairs={{0,126},{1,127},{2,0},{3,1},{4,2},{5,3},{6,4},{7,5},{8,6},{9,7},{1... | collective-permute-start | bytes 147464 | tf_op jit(solution)/shard_map/ppermute | solution.py:535
  44.2 0.9 %collective-permute-start.11 = (f32[96,128]{1,0:T(8,128)S(1)}, f32[96,128]{1,0:T(8,128)S(1)}, u32[]{:S(2)}, u32[]{:S(2)}) collective-permute-start(f32[96,128]{1,0:T(8,128)S(1)} %get-tuple-element.48), channel_id=1, source_target_pairs={{0,1},{1,0},{2,3},{3,2},{4,5},{5,4},{6,7},{7,6},{8,9},{9,8},{10,11... | collective-permute-start | bytes 147464 | tf_op jit(solution)/shard_map/ppermute | solution.py:535
  46.0 2.2 %shard_map.52 = (f32[4,608,128]{2,1,0:T(8,128)S(1)}, f32[24,16,128]{2,1,0:T(8,128)S(1)}, f32[96,128]{1,0:T(8,128)S(1)}, f32[96,128]{1,0:T(8,128)S(1)}, f32[96,128]{1,0:T(8,128)S(1)}, /*index=5*/f32[96,128]{1,0:T(8,128)S(1)}) custom-call(s32[24]{0:T(128)S(1)} %get-tuple-element.31.sends, s32[24]{0:T(128)S(1)} %get-tuple-element.30.receives, ...), custom_call_target="tpu_custom_call" | custom-call | flops 4915200 | bytes 2490368 | tf_op jit(solution)/shard_map/pallas_call | solution.py:567
  48.5 0.9 %collective-permute-start.13 = (f32[96,128]{1,0:T(8,128)S(1)}, f32[96,128]{1,0:T(8,128)S(1)}, u32[]{:S(2)}, u32[]{:S(2)}) collective-permute-start(f32[96,128]{1,0:T(8,128)S(1)} %get-tuple-element.52), channel_id=1, source_target_pairs={{0,127},{1,2},{2,1},{3,4},{4,3},{5,6},{6,5},{7,8},{8,7},{9,10},{10... | collective-permute-start | bytes 147464 | tf_op jit(solution)/shard_map/ppermute | solution.py:535
  49.3 7.5 %collective-permute-start.14 = (f32[96,128]{1,0:T(8,128)S(1)}, f32[96,128]{1,0:T(8,128)S(1)}, u32[]{:S(2)}, u32[]{:S(2)}) collective-permute-start(f32[96,128]{1,0:T(8,128)S(1)} %get-tuple-element.53), channel_id=1, source_target_pairs={{0,126},{1,127},{2,0},{3,1},{4,2},{5,3},{6,4},{7,5},{8,6},{9,7},{1... | collective-permute-start | bytes 147464 | tf_op jit(solution)/shard_map/ppermute | solution.py:535
  56.8 0.6 collective-permute-start.15
  57.4 0.4 shard_map.53.inside
  58.3 1.8 %shard_map.54 = f32[2432,128]{1,0:T(8,128)} custom-call(s32[24]{0:T(128)S(1)} %get-tuple-element.30.receives, f32[4,608,128]{2,1,0:T(8,128)S(1)} %get-tuple-element.49.post, f32[4,608,128]{2,1,0:T(8,128)S(1)} %shard_map.53.inside, f32[24,16,128]{2,1,0:T(8,128)S(1)} %get-tuple-element.50.own, f32[96,128]{1,0:T(8,128)S(1)} %collective-permute-done.12.refs_0_, ...), custom_call_target="tpu_custom_call" | custom-call | bytes 2490368 | tf_op jit(solution)/shard_map/pallas_call | solution.py:572
  (25 shorter events, 2.3 us)
Async XLA Ops:
  0.0 14.3 %copy-start.2 = (s32[4,6]{1,0:T(4,128)S(1)}, s32[4,6]{1,0:T(4,128)}, u32[]{:S(2)}) copy-start(s32[4,6]{1,0:T(4,128)} %neighbours.1) | copy-start | bytes 292
  0.8 1.3 %copy-start = (f32[4,19,4096]{2,0,1:T(4,128)S(1)}, f32[4,19,4096]{2,0,1:T(4,128)}, u32[]{:S(2)}) copy-start(f32[4,19,4096]{2,0,1:T(4,128)} %param.4) | copy-start | bytes 3735556
  2.0 17.7 %copy-start.1 = (s32[4,4096]{1,0:T(4,128)S(1)}, s32[4,4096]{1,0:T(4,128)}, u32[]{:S(2)}) copy-start(s32[4,4096]{1,0:T(4,128)} %param.7) | copy-start | bytes 196612
  2.8 16.4 %collective-permute-start = (f32[608,128]{1,0:T(8,128)S(1)}, f32[608,128]{1,0:T(8,128)S(1)}, u32[]{:S(2)}, u32[]{:S(2)}) collective-permute-start(f32[608,128]{1,0:T(8,128)S(1)} %get-tuple-element.32), channel_id=1, source_target_pairs={{0,2},{1,3},{2,4},{3,5},{4,6},{5,7},{6,8},{7,9},{8,10},{9,11},{10,... | collective-permute-start | bytes 933896 | tf_op jit(solution)/shard_map/ppermute | solution.py:535
  4.9 14.3 %collective-permute-start.1 = (f32[608,128]{1,0:T(8,128)S(1)}, f32[608,128]{1,0:T(8,128)S(1)}, u32[]{:S(2)}, u32[]{:S(2)}) collective-permute-start(f32[608,128]{1,0:T(8,128)S(1)} %get-tuple-element.33), channel_id=1, source_target_pairs={{0,127},{1,2},{2,1},{3,4},{4,3},{5,6},{6,5},{7,8},{8,7},{9,10},{10... | collective-permute-start | bytes 933896 | tf_op jit(solution)/shard_map/ppermute | solution.py:535
  7.0 12.7 %collective-permute-start.2 = (f32[608,128]{1,0:T(8,128)S(1)}, f32[608,128]{1,0:T(8,128)S(1)}, u32[]{:S(2)}, u32[]{:S(2)}) collective-permute-start(f32[608,128]{1,0:T(8,128)S(1)} %get-tuple-element.34), channel_id=1, source_target_pairs={{0,126},{1,127},{2,0},{3,1},{4,2},{5,3},{6,4},{7,5},{8,6},{9,7},{1... | collective-permute-start | bytes 933896 | tf_op jit(solution)/shard_map/ppermute | solution.py:535
  12.7 7.1 %collective-permute-start.3 = (f32[608,128]{1,0:T(8,128)S(1)}, f32[608,128]{1,0:T(8,128)S(1)}, u32[]{:S(2)}, u32[]{:S(2)}) collective-permute-start(f32[608,128]{1,0:T(8,128)S(1)} %get-tuple-element.35), channel_id=1, source_target_pairs={{0,1},{1,0},{2,3},{3,2},{4,5},{5,4},{6,7},{7,6},{8,9},{9,8},{10,11... | collective-permute-start | bytes 933896 | tf_op jit(solution)/shard_map/ppermute | solution.py:535
  21.2 12.5 %collective-permute-start.4 = (f32[96,128]{1,0:T(8,128)S(1)}, f32[96,128]{1,0:T(8,128)S(1)}, u32[]{:S(2)}, u32[]{:S(2)}) collective-permute-start(f32[96,128]{1,0:T(8,128)S(1)} %get-tuple-element.39), channel_id=1, source_target_pairs={{0,2},{1,3},{2,4},{3,5},{4,6},{5,7},{6,8},{7,9},{8,10},{9,11},{10,... | collective-permute-start | bytes 147464 | tf_op jit(solution)/shard_map/ppermute | solution.py:535
  21.3 12.4 %collective-permute-start.5 = (f32[96,128]{1,0:T(8,128)S(1)}, f32[96,128]{1,0:T(8,128)S(1)}, u32[]{:S(2)}, u32[]{:S(2)}) collective-permute-start(f32[96,128]{1,0:T(8,128)S(1)} %get-tuple-element.40), channel_id=1, source_target_pairs={{0,127},{1,2},{2,1},{3,4},{4,3},{5,6},{6,5},{7,8},{8,7},{9,10},{10... | collective-permute-start | bytes 147464 | tf_op jit(solution)/shard_map/ppermute | solution.py:535
  23.1 10.6 %collective-permute-start.6 = (f32[96,128]{1,0:T(8,128)S(1)}, f32[96,128]{1,0:T(8,128)S(1)}, u32[]{:S(2)}, u32[]{:S(2)}) collective-permute-start(f32[96,128]{1,0:T(8,128)S(1)} %get-tuple-element.41), channel_id=1, source_target_pairs={{0,126},{1,127},{2,0},{3,1},{4,2},{5,3},{6,4},{7,5},{8,6},{9,7},{1... | collective-permute-start | bytes 147464 | tf_op jit(solution)/shard_map/ppermute | solution.py:535
  32.2 1.9 %collective-permute-start.7 = (f32[96,128]{1,0:T(8,128)S(1)}, f32[96,128]{1,0:T(8,128)S(1)}, u32[]{:S(2)}, u32[]{:S(2)}) collective-permute-start(f32[96,128]{1,0:T(8,128)S(1)} %get-tuple-element.42), channel_id=1, source_target_pairs={{0,1},{1,0},{2,3},{3,2},{4,5},{5,4},{6,7},{7,6},{8,9},{9,8},{10,11... | collective-permute-start | bytes 147464 | tf_op jit(solution)/shard_map/ppermute | solution.py:535
  36.2 9.3 %collective-permute-start.8 = (f32[96,128]{1,0:T(8,128)S(1)}, f32[96,128]{1,0:T(8,128)S(1)}, u32[]{:S(2)}, u32[]{:S(2)}) collective-permute-start(f32[96,128]{1,0:T(8,128)S(1)} %get-tuple-element.45), channel_id=1, source_target_pairs={{0,2},{1,3},{2,4},{3,5},{4,6},{5,7},{6,8},{7,9},{8,10},{9,11},{10,... | collective-permute-start | bytes 147464 | tf_op jit(solution)/shard_map/ppermute | solution.py:535
  36.3 9.3 %collective-permute-start.9 = (f32[96,128]{1,0:T(8,128)S(1)}, f32[96,128]{1,0:T(8,128)S(1)}, u32[]{:S(2)}, u32[]{:S(2)}) collective-permute-start(f32[96,128]{1,0:T(8,128)S(1)} %get-tuple-element.46), channel_id=1, source_target_pairs={{0,127},{1,2},{2,1},{3,4},{4,3},{5,6},{6,5},{7,8},{8,7},{9,10},{10... | collective-permute-start | bytes 147464 | tf_op jit(solution)/shard_map/ppermute | solution.py:535
  36.4 9.2 %collective-permute-start.10 = (f32[96,128]{1,0:T(8,128)S(1)}, f32[96,128]{1,0:T(8,128)S(1)}, u32[]{:S(2)}, u32[]{:S(2)}) collective-permute-start(f32[96,128]{1,0:T(8,128)S(1)} %get-tuple-element.47), channel_id=1, source_target_pairs={{0,126},{1,127},{2,0},{3,1},{4,2},{5,3},{6,4},{7,5},{8,6},{9,7},{1... | collective-permute-start | bytes 147464 | tf_op jit(solution)/shard_map/ppermute | solution.py:535
  44.2 1.8 %collective-permute-start.11 = (f32[96,128]{1,0:T(8,128)S(1)}, f32[96,128]{1,0:T(8,128)S(1)}, u32[]{:S(2)}, u32[]{:S(2)}) collective-permute-start(f32[96,128]{1,0:T(8,128)S(1)} %get-tuple-element.48), channel_id=1, source_target_pairs={{0,1},{1,0},{2,3},{3,2},{4,5},{5,4},{6,7},{7,6},{8,9},{9,8},{10,11... | collective-permute-start | bytes 147464 | tf_op jit(solution)/shard_map/ppermute | solution.py:535
  48.2 9.7 %collective-permute-start.12 = (f32[96,128]{1,0:T(8,128)S(1)}, f32[96,128]{1,0:T(8,128)S(1)}, u32[]{:S(2)}, u32[]{:S(2)}) collective-permute-start(f32[96,128]{1,0:T(8,128)S(1)} %get-tuple-element.51), channel_id=1, source_target_pairs={{0,2},{1,3},{2,4},{3,5},{4,6},{5,7},{6,8},{7,9},{8,10},{9,11},{10,... | collective-permute-start | bytes 147464 | tf_op jit(solution)/shard_map/ppermute | solution.py:535
  48.5 9.4 %collective-permute-start.13 = (f32[96,128]{1,0:T(8,128)S(1)}, f32[96,128]{1,0:T(8,128)S(1)}, u32[]{:S(2)}, u32[]{:S(2)}) collective-permute-start(f32[96,128]{1,0:T(8,128)S(1)} %get-tuple-element.52), channel_id=1, source_target_pairs={{0,127},{1,2},{2,1},{3,4},{4,3},{5,6},{6,5},{7,8},{8,7},{9,10},{10... | collective-permute-start | bytes 147464 | tf_op jit(solution)/shard_map/ppermute | solution.py:535
  49.3 8.7 %collective-permute-start.14 = (f32[96,128]{1,0:T(8,128)S(1)}, f32[96,128]{1,0:T(8,128)S(1)}, u32[]{:S(2)}, u32[]{:S(2)}) collective-permute-start(f32[96,128]{1,0:T(8,128)S(1)} %get-tuple-element.53), channel_id=1, source_target_pairs={{0,126},{1,127},{2,0},{3,1},{4,2},{5,3},{6,4},{7,5},{8,6},{9,7},{1... | collective-permute-start | bytes 147464 | tf_op jit(solution)/shard_map/ppermute | solution.py:535
  56.8 1.5 %collective-permute-start.15 = (f32[96,128]{1,0:T(8,128)S(1)}, f32[96,128]{1,0:T(8,128)S(1)}, u32[]{:S(2)}, u32[]{:S(2)}) collective-permute-start(f32[96,128]{1,0:T(8,128)S(1)} %get-tuple-element.54), channel_id=1, source_target_pairs={{0,1},{1,0},{2,3},{3,2},{4,5},{5,4},{6,7},{7,6},{8,9},{9,8},{10,11... | collective-permute-start | bytes 147464 | tf_op jit(solution)/shard_map/ppermute | solution.py:535

commit v5 on v4

--- a/solution.py
+++ b/solution.py
@@ -303,8 +303,8 @@
     return jnp.where(offset < -REACH, offset + cycle, offset)
 
 
-def pack_kernel(moves, pdfs, *outs):
-    values = [sent_offset(kind)[0] for kind in BLOCK_ORDER] + [0]
+def pack_kernel(kinds, moves, pdfs, *outs):
+    values = [sent_offset(kind)[0] if kind else 0 for kind in kinds]
     for out, value in zip(outs, values):
         source = jnp.int32(0)
         for j in range(BLK_DEV):
@@ -413,12 +413,18 @@
     send_faces(sends, faces, outs)
 
 
-def fill_pool(pool, arrived, own):
+def fill_pool(pool, receives, arrived, own):
     for kind, source in zip(FACE_ORDER, arrived):
         o = offset_place(-sent_offset(kind)[1])
         for r in range(PEER_FACES):
             pool[o * PEER_FACES + r] = source[r * FACE_ROWS : (r + 1) * FACE_ROWS, :]
-    pool[FACES:] = own[...]
+    most = receives[0]
+    for n in range(1, FACES):
+        most = jnp.maximum(most, receives[n])
+
+    @pl.when(most >= FACES)
+    def _():
+        pool[FACES:] = own[...]
 
 
 def inside_kernel(post, new, wide):
@@ -453,7 +459,7 @@
 
 def step_kernel(sends, receives, flags, post, inside, own, *refs):
     arrived, (post_out, faces), outs, (pool, new) = refs[:4], refs[4:6], refs[6:10], refs[10:]
-    fill_pool(pool, arrived, own)
+    fill_pool(pool, receives, arrived, own)
 
     @pl.loop(0, BLK_DEV, unroll=BLK_DEV)
     def _(b):
@@ -471,7 +477,7 @@
 
 def last_kernel(receives, post, inside, own, *refs):
     arrived, out, (pool, new, whole, sem) = refs[:4], refs[4], refs[5:]
-    fill_pool(pool, arrived, own)
+    fill_pool(pool, receives, arrived, own)
 
     def store_out(i):
         for b in range(BLK_DEV):
@@ -544,9 +550,14 @@
     rows = rows.transpose(0, 2, 1, 3).reshape(BLK_DEV * BLOCK_ROWS, 128)
     moves = jnp.concatenate([cycle_offset(plan, cycle), plan & 3])
     sent = call(
-        pack_kernel, [SMEM, VMEM], [BLOCK] * 5, [VMEM] * 5, bytes_accessed=2 * size
+        functools.partial(pack_kernel, BLOCK_ORDER), [SMEM, VMEM], [BLOCK] * 4, [VMEM] * 4,
+        bytes_accessed=2 * size,
     )(moves, rows)
-    arrived = exchange(sent, BLOCK_ORDER, cycle) + [sent[4]]
+    kept = call(
+        functools.partial(pack_kernel, (None,)), [SMEM, VMEM], [BLOCK], [VMEM],
+        bytes_accessed=2 * size,
+    )(moves, rows)
+    arrived = exchange(sent, BLOCK_ORDER, cycle) + list(kept)
     table = jax.ShapeDtypeStruct((FACES,), jnp.int32)
     sends, receives = call(
         functools.partial(index_kernel, cycle), [SMEM], [table] * 2, [SMEM] * 2,

time: 60.3 us -> 60.3 us (level)
    ppermute x16, waiting for transfers between devices: 4.65 us -> 4.05 us  [exchange(): lax.ppermute(value, 'blocks', [(i, ROUTES[kind](i) % cycle) for i in rang...]
    pallas_call x1 -> x2, Pallas kernels: 0.75 us -> 1.29 us  [the longest x1 0.71 us: body(): call(functools.partial(pack_kernel, BLOCK_ORDER), [SMEM, VMEM], [BLOCK] *...]
  transfers between devices with their start and end apart: 16 -> 16, of which waited for: 6 -> 6; matrix products, arithmetic and copies ran while one was open for 0% -> 0% of each run, Pallas kernels for 6% -> 7%
where the time goes in v5:
time: 60.3 us; the launch traced here: 60.1 us
  starting transfers between devices  41.5 us (69%)
  Pallas kernels  12.3 us (20%)
  waiting for transfers between devices  4.05 us (7%)
  local copies, waits for them, and re-layouts  1.3 us (2%)
  other arithmetic  0.74 us (1%)
    ppermute x16, starting transfers between devices, exchange(): lax.ppermute(value, 'blocks', [(i, ROUTES[kind](i) % cycle) for i in rang...  41.5 us
    pallas_call x2, Pallas kernels, body(): call(step_kernel, [SMEM, SMEM] + [VMEM] * 8, scratch=[POOL, NEW], **outs)  4.36 us
    ppermute x16, waiting for transfers between devices, exchange(): lax.ppermute(value, 'blocks', [(i, ROUTES[kind](i) % cycle) for i in rang...  4.05 us
    pallas_call x1, Pallas kernels, body(): call(functools.partial(index_kernel, cycle), [SMEM], [table] * 2, [SMEM]...  2.02 us
    pallas_call x1, Pallas kernels, body(): call(last_kernel, [SMEM] + [VMEM] * 7, jax.ShapeDtypeStruct(whole, jnp.fl...  1.85 us
    pallas_call x1, Pallas kernels, body(): call(first_kernel, [SMEM, SMEM] + [VMEM] * 6, scratch=[pltpu.VMEM((BLK_DE...  1.46 us
    pallas_call x3, Pallas kernels, body(): inside(post)  1.34 us
    unnamed x6, local copies, waits for them, and re-layouts  1.3 us
  transfers between devices with their start and end apart: 16, of which 6 were waited for; matrix products, arithmetic and copies ran while one was open for 0% of the time, Pallas kernels for 7%

profile of v5, /device:TPU:1, one launch (start us, length us, event | category | flops | bytes accessed | tf_op | source)
XLA Modules:
  0.0 60.1 jit_solution(6621950766895444647)
XLA Ops:
  0.0 0.7 %compare_select_fusion = (s32[4]{0:T(128)S(1)}, s32[4]{0:T(128)S(1)}) fusion(s32[4]{0:T(128)} %param.5, s32[]{:T(128)S(6)} %axis_index.12), kind=kLoop, calls=%fused_computation | loop fusion | flops 36 | bytes 52 | tf_op jit(solution)/shard_map/jit(_where)/select_n | solution.py:303
  0.7 1.3 %copy-done = f32[4,19,4096]{2,0,1:T(4,128)S(1)} copy-done((f32[4,19,4096]{2,0,1:T(4,128)S(1)}, f32[4,19,4096]{2,0,1:T(4,128)}, u32[]{:S(2)}) %copy-start) | copy-done | bytes 1245208
  2.0 0.7 %shard_map.47 = (f32[608,128]{1,0:T(8,128)S(1)}, f32[608,128]{1,0:T(8,128)S(1)}, f32[608,128]{1,0:T(8,128)S(1)}, f32[608,128]{1,0:T(8,128)S(1)}) custom-call(s32[8]{0:T(128)S(1)} %pad_add_fusion.moves, f32[2432,128]{1,0:T(8,128)S(1)} %bitcast.17), custom_call_target="tpu_custom_call" | custom-call | bytes 2490368 | tf_op jit(solution)/shard_map/pallas_call | solution.py:552
  2.8 2.1 %collective-permute-start = (f32[608,128]{1,0:T(8,128)S(1)}, f32[608,128]{1,0:T(8,128)S(1)}, u32[]{:S(2)}, u32[]{:S(2)}) collective-permute-start(f32[608,128]{1,0:T(8,128)S(1)} %get-tuple-element.31), channel_id=1, source_target_pairs={{0,2},{1,3},{2,4},{3,5},{4,6},{5,7},{6,8},{7,9},{8,10},{9,11},{10,... | collective-permute-start | bytes 933896 | tf_op jit(solution)/shard_map/ppermute | solution.py:541
  4.9 2.1 %collective-permute-start.1 = (f32[608,128]{1,0:T(8,128)S(1)}, f32[608,128]{1,0:T(8,128)S(1)}, u32[]{:S(2)}, u32[]{:S(2)}) collective-permute-start(f32[608,128]{1,0:T(8,128)S(1)} %get-tuple-element.32), channel_id=1, source_target_pairs={{0,127},{1,2},{2,1},{3,4},{4,3},{5,6},{6,5},{7,8},{8,7},{9,10},{10... | collective-permute-start | bytes 933896 | tf_op jit(solution)/shard_map/ppermute | solution.py:541
  6.9 5.7 %collective-permute-start.2 = (f32[608,128]{1,0:T(8,128)S(1)}, f32[608,128]{1,0:T(8,128)S(1)}, u32[]{:S(2)}, u32[]{:S(2)}) collective-permute-start(f32[608,128]{1,0:T(8,128)S(1)} %get-tuple-element.33), channel_id=1, source_target_pairs={{0,126},{1,127},{2,0},{3,1},{4,2},{5,3},{6,4},{7,5},{8,6},{9,7},{1... | collective-permute-start | bytes 933896 | tf_op jit(solution)/shard_map/ppermute | solution.py:541
  12.6 1.6 %collective-permute-start.3 = (f32[608,128]{1,0:T(8,128)S(1)}, f32[608,128]{1,0:T(8,128)S(1)}, u32[]{:S(2)}, u32[]{:S(2)}) collective-permute-start(f32[608,128]{1,0:T(8,128)S(1)} %get-tuple-element.34), channel_id=1, source_target_pairs={{0,1},{1,0},{2,3},{3,2},{4,5},{5,4},{6,7},{7,6},{8,9},{9,8},{10,11... | collective-permute-start | bytes 933896 | tf_op jit(solution)/shard_map/ppermute | solution.py:541
  14.2 0.6 shard_map.48.refs_4_
  14.8 2.0 %shard_map.46 = (s32[24]{0:T(128)S(1)}, s32[24]{0:T(128)S(1)}) custom-call(s32[4,6]{1,0:T(4,128)S(1)} %copy-done.2), custom_call_target="tpu_custom_call" | custom-call | bytes 1000 | tf_op jit(solution)/shard_map/pallas_call | solution.py:562
  16.8 2.3 %collective-permute-done.refs_0_ = f32[608,128]{1,0:T(8,128)S(1)} collective-permute-done((f32[608,128]{1,0:T(8,128)S(1)}, f32[608,128]{1,0:T(8,128)S(1)}, u32[]{:S(2)}, u32[]{:S(2)}) %collective-permute-start) | collective-permute-done | bytes 311328 | tf_op jit(solution)/shard_map/ppermute | solution.py:541
  19.1 0.5 collective-permute-done.2.refs_2_
  19.7 1.5 %shard_map.49 = (f32[4,608,128]{2,1,0:T(8,128)S(1)}, f32[24,16,128]{2,1,0:T(8,128)S(1)}, f32[96,128]{1,0:T(8,128)S(1)}, f32[96,128]{1,0:T(8,128)S(1)}, f32[96,128]{1,0:T(8,128)S(1)}, /*index=5*/f32[96,128]{1,0:T(8,128)S(1)}) custom-call(s32[8]{0:T(128)S(1)} %pad_add_fusion.moves, s32[24]{0:T(128)S(1)} %get-tuple-element.30.sends, s32[128,128]{1,0:T(8,128)S(1)} %bitcast.19, ...), custom_call_target="tpu_custom_call" | custom-call | flops 4915200 | bytes 2490368 | tf_op jit(solution)/shard_map/pallas_call | solution.py:572
  21.2 1.8 %collective-permute-start.5 = (f32[96,128]{1,0:T(8,128)S(1)}, f32[96,128]{1,0:T(8,128)S(1)}, u32[]{:S(2)}, u32[]{:S(2)}) collective-permute-start(f32[96,128]{1,0:T(8,128)S(1)} %get-tuple-element.38), channel_id=1, source_target_pairs={{0,127},{1,2},{2,1},{3,4},{4,3},{5,6},{6,5},{7,8},{8,7},{9,10},{10... | collective-permute-start | bytes 147464 | tf_op jit(solution)/shard_map/ppermute | solution.py:541
  23.0 9.1 %collective-permute-start.6 = (f32[96,128]{1,0:T(8,128)S(1)}, f32[96,128]{1,0:T(8,128)S(1)}, u32[]{:S(2)}, u32[]{:S(2)}) collective-permute-start(f32[96,128]{1,0:T(8,128)S(1)} %get-tuple-element.39), channel_id=1, source_target_pairs={{0,126},{1,127},{2,0},{3,1},{4,2},{5,3},{6,4},{7,5},{8,6},{9,7},{1... | collective-permute-start | bytes 147464 | tf_op jit(solution)/shard_map/ppermute | solution.py:541
  32.1 1.0 %collective-permute-start.7 = (f32[96,128]{1,0:T(8,128)S(1)}, f32[96,128]{1,0:T(8,128)S(1)}, u32[]{:S(2)}, u32[]{:S(2)}) collective-permute-start(f32[96,128]{1,0:T(8,128)S(1)} %get-tuple-element.40), channel_id=1, source_target_pairs={{0,1},{1,0},{2,3},{3,2},{4,5},{5,4},{6,7},{7,6},{8,9},{9,8},{10,11... | collective-permute-start | bytes 147464 | tf_op jit(solution)/shard_map/ppermute | solution.py:541
  34.0 2.2 %shard_map.51 = (f32[4,608,128]{2,1,0:T(8,128)S(1)}, f32[24,16,128]{2,1,0:T(8,128)S(1)}, f32[96,128]{1,0:T(8,128)S(1)}, f32[96,128]{1,0:T(8,128)S(1)}, f32[96,128]{1,0:T(8,128)S(1)}, /*index=5*/f32[96,128]{1,0:T(8,128)S(1)}) custom-call(s32[24]{0:T(128)S(1)} %get-tuple-element.30.sends, s32[24]{0:T(128)S(1)} %get-tuple-element.29.receives, ...), custom_call_target="tpu_custom_call" | custom-call | flops 4915200 | bytes 2490368 | tf_op jit(solution)/shard_map/pallas_call | solution.py:578
  36.4 7.8 %collective-permute-start.10 = (f32[96,128]{1,0:T(8,128)S(1)}, f32[96,128]{1,0:T(8,128)S(1)}, u32[]{:S(2)}, u32[]{:S(2)}) collective-permute-start(f32[96,128]{1,0:T(8,128)S(1)} %get-tuple-element.45), channel_id=1, source_target_pairs={{0,126},{1,127},{2,0},{3,1},{4,2},{5,3},{6,4},{7,5},{8,6},{9,7},{1... | collective-permute-start | bytes 147464 | tf_op jit(solution)/shard_map/ppermute | solution.py:541
  44.2 0.9 %collective-permute-start.11 = (f32[96,128]{1,0:T(8,128)S(1)}, f32[96,128]{1,0:T(8,128)S(1)}, u32[]{:S(2)}, u32[]{:S(2)}) collective-permute-start(f32[96,128]{1,0:T(8,128)S(1)} %get-tuple-element.46), channel_id=1, source_target_pairs={{0,1},{1,0},{2,3},{3,2},{4,5},{5,4},{6,7},{7,6},{8,9},{9,8},{10,11... | collective-permute-start | bytes 147464 | tf_op jit(solution)/shard_map/ppermute | solution.py:541
  46.0 2.2 %shard_map.53 = (f32[4,608,128]{2,1,0:T(8,128)S(1)}, f32[24,16,128]{2,1,0:T(8,128)S(1)}, f32[96,128]{1,0:T(8,128)S(1)}, f32[96,128]{1,0:T(8,128)S(1)}, f32[96,128]{1,0:T(8,128)S(1)}, /*index=5*/f32[96,128]{1,0:T(8,128)S(1)}) custom-call(s32[24]{0:T(128)S(1)} %get-tuple-element.30.sends, s32[24]{0:T(128)S(1)} %get-tuple-element.29.receives, ...), custom_call_target="tpu_custom_call" | custom-call | flops 4915200 | bytes 2490368 | tf_op jit(solution)/shard_map/pallas_call | solution.py:578
  48.5 0.9 %collective-permute-start.13 = (f32[96,128]{1,0:T(8,128)S(1)}, f32[96,128]{1,0:T(8,128)S(1)}, u32[]{:S(2)}, u32[]{:S(2)}) collective-permute-start(f32[96,128]{1,0:T(8,128)S(1)} %get-tuple-element.50), channel_id=1, source_target_pairs={{0,127},{1,2},{2,1},{3,4},{4,3},{5,6},{6,5},{7,8},{8,7},{9,10},{10... | collective-permute-start | bytes 147464 | tf_op jit(solution)/shard_map/ppermute | solution.py:541
  49.3 7.5 %collective-permute-start.14 = (f32[96,128]{1,0:T(8,128)S(1)}, f32[96,128]{1,0:T(8,128)S(1)}, u32[]{:S(2)}, u32[]{:S(2)}) collective-permute-start(f32[96,128]{1,0:T(8,128)S(1)} %get-tuple-element.51), channel_id=1, source_target_pairs={{0,126},{1,127},{2,0},{3,1},{4,2},{5,3},{6,4},{7,5},{8,6},{9,7},{1... | collective-permute-start | bytes 147464 | tf_op jit(solution)/shard_map/ppermute | solution.py:541
  56.8 0.6 collective-permute-start.15
  57.4 0.4 shard_map.54.inside
  58.3 1.9 %shard_map.55 = f32[2432,128]{1,0:T(8,128)} custom-call(s32[24]{0:T(128)S(1)} %get-tuple-element.29.receives, f32[4,608,128]{2,1,0:T(8,128)S(1)} %get-tuple-element.47.post, f32[4,608,128]{2,1,0:T(8,128)S(1)} %shard_map.54.inside, f32[24,16,128]{2,1,0:T(8,128)S(1)} %get-tuple-element.48.own, f32[96,128]{1,0:T(8,128)S(1)} %collective-permute-done.12.refs_0_, ...), custom_call_target="tpu_custom_call" | custom-call | bytes 2490368 | tf_op jit(solution)/shard_map/pallas_call | solution.py:583
  (26 shorter events, 2.7 us)
Async XLA Ops:
  0.7 1.3 %copy-start = (f32[4,19,4096]{2,0,1:T(4,128)S(1)}, f32[4,19,4096]{2,0,1:T(4,128)}, u32[]{:S(2)}) copy-start(f32[4,19,4096]{2,0,1:T(4,128)} %param.4) | copy-start | bytes 3735556
  2.0 12.8 %copy-start.2 = (s32[4,6]{1,0:T(4,128)S(1)}, s32[4,6]{1,0:T(4,128)}, u32[]{:S(2)}) copy-start(s32[4,6]{1,0:T(4,128)} %neighbours.1) | copy-start | bytes 292
  2.0 17.6 %copy-start.1 = (s32[4,4096]{1,0:T(4,128)S(1)}, s32[4,4096]{1,0:T(4,128)}, u32[]{:S(2)}) copy-start(s32[4,4096]{1,0:T(4,128)} %param.7) | copy-start | bytes 196612
  2.8 16.4 %collective-permute-start = (f32[608,128]{1,0:T(8,128)S(1)}, f32[608,128]{1,0:T(8,128)S(1)}, u32[]{:S(2)}, u32[]{:S(2)}) collective-permute-start(f32[608,128]{1,0:T(8,128)S(1)} %get-tuple-element.31), channel_id=1, source_target_pairs={{0,2},{1,3},{2,4},{3,5},{4,6},{5,7},{6,8},{7,9},{8,10},{9,11},{10,... | collective-permute-start | bytes 933896 | tf_op jit(solution)/shard_map/ppermute | solution.py:541
  4.9 14.3 %collective-permute-start.1 = (f32[608,128]{1,0:T(8,128)S(1)}, f32[608,128]{1,0:T(8,128)S(1)}, u32[]{:S(2)}, u32[]{:S(2)}) collective-permute-start(f32[608,128]{1,0:T(8,128)S(1)} %get-tuple-element.32), channel_id=1, source_target_pairs={{0,127},{1,2},{2,1},{3,4},{4,3},{5,6},{6,5},{7,8},{8,7},{9,10},{10... | collective-permute-start | bytes 933896 | tf_op jit(solution)/shard_map/ppermute | solution.py:541
  6.9 12.7 %collective-permute-start.2 = (f32[608,128]{1,0:T(8,128)S(1)}, f32[608,128]{1,0:T(8,128)S(1)}, u32[]{:S(2)}, u32[]{:S(2)}) collective-permute-start(f32[608,128]{1,0:T(8,128)S(1)} %get-tuple-element.33), channel_id=1, source_target_pairs={{0,126},{1,127},{2,0},{3,1},{4,2},{5,3},{6,4},{7,5},{8,6},{9,7},{1... | collective-permute-start | bytes 933896 | tf_op jit(solution)/shard_map/ppermute | solution.py:541
  12.6 7.1 %collective-permute-start.3 = (f32[608,128]{1,0:T(8,128)S(1)}, f32[608,128]{1,0:T(8,128)S(1)}, u32[]{:S(2)}, u32[]{:S(2)}) collective-permute-start(f32[608,128]{1,0:T(8,128)S(1)} %get-tuple-element.34), channel_id=1, source_target_pairs={{0,1},{1,0},{2,3},{3,2},{4,5},{5,4},{6,7},{7,6},{8,9},{9,8},{10,11... | collective-permute-start | bytes 933896 | tf_op jit(solution)/shard_map/ppermute | solution.py:541
  21.1 12.5 %collective-permute-start.4 = (f32[96,128]{1,0:T(8,128)S(1)}, f32[96,128]{1,0:T(8,128)S(1)}, u32[]{:S(2)}, u32[]{:S(2)}) collective-permute-start(f32[96,128]{1,0:T(8,128)S(1)} %get-tuple-element.37), channel_id=1, source_target_pairs={{0,2},{1,3},{2,4},{3,5},{4,6},{5,7},{6,8},{7,9},{8,10},{9,11},{10,... | collective-permute-start | bytes 147464 | tf_op jit(solution)/shard_map/ppermute | solution.py:541
  21.2 12.4 %collective-permute-start.5 = (f32[96,128]{1,0:T(8,128)S(1)}, f32[96,128]{1,0:T(8,128)S(1)}, u32[]{:S(2)}, u32[]{:S(2)}) collective-permute-start(f32[96,128]{1,0:T(8,128)S(1)} %get-tuple-element.38), channel_id=1, source_target_pairs={{0,127},{1,2},{2,1},{3,4},{4,3},{5,6},{6,5},{7,8},{8,7},{9,10},{10... | collective-permute-start | bytes 147464 | tf_op jit(solution)/shard_map/ppermute | solution.py:541
  23.0 10.6 %collective-permute-start.6 = (f32[96,128]{1,0:T(8,128)S(1)}, f32[96,128]{1,0:T(8,128)S(1)}, u32[]{:S(2)}, u32[]{:S(2)}) collective-permute-start(f32[96,128]{1,0:T(8,128)S(1)} %get-tuple-element.39), channel_id=1, source_target_pairs={{0,126},{1,127},{2,0},{3,1},{4,2},{5,3},{6,4},{7,5},{8,6},{9,7},{1... | collective-permute-start | bytes 147464 | tf_op jit(solution)/shard_map/ppermute | solution.py:541
  32.1 1.9 %collective-permute-start.7 = (f32[96,128]{1,0:T(8,128)S(1)}, f32[96,128]{1,0:T(8,128)S(1)}, u32[]{:S(2)}, u32[]{:S(2)}) collective-permute-start(f32[96,128]{1,0:T(8,128)S(1)} %get-tuple-element.40), channel_id=1, source_target_pairs={{0,1},{1,0},{2,3},{3,2},{4,5},{5,4},{6,7},{7,6},{8,9},{9,8},{10,11... | collective-permute-start | bytes 147464 | tf_op jit(solution)/shard_map/ppermute | solution.py:541
  36.2 9.3 %collective-permute-start.8 = (f32[96,128]{1,0:T(8,128)S(1)}, f32[96,128]{1,0:T(8,128)S(1)}, u32[]{:S(2)}, u32[]{:S(2)}) collective-permute-start(f32[96,128]{1,0:T(8,128)S(1)} %get-tuple-element.43), channel_id=1, source_target_pairs={{0,2},{1,3},{2,4},{3,5},{4,6},{5,7},{6,8},{7,9},{8,10},{9,11},{10,... | collective-permute-start | bytes 147464 | tf_op jit(solution)/shard_map/ppermute | solution.py:541
  36.3 9.3 %collective-permute-start.9 = (f32[96,128]{1,0:T(8,128)S(1)}, f32[96,128]{1,0:T(8,128)S(1)}, u32[]{:S(2)}, u32[]{:S(2)}) collective-permute-start(f32[96,128]{1,0:T(8,128)S(1)} %get-tuple-element.44), channel_id=1, source_target_pairs={{0,127},{1,2},{2,1},{3,4},{4,3},{5,6},{6,5},{7,8},{8,7},{9,10},{10... | collective-permute-start | bytes 147464 | tf_op jit(solution)/shard_map/ppermute | solution.py:541
  36.4 9.2 %collective-permute-start.10 = (f32[96,128]{1,0:T(8,128)S(1)}, f32[96,128]{1,0:T(8,128)S(1)}, u32[]{:S(2)}, u32[]{:S(2)}) collective-permute-start(f32[96,128]{1,0:T(8,128)S(1)} %get-tuple-element.45), channel_id=1, source_target_pairs={{0,126},{1,127},{2,0},{3,1},{4,2},{5,3},{6,4},{7,5},{8,6},{9,7},{1... | collective-permute-start | bytes 147464 | tf_op jit(solution)/shard_map/ppermute | solution.py:541
  44.2 1.8 %collective-permute-start.11 = (f32[96,128]{1,0:T(8,128)S(1)}, f32[96,128]{1,0:T(8,128)S(1)}, u32[]{:S(2)}, u32[]{:S(2)}) collective-permute-start(f32[96,128]{1,0:T(8,128)S(1)} %get-tuple-element.46), channel_id=1, source_target_pairs={{0,1},{1,0},{2,3},{3,2},{4,5},{5,4},{6,7},{7,6},{8,9},{9,8},{10,11... | collective-permute-start | bytes 147464 | tf_op jit(solution)/shard_map/ppermute | solution.py:541
  48.2 9.7 %collective-permute-start.12 = (f32[96,128]{1,0:T(8,128)S(1)}, f32[96,128]{1,0:T(8,128)S(1)}, u32[]{:S(2)}, u32[]{:S(2)}) collective-permute-start(f32[96,128]{1,0:T(8,128)S(1)} %get-tuple-element.49), channel_id=1, source_target_pairs={{0,2},{1,3},{2,4},{3,5},{4,6},{5,7},{6,8},{7,9},{8,10},{9,11},{10,... | collective-permute-start | bytes 147464 | tf_op jit(solution)/shard_map/ppermute | solution.py:541
  48.5 9.4 %collective-permute-start.13 = (f32[96,128]{1,0:T(8,128)S(1)}, f32[96,128]{1,0:T(8,128)S(1)}, u32[]{:S(2)}, u32[]{:S(2)}) collective-permute-start(f32[96,128]{1,0:T(8,128)S(1)} %get-tuple-element.50), channel_id=1, source_target_pairs={{0,127},{1,2},{2,1},{3,4},{4,3},{5,6},{6,5},{7,8},{8,7},{9,10},{10... | collective-permute-start | bytes 147464 | tf_op jit(solution)/shard_map/ppermute | solution.py:541
  49.3 8.7 %collective-permute-start.14 = (f32[96,128]{1,0:T(8,128)S(1)}, f32[96,128]{1,0:T(8,128)S(1)}, u32[]{:S(2)}, u32[]{:S(2)}) collective-permute-start(f32[96,128]{1,0:T(8,128)S(1)} %get-tuple-element.51), channel_id=1, source_target_pairs={{0,126},{1,127},{2,0},{3,1},{4,2},{5,3},{6,4},{7,5},{8,6},{9,7},{1... | collective-permute-start | bytes 147464 | tf_op jit(solution)/shard_map/ppermute | solution.py:541
  56.8 1.5 %collective-permute-start.15 = (f32[96,128]{1,0:T(8,128)S(1)}, f32[96,128]{1,0:T(8,128)S(1)}, u32[]{:S(2)}, u32[]{:S(2)}) collective-permute-start(f32[96,128]{1,0:T(8,128)S(1)} %get-tuple-element.52), channel_id=1, source_target_pairs={{0,1},{1,0},{2,3},{3,2},{4,5},{5,4},{6,7},{7,6},{8,9},{9,8},{10,11... | collective-permute-start | bytes 147464 | tf_op jit(solution)/shard_map/ppermute | solution.py:541
